TPU v7x, 256 devices: a whole 4x4x8 slice. The times are simulated.
256 devices in a mesh: pool: 32 (over x, y, core), tp: 8 (over z).
Axes of the slice: x: 4, y: 4, z: 8, core: 2. Of those that a mesh axis runs over, the one named last changes fastest.
Arguments:
- tokens: bfloat16 [2, 8192, 8192], P(None, 'pool', 'tp'), may hold values from -6 to 6
- query_weight: bfloat16 [8192, 4096], P('tp'), may hold values from -0.0625 to 0.0625
- down_weight: bfloat16 [512, 64, 8192], P('pool', None, 'tp'), may hold values from -0.0625 to 0.0625
- up_weight: bfloat16 [512, 64, 4096], P('pool', None, 'tp'), may hold values from -0.75 to 0.75
- requests: int32 [2, 32, 32], P(None, 'pool'), may hold values from 0 to 15
- row_slot_index: int32 [2, 32, 256], P(None, 'pool'), may hold values from 0 to 31, never falling along the last dimension, each value on 1 to 32 neighbouring positions
Outputs:
- queries: bfloat16 [2, 8192, 4096], P(None, 'pool', 'tp')
Inputs may be any that keep to these rules, and one draw needn't show every extreme that they name: `requests`: slot s of every group names an adapter held by group s. `row_slot_index`: within one group and step the slots never fall from row to row; every slot is used by 1 to 32 rows, and one slot by exactly 32.
All inputs are finite; a program needn't handle non-finite values.
Results may differ from a plain program's by a relative error of at most 0.0049.
Values may be sent and summed in bfloat16 or wider, within the bound.
No kernel may reach another device: no remote copies, remote signals or barrier semaphores. Data moves between devices by JAX's collectives and lax.ppermute only.
A program may use at most 128 MiB of HBM per device.

v0:
```python
import jax
import jax.numpy as jnp
from jax import lax
from jax.sharding import PartitionSpec as P


def slot_table(slot_list, count, most):
    onehot = (slot_list[:, :, None] == jnp.arange(count, dtype=jnp.int32)[None, None, :]).astype(
        jnp.int32
    )
    running = jnp.cumsum(onehot, axis=1)
    position = jnp.sum(running * onehot, axis=2) - 1
    place = slot_list * most + position
    return (jnp.arange(count * most, dtype=jnp.int32)[None, :, None] == place[:, None, :]).astype(
        jnp.bfloat16
    )


def gather_pages(wanted_pages, down_weight, up_weight):
    page_picker = (
        wanted_pages[:, :, None] == jnp.arange(down_weight.shape[0], dtype=jnp.int32)[None, None, :]
    ).astype(jnp.bfloat16)
    down_selected = jnp.einsum(
        "ovb,bwy->ovwy", page_picker, down_weight, preferred_element_type=jnp.float32
    ).astype(jnp.bfloat16)
    up_selected = jnp.einsum(
        "udw,wtv->udtv", page_picker, up_weight, preferred_element_type=jnp.float32
    ).astype(jnp.bfloat16)
    return (down_selected, up_selected)


def expand(summed, up_selected):
    shrink = summed.astype(jnp.bfloat16)
    return jnp.einsum(
        "knmr,knro->knmo", shrink, up_selected, preferred_element_type=jnp.float32
    ).astype(jnp.bfloat16)


def body(tokens, query_weight, down_weight, up_weight, requests, row_slot_index):
    count = lax.axis_size("pool")
    steps, rows, width = tokens.shape
    most = 4 * rows // count
    wanted_pages = requests[:, 0, :]
    table = slot_table(row_slot_index[:, 0, :], count, most)
    padded = jnp.einsum("kpr,krd->kpd", table, tokens, preferred_element_type=jnp.float32)
    padded = padded.astype(jnp.bfloat16).reshape(steps, count, most, width)
    asked_slots = lax.all_to_all(wanted_pages, "pool", split_axis=1, concat_axis=1, tiled=True)
    down_selected, up_selected = gather_pages(asked_slots, down_weight, up_weight)
    a_got, b_got = (
        lax.all_to_all(down_selected, "pool", split_axis=1, concat_axis=1, tiled=True),
        lax.all_to_all(up_selected, "pool", split_axis=1, concat_axis=1, tiled=True),
    )
    partial_value = jnp.einsum("knmd,knrd->knmr", padded, a_got, preferred_element_type=jnp.float32)
    summed = lax.psum(partial_value, "tp")
    adapter_delta = expand(summed, b_got)
    flat = adapter_delta.reshape(steps, count * most, adapter_delta.shape[-1])
    delta_rows = jnp.einsum("kpr,kpo->kro", table, flat, preferred_element_type=jnp.float32)
    base = jnp.einsum("krd,do->kro", tokens, query_weight, preferred_element_type=jnp.float32)
    base_part = lax.psum_scatter(base, "tp", scatter_dimension=2, tiled=True)
    return (base_part + delta_rows).astype(jnp.bfloat16)


def solution(mesh):
    placed = (
        P(None, "pool", "tp"),
        P("tp", None),
        P("pool", None, "tp"),
        P("pool", None, "tp"),
        P(None, "pool", None),
        P(None, "pool", None),
    )
    return jax.shard_map(
        body, mesh=mesh, in_specs=placed, out_specs=P(None, "pool", "tp"), check_vma=False
    )
```

profile of v0, /device:TPU:2, one launch (start us, length us, event | category | flops | bytes accessed | tf_op | source)
XLA Modules:
  0.0 272.4 jit_solution(17581598312078195243)
XLA Ops:
  6.5 0.0 copy-start
  6.5 0.0 reduce-scatter.2.cloned.1.call-start
  6.5 1.2 copy-done
  7.8 10.0 %fusion = f32[2,256,4096]{2,1,0:T(8,128)} fusion(bf16[2,256,1024]{2,1,0:T(8,128)(2,1)S(1)} %copy-done, bf16[1024,4096]{1,0:T(8,128)(2,1)} %param.7), kind=kOutput, calls=%fused_computation | convolution fusion | flops 4294967296 | bytes 17825792 | tf_op jit(solution)/shard_map/krd,do->kro/dot_general | solution.py:58
  17.8 0.0 copy-start.4
  17.8 0.0 copy-start.1
  17.8 0.0 reduce-scatter.2.cloned.1.call-update
  17.8 0.7 copy-done.4
  18.5 0.1 copy.12
  18.6 13.6 %all_to_all.19 = s32[2,32,1]{0,2,1:T(1,128)S(1)} all-to-all(s32[2,32,1]{0,2,1:T(1,128)S(1)} %copy.12), channel_id=1, replica_groups=mesh['pool'=32,'tp'=8] {'pool'}, dimensions={1} | all-to-all | bytes 512 | tf_op jit(solution)/shard_map/all_to_all | solution.py:47
  32.2 0.1 copy.13
  32.2 0.0 copy-done.1
  32.2 4.6 %convolution_convert_fusion = bf16[2,32,64,1024]{3,1,2,0:T(8,128)(2,1)} fusion(bf16[16,64,1024]{2,1,0:T(8,128)(2,1)S(1)} %copy-done.1, s32[2,32]{1,0:T(2,128)S(1)} %bitcast.48), kind=kOutput, calls=%fused_computation.4 | convolution fusion | flops 138413056 | bytes 10486016 | tf_op jit(solution)/shard_map/ovb,bwy->ovwy/dot_general | solution.py:23
  36.9 11.3 %copy.15 = bf16[2,32,64,1024]{3,2,0,1:T(8,128)(2,1)} copy(bf16[2,32,64,1024]{3,1,2,0:T(8,128)(2,1)} %convolution_convert_fusion) | data formatting | bytes 16777216 | tf_op jit(solution)/shard_map/convert_element_type | solution.py:25
  48.2 0.0 copy-start.2
  48.2 6.2 %all-to-all-start.1 = ((bf16[2,32,64,1024]{3,2,0,1:T(8,128)(2,1)}), bf16[2,32,64,1024]{3,2,0,1:T(8,128)(2,1)}, u32[]{:S(2)}, u32[]{:S(2)}) async-start(bf16[2,32,64,1024]{3,2,0,1:T(8,128)(2,1)} %copy.15), calls=%async_computation.2 | async-start | bytes 16777216 | tf_op jit(solution)/shard_map/all_to_all | solution.py:50
  54.4 0.0 copy-done.2
  54.4 1.3 convolution_convert_fusion.1
  55.7 4.4 %copy.18 = bf16[2,32,64,512]{3,2,0,1:T(8,128)(2,1)} copy(bf16[2,32,64,512]{3,1,2,0:T(8,128)(2,1)S(1)} %convolution_convert_fusion.1) | data formatting | bytes 8388608 | tf_op jit(solution)/shard_map/convert_element_type | solution.py:28
  60.1 0.0 copy-start.3
  60.1 98.4 %all-to-all-done.1 = bf16[2,32,64,1024]{3,2,0,1:T(8,128)(2,1)} async-done(((bf16[2,32,64,1024]{3,2,0,1:T(8,128)(2,1)}), bf16[2,32,64,1024]{3,2,0,1:T(8,128)(2,1)}, u32[]{:S(2)}, u32[]{:S(2)}) %all-to-all-start.1) | async-done | bytes 8388640 | tf_op jit(solution)/shard_map/all_to_all | solution.py:50
  158.5 28.0 %all-to-all-start.2 = ((bf16[2,32,64,512]{3,2,0,1:T(8,128)(2,1)}), bf16[2,32,64,512]{3,2,0,1:T(8,128)(2,1)}, u32[]{:S(2)}, u32[]{:S(2)}) async-start(bf16[2,32,64,512]{3,2,0,1:T(8,128)(2,1)} %copy.18), calls=%async_computation.3 | async-start | bytes 8388608 | tf_op jit(solution)/shard_map/all_to_all | solution.py:51
  186.4 0.0 copy-done.3
  186.5 1.2 reduce-window.6
  187.6 0.2 slice_reduce_fusion
  187.9 0.1 fusion.20
  188.1 1.4 convolution_convert_fusion.2
  189.4 5.8 %fusion.2 = f32[2,32,32,64]{3,2,1,0:T(8,128)S(1)} fusion(bf16[2,32,32,1024]{3,2,1,0:T(8,128)(2,1)S(1)} %bitcast.46, bf16[2,32,64,1024]{3,2,0,1:T(8,128)(2,1)} %all-to-all-done.1), kind=kOutput, calls=%fused_computation.2 | convolution fusion | flops 268435456 | bytes 13107200 | tf_op jit(solution)/shard_map/knmd,knrd->knmr/dot_general | solution.py:53
  195.2 64.5 %all-reduce.1 = bf16[2,32,32,64]{3,2,1,0:T(8,128)(2,1)} all-reduce(f32[2,32,32,64]{3,2,1,0:T(8,128)S(1)} %fusion.2), channel_id=1, replica_groups=mesh['pool'=32,'tp'=8] {'tp'}, use_global_device_ids=true, to_apply=%region_4.5 | all-reduce | flops 131072 | bytes 786432 | tf_op jit(solution)/shard_map/psum | solution.py:54
  259.7 0.0 all-to-all-done.2
  259.7 3.1 %fusion.9 = bf16[2,32,32,512]{3,2,1,0:T(8,128)(2,1)S(1)} fusion(bf16[2,32,64,512]{3,2,0,1:T(8,128)(2,1)} %all-to-all-done.2, bf16[2,32,32,64]{3,2,1,0:T(8,128)(2,1)} %all-reduce.1), kind=kOutput, calls=%fused_computation.13 | convolution fusion | flops 135266304 | bytes 6553600 | tf_op jit(solution)/shard_map/knmr,knro->knmo/dot_general | solution.py:34
  262.7 0.0 reduce-scatter.2.cloned.1.call-done
  262.8 2.8 %fusion.13 = bf16[2,256,512]{2,1,0:T(8,128)(2,1)} fusion(f32[2,256,512]{2,1,0:T(8,128)} %reduce-scatter.2.cloned.1.call-done, bf16[2,1024,512]{2,1,0:T(8,128)(2,1)S(1)} %bitcast.47, s32[2,256]{1,0:T(2,128)S(1)} %bitcast.52), kind=kOutput, calls=%fused_computation.15 | convolution fusion | flops 537919488 | bytes 3672064 | tf_op jit(solution)/shard_map/kpr,kpo->kro/dot_general | solution.py:57
  (7 shorter events, 0.1 us)
Async XLA Ops:
  6.5 1.2 copy-start
  6.5 256.2 %reduce-scatter.2.cloned.1.call-start = ((), (), s32[]{:S(2)}) async-start(), calls=%async_computation.4 | async-start | bytes 9437184 | tf_op jit(solution)/shard_map/reduce_scatter | solution.py:59
  17.8 0.7 copy-start.4
  17.8 14.4 %copy-start.1 = (bf16[16,64,1024]{2,1,0:T(8,128)(2,1)S(1)}, bf16[16,64,1024]{2,1,0:T(8,128)(2,1)}, u32[]{:S(2)}) copy-start(bf16[16,64,1024]{2,1,0:T(8,128)(2,1)} %param.8) | copy-start | bytes 6291460
  48.2 6.3 %copy-start.2 = (bf16[16,64,512]{2,1,0:T(8,128)(2,1)S(1)}, bf16[16,64,512]{2,1,0:T(8,128)(2,1)}, u32[]{:S(2)}) copy-start(bf16[16,64,512]{2,1,0:T(8,128)(2,1)} %param.9) | copy-start | bytes 3145732
  48.2 110.3 %all-to-all-start.1 = ((bf16[2,32,64,1024]{3,2,0,1:T(8,128)(2,1)}), bf16[2,32,64,1024]{3,2,0,1:T(8,128)(2,1)}, u32[]{:S(2)}, u32[]{:S(2)}) async-start(bf16[2,32,64,1024]{3,2,0,1:T(8,128)(2,1)} %copy.15), calls=%async_computation.2 | async-start | bytes 16777216 | tf_op jit(solution)/shard_map/all_to_all | solution.py:50
  60.1 126.3 %copy-start.3 = (s32[2,1,256]{2,1,0:T(1,128)S(1)}, s32[2,1,256]{2,1,0:T(1,128)}, u32[]{:S(2)}) copy-start(s32[2,1,256]{2,1,0:T(1,128)} %param.11) | copy-start | bytes 6148
  158.5 101.2 %all-to-all-start.2 = ((bf16[2,32,64,512]{3,2,0,1:T(8,128)(2,1)}), bf16[2,32,64,512]{3,2,0,1:T(8,128)(2,1)}, u32[]{:S(2)}, u32[]{:S(2)}) async-start(bf16[2,32,64,512]{3,2,0,1:T(8,128)(2,1)} %copy.18), calls=%async_computation.3 | async-start | bytes 8388608 | tf_op jit(solution)/shard_map/all_to_all | solution.py:51
Sparse Core Ops, SparseCore 0:
  17.9 97.8 reduce-scatter.1
where the time goes:
time: 273 us; the launch traced here: 272 us
  waiting for transfers between devices  98.4 us (36%)
  blocking collectives  78.1 us (29%)
  starting transfers between devices  34.2 us (13%)
  matrix products  28.9 us (11%)
  local copies, waits for them, and re-layouts  18 us (7%)
  between operations  13.5 us (5%)
    all_to_all x1, waiting for transfers between devices, body(): lax.all_to_all(down_selected, 'pool', split_axis=1, concat_axis=1, tiled=...  98.4 us
    psum x1, blocking collectives, body(): summed = lax.psum(partial_value, 'tp')  64.5 us
    all_to_all x1, starting transfers between devices, body(): lax.all_to_all(up_selected, 'pool', split_axis=1, concat_axis=1, tiled=True)  28 us
    all_to_all x1, blocking collectives, body(): lax.all_to_all(wanted_pages, 'pool', split_axis=1, concat_axis=1, tiled=T...  13.6 us
    convert_element_type x1, local copies, waits for them, and re-layouts, gather_pages(): down_selected = jnp.einsum('ovb,bwy->ovwy', page_picker, down_weight, pre...  11.3 us
    dot_general x1, matrix products, body(): jnp.einsum('krd,do->kro', tokens, query_weight, preferred_element_type=jn...  10 us
    all_to_all x1, starting transfers between devices, body(): lax.all_to_all(down_selected, 'pool', split_axis=1, concat_axis=1, tiled=...  6.25 us
    dot_general x1, matrix products, body(): jnp.einsum('knmd,knrd->knmr', padded, a_got, preferred_element_type=jnp.f...  5.76 us
  transfers between devices with their start and end apart: 3, of which 1 were waited for; matrix products, arithmetic and copies ran while one was open for 12% of the time, Pallas kernels for 0%

commit v1 on v0

v1 whole, which is shorter than its diff:
```python
import functools

import jax
import jax.numpy as jnp
from jax import lax
from jax.experimental import pallas as pl
from jax.experimental.pallas import tpu as pltpu
from jax.sharding import PartitionSpec as P

BF16 = jnp.bfloat16
F32 = jnp.float32
LANES = 128


def shrink_kernel(most, rank, ids_ref, x_ref, down_ref, out_ref, acc_ref):
    block, steps = x_ref.shape[0], x_ref.shape[1]
    first = pl.program_id(0) * block
    rows = x_ref[...].reshape(block * steps * most, x_ref.shape[-1])
    acc_ref[...] = lax.dot_general(
        rows, down_ref[...], (((1,), (0,)), ((), ())), preferred_element_type=F32
    )
    lane = lax.broadcasted_iota(jnp.int32, (most, LANES), 1)
    for i in range(block):
        parts = []
        for t in range(steps):
            adapter = ids_ref[first + i, t]
            column = pl.multiple_of((adapter // 2) * LANES, LANES)
            two = acc_ref[pl.ds((i * steps + t) * most, most), pl.ds(column, LANES)]
            swapped = pltpu.roll(two, rank, 1)
            parts.append(jnp.where(adapter % 2 == t, two, swapped))
        out_ref[i] = jnp.where(lane < rank, parts[0], parts[1]).astype(BF16)


def expand_kernel(most, rank, ids_ref, s_ref, up_ref, out_ref, wide_ref):
    block, steps = out_ref.shape[0], out_ref.shape[1]
    first = pl.program_id(0) * block
    wide_ref[...] = jnp.zeros_like(wide_ref)
    lane = lax.broadcasted_iota(jnp.int32, (most, LANES), 1)
    for i in range(block):
        both = s_ref[i].astype(F32)
        swapped = pltpu.roll(both, rank, 1)
        for t in range(steps):
            adapter = ids_ref[first + i, t]
            half = adapter % 2
            value = jnp.where(half == t, both, swapped)
            value = jnp.where((lane >= rank) == (half == 1), value, 0.0)
            column = pl.multiple_of((adapter // 2) * LANES, LANES)
            wide_ref[pl.ds((i * steps + t) * most, most), pl.ds(column, LANES)] = value.astype(BF16)
    out = jnp.dot(wide_ref[...], up_ref[...], preferred_element_type=F32)
    out_ref[...] = out.astype(BF16).reshape(out_ref.shape)


def shrink_rows(ids, x, down_t, block=8):
    groups, steps, most, width = x.shape
    held = down_t.shape[1]
    rank = LANES // 2
    return pl.pallas_call(
        functools.partial(shrink_kernel, most, rank),
        out_shape=jax.ShapeDtypeStruct((groups, most, steps * rank), BF16),
        grid_spec=pltpu.PrefetchScalarGridSpec(
            num_scalar_prefetch=1,
            grid=(groups // block,),
            in_specs=[
                pl.BlockSpec((block, steps, most, width), lambda i, ids: (i, 0, 0, 0)),
                pl.BlockSpec((width, held), lambda i, ids: (0, 0)),
            ],
            out_specs=pl.BlockSpec((block, most, steps * rank), lambda i, ids: (i, 0, 0)),
            scratch_shapes=[pltpu.VMEM((block * steps * most, held), F32)],
        ),
        compiler_params=pltpu.CompilerParams(vmem_limit_bytes=32 << 20),
        cost_estimate=pl.CostEstimate(
            flops=2 * groups * steps * most * width * held,
            bytes_accessed=2 * (x.size + down_t.size),
            transcendentals=0,
        ),
        name="shrink",
    )(ids, x, down_t)


def expand_rows(ids, s, up, steps, block=8):
    groups, most, both = s.shape
    held, features = up.shape
    rank = both // steps
    return pl.pallas_call(
        functools.partial(expand_kernel, most, rank),
        out_shape=jax.ShapeDtypeStruct((groups, steps, most, features), BF16),
        grid_spec=pltpu.PrefetchScalarGridSpec(
            num_scalar_prefetch=1,
            grid=(groups // block,),
            in_specs=[
                pl.BlockSpec((block, most, both), lambda i, ids: (i, 0, 0)),
                pl.BlockSpec((held, features), lambda i, ids: (0, 0)),
            ],
            out_specs=pl.BlockSpec((block, steps, most, features), lambda i, ids: (i, 0, 0, 0)),
            scratch_shapes=[pltpu.VMEM((block * steps * most, held), BF16)],
        ),
        compiler_params=pltpu.CompilerParams(vmem_limit_bytes=32 << 20),
        cost_estimate=pl.CostEstimate(
            flops=2 * groups * steps * most * held * features,
            bytes_accessed=2 * (s.size + up.size + groups * steps * most * features),
            transcendentals=0,
        ),
        name="expand",
    )(ids, s, up)


def sum_over_tp(partial_value):
    size = lax.axis_size("tp")
    groups, most, lanes = partial_value.shape
    flat = partial_value.reshape(groups * most, lanes)
    got = lax.all_to_all(flat, "tp", split_axis=0, concat_axis=0, tiled=True)
    share = got.reshape(size, groups * most // size, lanes).astype(F32).sum(0).astype(BF16)
    copies = jnp.broadcast_to(share[None], (size,) + share.shape).reshape(groups * most, lanes)
    full = lax.all_to_all(copies, "tp", split_axis=0, concat_axis=0, tiled=True)
    return full.reshape(groups, most, lanes)


def body(tokens, query_weight, down_weight, up_weight, requests, row_slot_index):
    count = lax.axis_size("pool")
    steps, rows, width = tokens.shape
    most = 4 * rows // count
    adapters, rank, _ = down_weight.shape
    features = up_weight.shape[-1]
    flat_tokens = tokens.reshape(steps * rows, width)

    slots = row_slot_index[:, 0, :]
    before = slots[:, None, :] < jnp.arange(count, dtype=jnp.int32)[None, :, None]
    start = jnp.minimum(jnp.sum(before.astype(jnp.int32), axis=2), rows - most)
    source = (
        jnp.arange(steps, dtype=jnp.int32)[None, :, None] * rows
        + start.T[:, :, None]
        + jnp.arange(most, dtype=jnp.int32)[None, None, :]
    ).reshape(count * steps * most)
    pick = (source[:, None] == jnp.arange(steps * rows, dtype=jnp.int32)[None, :]).astype(BF16)
    windows = jnp.dot(pick, flat_tokens, preferred_element_type=F32).astype(BF16)
    windows = windows.reshape(count, steps, most, width)
    x = lax.all_to_all(windows, "pool", split_axis=0, concat_axis=0, tiled=True)

    asked = lax.all_gather(requests[:, 0, :], "pool")
    ids = lax.dynamic_index_in_dim(asked, lax.axis_index("pool"), 2, False)

    base = jnp.dot(flat_tokens, query_weight, preferred_element_type=F32).astype(BF16)
    base_part = lax.psum_scatter(base, "tp", scatter_dimension=1, tiled=True)

    down_t = down_weight.reshape(adapters * rank, width).T
    shrink = sum_over_tp(shrink_rows(ids, x, down_t))
    delta = expand_rows(ids, shrink, up_weight.reshape(adapters * rank, features), steps)
    back = lax.all_to_all(delta, "pool", split_axis=0, concat_axis=0, tiled=True)

    mine = slots[:, :, None] == jnp.arange(count, dtype=jnp.int32)[None, None, :]
    own_start = jnp.sum(jnp.where(mine, start[:, None, :], 0), axis=2)
    place = (
        slots * (steps * most)
        + jnp.arange(steps, dtype=jnp.int32)[:, None] * most
        + jnp.arange(rows, dtype=jnp.int32)[None, :]
        - own_start
    ).reshape(steps * rows)
    spread = (place[:, None] == jnp.arange(count * steps * most, dtype=jnp.int32)[None, :]).astype(BF16)
    delta_rows = jnp.dot(
        spread, back.reshape(count * steps * most, features), preferred_element_type=F32
    )
    out = (base_part.astype(F32) + delta_rows).astype(BF16)
    return out.reshape(steps, rows, features)


def solution(mesh):
    placed = (
        P(None, "pool", "tp"),
        P("tp", None),
        P("pool", None, "tp"),
        P("pool", None, "tp"),
        P(None, "pool", None),
        P(None, "pool", None),
    )
    return jax.shard_map(
        body, mesh=mesh, in_specs=placed, out_specs=P(None, "pool", "tp"), check_vma=False
    )
```

time: 273 us -> 195 us (0.71)
  the two profiles are of different devices: /device:TPU:2 before, /device:TPU:1 now
where the time goes in v1:
time: 195 us
  blocking collectives  102 us (52%)
  waiting for transfers between devices  28.1 us (14%)
  matrix products  16.4 us (8%)
  starting transfers between devices  15.7 us (8%)
  between operations  13.5 us (7%)
  Pallas kernels  12.6 us (6%)
  local copies, waits for them, and re-layouts  6.54 us (3%)
    all_gather x1, blocking collectives, body(): asked = lax.all_gather(requests[:, 0, :], 'pool')  67.2 us
    all_to_all x1, waiting for transfers between devices, body(): lax.all_to_all(delta, 'pool', split_axis=0, concat_axis=0, tiled=True)  28.1 us
    all_to_all x1, blocking collectives, sum_over_tp(): got = lax.all_to_all(flat, 'tp', split_axis=0, concat_axis=0, tiled=True)  20.2 us
    all_to_all x1, blocking collectives, sum_over_tp(): full = lax.all_to_all(copies, 'tp', split_axis=0, concat_axis=0, tiled=True)  14.1 us
    dot_general x1, matrix products, body(): jnp.dot(flat_tokens, query_weight, preferred_element_type=F32).astype(BF16)  9.37 us
    all_to_all x1, starting transfers between devices, body(): x = lax.all_to_all(windows, 'pool', split_axis=0, concat_axis=0, tiled=True)  8.77 us
    pallas_call x1, Pallas kernels, shrink_rows(): pl.pallas_call(functools.partial(shrink_kernel, most, rank), out_shape=ja...  7.61 us
    all_to_all x1, starting transfers between devices, body(): lax.all_to_all(delta, 'pool', split_axis=0, concat_axis=0, tiled=True)  6.9 us
  transfers between devices with their start and end apart: 3, of which 1 were waited for; matrix products, arithmetic and copies ran while one was open for 4% of the time, Pallas kernels for 6%

profile of v1, /device:TPU:1, one launch (start us, length us, event | category | flops | bytes accessed | tf_op | source)
XLA Modules:
  0.0 194.9 jit_solution(8020500927260667692)
XLA Ops:
  6.5 0.0 copy-start
  6.5 0.0 reduce-scatter.2.cloned.1.call-start
  6.5 1.2 copy-done
  7.8 9.4 %convolution_convert_fusion = bf16[512,4096]{1,0:T(8,128)(2,1)} fusion(bf16[512,1024]{1,0:T(8,128)(2,1)S(1)} %bitcast.29, bf16[1024,4096]{1,0:T(8,128)(2,1)} %param.7), kind=kOutput, calls=%fused_computation | convolution fusion | flops 4297064448 | bytes 13631488 | tf_op jit(solution)/shard_map/dot_general | solution.py:142
  17.1 0.0 copy-start.2
  17.1 0.0 reduce-scatter.2.cloned.1.call-update
  17.2 0.6 copy-done.2
  17.8 0.1 convert_reduce_fusion
  17.9 0.1 broadcast_minimum_fusion
  18.0 0.1 copy.23
  18.1 0.1 iota_add_fusion
  18.2 0.1 add.82
  18.3 3.9 %fusion.2 = bf16[2048,1024]{1,0:T(8,128)(2,1)} fusion(bf16[512,1024]{1,0:T(8,128)(2,1)S(1)} %bitcast.30, s32[2048]{0:T(1024)S(1)} %add.82), kind=kOutput, calls=%fused_computation.5 | convolution fusion | flops 2150629376 | bytes 5251072 | tf_op jit(solution)/shard_map/dot_general | solution.py:135
  22.2 0.0 copy-start.3
  22.2 8.8 %all-to-all-start = ((bf16[32,2,32,1024]{3,2,1,0:T(8,128)(2,1)}), bf16[32,2,32,1024]{3,2,1,0:T(8,128)(2,1)}, u32[]{:S(2)}, u32[]{:S(2)}) async-start(bf16[32,2,32,1024]{3,2,1,0:T(8,128)(2,1)} %bitcast.35), calls=%async_computation.1 | async-start | bytes 8388608 | tf_op jit(solution)/shard_map/all_to_all | solution.py:137
  31.0 0.0 copy-done.3
  31.0 67.2 %all-gather = s32[64,1,32]{2,1,0:T(1,128)S(1)} all-gather(s32[2,1,32]{2,1,0:T(1,128)S(1)} %copy-done.3), channel_id=2, replica_groups=mesh['pool'=32,'tp'=8] {'pool'}, dimensions={0}, use_global_device_ids=true | all-gather | bytes 8448 | tf_op jit(solution)/shard_map/all_gather | solution.py:139
  98.2 0.1 constant_dynamic-slice_fusion
  98.3 0.1 copy.28
  98.4 0.1 copy.26.ids_ref
  98.5 2.9 %copy.24 = bf16[1024,1024]{0,1:T(8,128)(2,1)S(1)} copy(bf16[1024,1024]{1,0:T(8,128)(2,1)} %bitcast.36) | data formatting | bytes 4194304 | tf_op jit(solution)/shard_map/reshape | solution.py:145
  101.4 0.0 all-to-all-done.x_ref
  101.4 7.6 %shrink.1 = bf16[32,32,128]{2,1,0:T(8,128)(2,1)S(1)} custom-call(s32[32,2]{1,0:T(8,128)S(1)} %copy.26.ids_ref, bf16[32,2,32,1024]{3,2,1,0:T(8,128)(2,1)} %all-to-all-done.x_ref, bf16[1024,1024]{1,0:T(8,128)(2,1)S(1)} %bitcast.31), custom_call_target="tpu_custom_call" | custom-call | flops 4294967296 | bytes 6291456 | tf_op jit(solution)/shard_map/shrink/pallas_call | solution.py:57
  109.0 20.2 %all_to_all.25 = bf16[8,128,128]{2,1,0:T(8,128)(2,1)S(1)} all-to-all(bf16[8,128,128]{2,1,0:T(8,128)(2,1)S(1)} %bitcast.32), channel_id=1, replica_groups=mesh['pool'=32,'tp'=8] {'tp'}, dimensions={0} | all-to-all | bytes 524288 | tf_op jit(solution)/shard_map/all_to_all | solution.py:111
  129.3 14.1 %all_to_all.26 = bf16[8,128,128]{2,1,0:T(8,128)(2,1)S(1)} all-to-all(bf16[8,128,128]{2,1,0:T(8,128)(2,1)S(1)} %broadcast_in_dim.12), channel_id=1, replica_groups=mesh['pool'=32,'tp'=8] {'tp'}, dimensions={0} | all-to-all | bytes 524288 | tf_op jit(solution)/shard_map/all_to_all | solution.py:114
  143.5 0.0 copy-start.1
  143.5 1.2 copy-done.1
  144.7 5.0 %expand.1 = bf16[32,2,32,512]{3,2,1,0:T(8,128)(2,1)} custom-call(s32[32,2]{1,0:T(8,128)S(1)} %copy.26.ids_ref, bf16[32,32,128]{2,1,0:T(8,128)(2,1)S(1)} %bitcast.33, bf16[1024,512]{1,0:T(8,128)(2,1)S(1)} %bitcast.34), custom_call_target="tpu_custom_call" | custom-call | flops 2147483648 | bytes 3407872 | tf_op jit(solution)/shard_map/expand/pallas_call | solution.py:84
  149.7 6.9 %all-to-all-start.3 = ((bf16[32,2,32,512]{3,2,1,0:T(8,128)(2,1)}), bf16[32,2,32,512]{3,2,1,0:T(8,128)(2,1)S(1)}, u32[]{:S(2)}, u32[]{:S(2)}) async-start(bf16[32,2,32,512]{3,2,1,0:T(8,128)(2,1)} %expand.1), calls=%async_computation.4 | async-start | bytes 4194304 | tf_op jit(solution)/shard_map/all_to_all | solution.py:148
  156.6 0.1 select_reduce_fusion
  156.7 0.1 broadcast_bitcast_fusion
  156.8 28.1 %all-to-all-done.3 = bf16[32,2,32,512]{3,2,1,0:T(8,128)(2,1)S(1)} async-done(((bf16[32,2,32,512]{3,2,1,0:T(8,128)(2,1)}), bf16[32,2,32,512]{3,2,1,0:T(8,128)(2,1)S(1)}, u32[]{:S(2)}, u32[]{:S(2)}) %all-to-all-start.3) | async-done | bytes 2097184 | tf_op jit(solution)/shard_map/all_to_all | solution.py:148
  184.9 0.0 reduce-scatter.2.cloned.1.call-done
  184.9 3.1 %fusion.6 = bf16[512,512]{1,0:T(8,128)(2,1)} fusion(bf16[2048,512]{1,0:T(8,128)(2,1)S(1)} %bitcast.37, s32[512]{0:T(512)S(1)} %add_subtract_fusion, bf16[512,512]{1,0:T(8,128)(2,1)} %reduce-scatter.2.cloned.1.call-done), kind=kOutput, calls=%fused_computation.9 | convolution fusion | flops 1075576832 | bytes 3147776 | tf_op jit(solution)/shard_map/dot_general | solution.py:159
  (11 shorter events, 0.1 us)
Async XLA Ops:
  6.5 1.2 copy-start
  6.5 178.4 %reduce-scatter.2.cloned.1.call-start = ((), (), s32[]{:S(2)}) async-start(), calls=%async_computation.5 | async-start | bytes 4718592 | tf_op jit(solution)/shard_map/reduce_scatter | solution.py:143
  17.1 0.7 copy-start.2
  22.2 8.8 %copy-start.3 = (s32[2,1,32]{2,1,0:T(1,128)S(1)}, s32[2,1,32]{2,1,0:T(1,128)}, u32[]{:S(2)}) copy-start(s32[2,1,32]{2,1,0:T(1,128)} %param.10) | copy-start | bytes 772
  22.2 79.1 %all-to-all-start = ((bf16[32,2,32,1024]{3,2,1,0:T(8,128)(2,1)}), bf16[32,2,32,1024]{3,2,1,0:T(8,128)(2,1)}, u32[]{:S(2)}, u32[]{:S(2)}) async-start(bf16[32,2,32,1024]{3,2,1,0:T(8,128)(2,1)} %bitcast.35), calls=%async_computation.1 | async-start | bytes 8388608 | tf_op jit(solution)/shard_map/all_to_all | solution.py:137
  143.5 1.2 copy-start.1
  149.7 35.2 %all-to-all-start.3 = ((bf16[32,2,32,512]{3,2,1,0:T(8,128)(2,1)}), bf16[32,2,32,512]{3,2,1,0:T(8,128)(2,1)S(1)}, u32[]{:S(2)}, u32[]{:S(2)}) async-start(bf16[32,2,32,512]{3,2,1,0:T(8,128)(2,1)} %expand.1), calls=%async_computation.4 | async-start | bytes 4194304 | tf_op jit(solution)/shard_map/all_to_all | solution.py:148
Sparse Core Ops, SparseCore 0:
  17.3 59.1 reduce-scatter.1

commit v2 on v1

v2 whole, which is shorter than its diff:
```python
import functools

import jax
import jax.numpy as jnp
from jax import lax
from jax.experimental import pallas as pl
from jax.experimental.pallas import tpu as pltpu
from jax.sharding import PartitionSpec as P

BF16 = jnp.bfloat16
F32 = jnp.float32
LANES = 128
TILE = 16
VMEM = 40 << 20


def pack_kernel(asked_ref, slots_ref, tokens_ref, out_ref):
    steps, rows, width = tokens_ref.shape
    block, tiles = out_ref.shape[0], out_ref.shape[1] - 1
    across = width // LANES
    most = tiles // (steps * across) * TILE
    first = pl.program_id(0) * block
    shape = (block, most, rows)
    slot = lax.broadcasted_iota(jnp.int32, shape, 0) + first
    ahead = lax.broadcasted_iota(jnp.int32, shape, 1)
    position = lax.broadcasted_iota(jnp.int32, shape, 2)
    for t in range(steps):
        held = jnp.broadcast_to(slots_ref[t].reshape(1, 1, rows), shape)
        before = jnp.where(held < slot, 1.0, 0.0)
        start = jnp.minimum(jnp.sum(before, axis=2, keepdims=True).astype(jnp.int32), rows - most)
        pick = jnp.where(position == start + ahead, 1.0, 0.0).astype(BF16)
        value = jnp.dot(pick.reshape(block * most, rows), tokens_ref[t], preferred_element_type=F32)
        value = value.astype(BF16).reshape(block, most // TILE, TILE, width)
        for down in range(most // TILE):
            for c in range(across):
                tile = (t * (most // TILE) + down) * across + c
                out_ref[:, tile] = value[:, down, :, c * LANES : (c + 1) * LANES]
    line = lax.broadcasted_iota(jnp.int32, (TILE, LANES), 0)
    for s in range(block):
        names = jnp.where(line < TILE // 2, asked_ref[0, first + s], asked_ref[1, first + s])
        out_ref[s, tiles] = names.astype(F32).astype(BF16)


def pack(asked, slots, tokens, most, block=8):
    steps, rows, width = tokens.shape
    count = asked.shape[1]
    tiles = steps * (most // TILE) * (width // LANES)
    return pl.pallas_call(
        pack_kernel,
        out_shape=jax.ShapeDtypeStruct((count, tiles + 1, TILE, LANES), BF16),
        grid_spec=pltpu.PrefetchScalarGridSpec(
            num_scalar_prefetch=1,
            grid=(count // block,),
            in_specs=[
                pl.BlockSpec((steps, 1, rows), lambda i, asked: (0, 0, 0)),
                pl.BlockSpec((steps, rows, width), lambda i, asked: (0, 0, 0)),
            ],
            out_specs=pl.BlockSpec((block, tiles + 1, TILE, LANES), lambda i, asked: (i, 0, 0, 0)),
        ),
        compiler_params=pltpu.CompilerParams(vmem_limit_bytes=VMEM),
        cost_estimate=pl.CostEstimate(
            flops=2 * count * steps * most * rows * width,
            bytes_accessed=2 * (tokens.size + count * (tiles + 1) * TILE * LANES),
            transcendentals=0,
        ),
        name="pack",
    )(asked, slots, tokens)


def shrink_kernel(rank, names_ref, x_ref, down_ref, out_ref, rows_ref, acc_ref):
    block, steps, most, held = acc_ref.shape
    width = rows_ref.shape[-1]
    across = width // LANES
    for d in range(rows_ref.shape[1]):
        for c in range(across):
            rows_ref[:, d, :, c * LANES : (c + 1) * LANES] = x_ref[:, d * across + c]
    acc = jnp.dot(rows_ref[...].reshape(block * steps * most, width), down_ref[...], preferred_element_type=F32)
    acc_ref[...] = acc.reshape(acc_ref.shape)
    names = names_ref[:, 0].astype(F32)
    lane = lax.broadcasted_iota(jnp.int32, (block * most, LANES), 1)
    parts = []
    for t in range(steps):
        wanted = names[:, t * (TILE // steps) : t * (TILE // steps) + 1, :]
        wanted = jnp.broadcast_to(wanted, (block, most, LANES))
        value = jnp.zeros((block, most, LANES), F32)
        odd = jnp.zeros((block, most, LANES), F32)
        for c in range(held // LANES):
            here = acc_ref[:, t, :, c * LANES : (c + 1) * LANES]
            value = jnp.where((wanted == 2.0 * c) | (wanted == 2.0 * c + 1.0), here, value)
            odd = jnp.where(wanted == 2.0 * c + 1.0, 1.0, odd)
        value = value.reshape(block * most, LANES)
        odd = odd.reshape(block * most, LANES)
        parts.append(jnp.where(odd == 1.0 * t, value, pltpu.roll(value, rank, 1)))
    out = jnp.where(lane < rank, parts[0], parts[1])
    out_ref[...] = out.astype(BF16).reshape(out_ref.shape)


def shrink_rows(x, down_t, steps, most, rank, block=8):
    groups, tiles = x.shape[0], x.shape[1] - 1
    width, held = down_t.shape
    return pl.pallas_call(
        functools.partial(shrink_kernel, rank),
        out_shape=jax.ShapeDtypeStruct((groups, most, LANES), BF16),
        grid=(groups // block,),
        in_specs=[
            pl.BlockSpec((block, 1, TILE, LANES), lambda i: (i, tiles, 0, 0)),
            pl.BlockSpec((block, tiles, TILE, LANES), lambda i: (i, 0, 0, 0)),
            pl.BlockSpec((width, held), lambda i: (0, 0)),
        ],
        out_specs=pl.BlockSpec((block, most, LANES), lambda i: (i, 0, 0)),
        scratch_shapes=[
            pltpu.VMEM((block, steps * most // TILE, TILE, width), BF16),
            pltpu.VMEM((block, steps, most, held), F32),
        ],
        compiler_params=pltpu.CompilerParams(vmem_limit_bytes=VMEM),
        cost_estimate=pl.CostEstimate(
            flops=2 * groups * steps * most * width * held,
            bytes_accessed=2 * (x.size + down_t.size),
            transcendentals=0,
        ),
        name="shrink",
    )(x, x, down_t)


def expand_kernel(rank, names_ref, s_ref, up_ref, out_ref, wide_ref):
    block, steps, most, held = wide_ref.shape
    names = names_ref[:, 0].astype(F32)
    both = s_ref[...].astype(F32).reshape(block * most, LANES)
    swapped = pltpu.roll(both, rank, 1).reshape(block, most, LANES)
    both = both.reshape(block, most, LANES)
    high = jnp.where(lax.broadcasted_iota(jnp.int32, (block, most, LANES), 2) < rank, 0.0, 1.0)
    for t in range(steps):
        wanted = names[:, t * (TILE // steps) : t * (TILE // steps) + 1, :]
        wanted = jnp.broadcast_to(wanted, (block, most, LANES))
        for c in range(held // LANES):
            chosen = jnp.where(high == 1.0 * t, both, swapped)
            value = jnp.where(wanted == 2.0 * c + high, chosen, 0.0)
            wide_ref[:, t, :, c * LANES : (c + 1) * LANES] = value.astype(BF16)
    wide = wide_ref[...].reshape(block * steps * most, held)
    out = jnp.dot(wide, up_ref[...], preferred_element_type=F32)
    out_ref[...] = out.astype(BF16).reshape(out_ref.shape)


def expand_rows(x, s, up, steps, rank, block=8):
    groups, most, _ = s.shape
    tiles = x.shape[1] - 1
    held, features = up.shape
    return pl.pallas_call(
        functools.partial(expand_kernel, rank),
        out_shape=jax.ShapeDtypeStruct((groups, steps, most, features), BF16),
        grid=(groups // block,),
        in_specs=[
            pl.BlockSpec((block, 1, TILE, LANES), lambda i: (i, tiles, 0, 0)),
            pl.BlockSpec((block, most, LANES), lambda i: (i, 0, 0)),
            pl.BlockSpec((held, features), lambda i: (0, 0)),
        ],
        out_specs=pl.BlockSpec((block, steps, most, features), lambda i: (i, 0, 0, 0)),
        scratch_shapes=[pltpu.VMEM((block, steps, most, held), BF16)],
        compiler_params=pltpu.CompilerParams(vmem_limit_bytes=VMEM),
        cost_estimate=pl.CostEstimate(
            flops=2 * groups * steps * most * held * features,
            bytes_accessed=2 * (s.size + up.size + groups * steps * most * features),
            transcendentals=0,
        ),
        name="expand",
    )(x, s, up)


def shares_kernel(order_ref, tokens_ref, weight_ref, out_ref):
    out_ref[0] = jnp.dot(tokens_ref[...], weight_ref[...], preferred_element_type=F32)


def base_shares(flat_tokens, query_weight):
    size = lax.axis_size("tp")
    rows, width = flat_tokens.shape
    columns = query_weight.shape[1] // size
    order = lax.rem(lax.axis_index("tp") + jnp.arange(size, dtype=jnp.int32), size)
    return pl.pallas_call(
        shares_kernel,
        out_shape=jax.ShapeDtypeStruct((size, rows, columns), F32),
        grid_spec=pltpu.PrefetchScalarGridSpec(
            num_scalar_prefetch=1,
            grid=(size,),
            in_specs=[
                pl.BlockSpec((rows, width), lambda k, order: (0, 0)),
                pl.BlockSpec((width, columns), lambda k, order: (0, order[k])),
            ],
            out_specs=pl.BlockSpec((1, rows, columns), lambda k, order: (k, 0, 0)),
        ),
        compiler_params=pltpu.CompilerParams(vmem_limit_bytes=VMEM),
        cost_estimate=pl.CostEstimate(
            flops=2 * rows * width * columns * size,
            bytes_accessed=2 * query_weight.size + 4 * rows * columns * size,
            transcendentals=0,
        ),
        name="shares",
    )(order, flat_tokens, query_weight)


def sum_over_tp(partial_value):
    size = lax.axis_size("tp")
    groups, most, lanes = partial_value.shape
    flat = partial_value.reshape(groups * most, lanes)
    got = lax.all_to_all(flat, "tp", split_axis=0, concat_axis=0, tiled=True)
    share = got.reshape(size, groups * most // size, lanes).astype(F32).sum(0).astype(BF16)
    copies = jnp.broadcast_to(share[None], (size,) + share.shape).reshape(groups * most, lanes)
    full = lax.all_to_all(copies, "tp", split_axis=0, concat_axis=0, tiled=True)
    return full.reshape(groups, most, lanes)


def body(tokens, query_weight, down_weight, up_weight, requests, row_slot_index):
    count = lax.axis_size("pool")
    size = lax.axis_size("tp")
    steps, rows, width = tokens.shape
    most = 4 * rows // count
    adapters, rank, _ = down_weight.shape
    features = up_weight.shape[-1]
    middle = steps * rows // 2
    right = [(i, (i + 1) % size) for i in range(size)]
    left = [(i, (i - 1) % size) for i in range(size)]

    sent = pack(requests[:, 0, :], row_slot_index, tokens, most)
    sent, late_tokens, late_slots = lax.optimization_barrier((sent, tokens, row_slot_index))
    x = lax.all_to_all(sent, "pool", split_axis=0, concat_axis=0, tiled=True)

    shares = base_shares(late_tokens.reshape(steps * rows, width), query_weight)
    far = size // 2
    top = lax.ppermute(shares[far, :middle].astype(BF16), "tp", right).astype(F32)
    low = lax.ppermute(shares[far, middle:].astype(BF16), "tp", left).astype(F32)
    going_right = jnp.concatenate([shares[far - 1, :middle] + top, shares[far - 1, middle:]], 0)
    going_left = jnp.concatenate([shares[far + 1, :middle], shares[far + 1, middle:] + low], 0)
    for ahead in range(far - 2, 0, -1):
        going_right = lax.ppermute(going_right.astype(BF16), "tp", right).astype(F32) + shares[ahead]
        going_left = lax.ppermute(going_left.astype(BF16), "tp", left).astype(F32) + shares[size - ahead]
    going_right, going_left = going_right.astype(BF16), going_left.astype(BF16)

    down_t = down_weight.reshape(adapters * rank, width).T
    shrink = sum_over_tp(shrink_rows(x, down_t, steps, most, rank))
    delta = expand_rows(x, shrink, up_weight.reshape(adapters * rank, features), steps, rank)
    delta, going_right, going_left = lax.optimization_barrier((delta, going_right, going_left))
    back = lax.all_to_all(delta, "pool", split_axis=0, concat_axis=0, tiled=True)
    from_left = lax.ppermute(going_right, "tp", right).astype(F32)
    from_right = lax.ppermute(going_left, "tp", left).astype(F32)
    base = shares[0] + from_left + from_right

    slots = late_slots[:, 0, :]
    before = slots[:, None, :] < jnp.arange(count, dtype=jnp.int32)[None, :, None]
    start = jnp.minimum(jnp.sum(before.astype(jnp.int32), axis=2), rows - most)
    mine = slots[:, :, None] == jnp.arange(count, dtype=jnp.int32)[None, None, :]
    own_start = jnp.sum(jnp.where(mine, start[:, None, :], 0), axis=2)
    place = (
        slots * (steps * most)
        + jnp.arange(steps, dtype=jnp.int32)[:, None] * most
        + jnp.arange(rows, dtype=jnp.int32)[None, :]
        - own_start
    ).reshape(steps * rows)
    spread = (place[:, None] == jnp.arange(count * steps * most, dtype=jnp.int32)[None, :]).astype(BF16)
    delta_rows = jnp.dot(
        spread, back.reshape(count * steps * most, features), preferred_element_type=F32
    )
    return (base + delta_rows).astype(BF16).reshape(steps, rows, features)


def solution(mesh):
    placed = (
        P(None, "pool", "tp"),
        P("tp", None),
        P("pool", None, "tp"),
        P("pool", None, "tp"),
        P(None, "pool", None),
        P(None, "pool", None),
    )
    return jax.shard_map(
        body, mesh=mesh, in_specs=placed, out_specs=P(None, "pool", "tp"), check_vma=False
    )
```

time: 195 us -> 159 us (0.82)
  blocking collectives: 102 us -> 0 us
  waiting for transfers between devices: 28.1 us -> 72.6 us
  starting transfers between devices: 15.7 us -> 43.1 us
  between operations: 13.5 us -> 0.21 us
  matrix products: 16.4 us -> 3.61 us
  Pallas kernels: 12.6 us -> 24.3 us
  other arithmetic: 0.44 us -> 5.39 us
  local copies, waits for them, and re-layouts: 6.54 us -> 9.11 us
    all_gather x1 -> x0, blocking collectives: 67.2 us -> none  [body(): asked = lax.all_gather(requests[:, 0, :], 'pool')]
    all_to_all x2 -> x0, blocking collectives: 34.4 us -> none  [the longest x1 20.2 us: sum_over_tp(): got = lax.all_to_all(flat, 'tp', split_axis=0, concat_axis=0, tiled=True)]
    all_to_all x1 -> x3, waiting for transfers between devices: 0.01 us -> 34.2 us  [the longest x1 23.6 us: body(): x = lax.all_to_all(sent, 'pool', split_axis=0, concat_axis=0, tiled=True)]
    ppermute x0 -> x8, waiting for transfers between devices: none -> 25.7 us  [the longest x1 11.7 us: body(): from_left = lax.ppermute(going_right, 'tp', right).astype(F32)]
    all_to_all x1, waiting for transfers between devices: 28.1 us -> 12.7 us  [body(): lax.all_to_all(delta, 'pool', split_axis=0, concat_axis=0, tiled=True)]
    ppermute x0 -> x8, starting transfers between devices: none -> 14 us  [the longest x1 5.65 us: body(): lax.ppermute(shares[far, middle:].astype(BF16), 'tp', left).astype(F32)]
    dot_general x2 -> x0, matrix products: 13.3 us -> none  [the longest x1 9.37 us: body(): jnp.dot(flat_tokens, query_weight, preferred_element_type=F32).astype(BF16)]
    pallas_call x2 -> x4, Pallas kernels: 12.6 us -> 24.3 us  [the longest x1 9.26 us: base_shares(): pl.pallas_call(shares_kernel, out_shape=jax.ShapeDtypeStruct((size, rows,...]
  transfers between devices with their start and end apart: 3 -> 12, of which waited for: 1 -> 9; matrix products, arithmetic and copies ran while one was open for 4% -> 6% of each run, Pallas kernels for 6% -> 10%
where the time goes in v2:
time: 159 us; the launch traced here: 158 us
  waiting for transfers between devices  72.6 us (46%)
  starting transfers between devices  43.1 us (27%)
  Pallas kernels  24.3 us (15%)
  local copies, waits for them, and re-layouts  9.11 us (6%)
  other arithmetic  5.39 us (3%)
  matrix products  3.61 us (2%)
    all_to_all x1, waiting for transfers between devices, body(): x = lax.all_to_all(sent, 'pool', split_axis=0, concat_axis=0, tiled=True)  23.6 us
    all_to_all x1, waiting for transfers between devices, body(): lax.all_to_all(delta, 'pool', split_axis=0, concat_axis=0, tiled=True)  12.7 us
    ppermute x1, waiting for transfers between devices, body(): from_left = lax.ppermute(going_right, 'tp', right).astype(F32)  11.7 us
    pallas_call x1, Pallas kernels, base_shares(): pl.pallas_call(shares_kernel, out_shape=jax.ShapeDtypeStruct((size, rows,...  9.26 us
    all_to_all x1, starting transfers between devices, body(): x = lax.all_to_all(sent, 'pool', split_axis=0, concat_axis=0, tiled=True)  8.77 us
    all_to_all x1, starting transfers between devices, body(): lax.all_to_all(delta, 'pool', split_axis=0, concat_axis=0, tiled=True)  8.73 us
    all_to_all x1, starting transfers between devices, sum_over_tp(): got = lax.all_to_all(flat, 'tp', split_axis=0, concat_axis=0, tiled=True)  8.19 us
    pallas_call x1, Pallas kernels, shrink_rows(): pl.pallas_call(functools.partial(shrink_kernel, rank), out_shape=jax.Shap...  7.27 us
  transfers between devices with their start and end apart: 12, of which 9 were waited for; matrix products, arithmetic and copies ran while one was open for 6% of the time, Pallas kernels for 10%

profile of v2, /device:TPU:1, one launch (start us, length us, event | category | flops | bytes accessed | tf_op | source)
XLA Modules:
  0.0 158.3 jit_solution(16637774701963974330)
XLA Ops:
  0.0 0.0 copy-start.2
  0.0 1.2 copy-done.2
  1.2 0.0 copy-start.4
  1.2 0.7 copy-done.4
  1.9 0.0 copy-start.6
  1.9 0.7 copy-done.6
  2.6 2.5 %pack.1 = bf16[32,33,16,128]{3,2,1,0:T(8,128)(2,1)S(1)} custom-call(s32[2,32]{1,0:T(2,128)S(1)} %bitcast.79, s32[2,1,256]{2,1,0:T(1,128)S(1)} %copy-done.4, bf16[2,256,1024]{2,1,0:T(8,128)(2,1)S(1)} %copy-done.2), custom_call_target="tpu_custom_call" | custom-call | flops 1073741824 | bytes 5373952 | tf_op jit(solution)/shard_map/pack/pallas_call | solution.py:48
  5.1 0.0 copy-start.1
  5.1 2.0 %copy-done.1 = bf16[32,33,16,128]{3,2,1,0:T(8,128)(2,1)} copy-done((bf16[32,33,16,128]{3,2,1,0:T(8,128)(2,1)}, bf16[32,33,16,128]{3,2,1,0:T(8,128)(2,1)S(1)}, u32[]{:S(2)}) %copy-start.1) | copy-done | bytes 4325400
  7.1 0.0 copy-start.3
  7.1 8.8 %all-to-all-start = ((bf16[32,33,16,128]{3,2,1,0:T(8,128)(2,1)}), bf16[32,33,16,128]{3,2,1,0:T(8,128)(2,1)}, u32[]{:S(2)}, u32[]{:S(2)}) async-start(bf16[32,33,16,128]{3,2,1,0:T(8,128)(2,1)} %copy-done.1), calls=%async_computation | async-start | bytes 8650752 | tf_op jit(solution)/shard_map/all_to_all | solution.py:224
  15.9 0.0 copy-done.3
  15.9 9.3 %shares.1 = f32[8,512,512]{2,1,0:T(8,128)S(1)} custom-call(s32[8]{0:T(128)S(1)} %compare_select_fusion.order_ref, bf16[512,1024]{1,0:T(8,128)(2,1)S(1)} %bitcast.76, bf16[1024,4096]{1,0:T(8,128)(2,1)} %weight_ref.1), custom_call_target="tpu_custom_call" | custom-call | flops 4294967296 | bytes 16777216 | tf_op jit(solution)/shard_map/shares/pallas_call | solution.py:178
  25.2 0.0 copy-start
  25.2 0.6 convert.17
  25.8 0.1 slice_bitcast_fusion.8
  25.8 5.7 %collective-permute-start.3 = (bf16[256,512]{1,0:T(8,128)(2,1)S(1)}, bf16[256,512]{1,0:T(8,128)(2,1)S(1)}, u32[]{:S(2)}, u32[]{:S(2)}) collective-permute-start(bf16[256,512]{1,0:T(8,128)(2,1)S(1)} %get-tuple-element.24), channel_id=1, source_target_pairs={{0,7},{1,0},{2,1},{3,2},{4,3},{5,4},{6,5},{7,6},{8,15},{9,8},{10,9... | collective-permute-start | bytes 786440 | tf_op jit(solution)/shard_map/ppermute | solution.py:229
  31.5 0.0 collective-permute-start
  31.5 5.4 %collective-permute-done.3 = bf16[256,512]{1,0:T(8,128)(2,1)S(1)} collective-permute-done((bf16[256,512]{1,0:T(8,128)(2,1)S(1)}, bf16[256,512]{1,0:T(8,128)(2,1)S(1)}, u32[]{:S(2)}, u32[]{:S(2)}) %collective-permute-start.3) | collective-permute-done | bytes 262176 | tf_op jit(solution)/shard_map/ppermute | solution.py:229
  36.9 3.2 %collective-permute-done = bf16[256,512]{1,0:T(8,128)(2,1)S(1)} collective-permute-done((bf16[256,512]{1,0:T(8,128)(2,1)S(1)}, bf16[256,512]{1,0:T(8,128)(2,1)S(1)}, u32[]{:S(2)}, u32[]{:S(2)}) %collective-permute-start) | collective-permute-done | bytes 262176 | tf_op jit(solution)/shard_map/ppermute | solution.py:228
  40.1 0.0 copy-done
  40.1 0.2 fusion.15
  40.3 0.1 collective-permute-start.1
  40.5 2.7 %collective-permute-start.4 = (bf16[512,512]{1,0:T(8,128)(2,1)S(1)}, bf16[512,512]{1,0:T(8,128)(2,1)}, u32[]{:S(2)}, u32[]{:S(2)}) collective-permute-start(bf16[512,512]{1,0:T(8,128)(2,1)S(1)} %pad_maximum_fusion.1), channel_id=1, source_target_pairs={{0,7},{1,0},{2,1},{3,2},{4,3},{5,4},{6,5},{7,6},{8,15},{9,8},{10,9... | collective-permute-start | bytes 1572872 | tf_op jit(solution)/shard_map/ppermute | solution.py:234
  43.2 2.9 %copy.9 = bf16[1024,1024]{0,1:T(8,128)(2,1)S(1)} copy(bf16[1024,1024]{1,0:T(8,128)(2,1)} %bitcast.81) | data formatting | bytes 4194304 | tf_op jit(solution)/shard_map/reshape | solution.py:237
  46.1 23.6 %all-to-all-done.names_ref.x_ref = bf16[32,33,16,128]{3,2,1,0:T(8,128)(2,1)} async-done(((bf16[32,33,16,128]{3,2,1,0:T(8,128)(2,1)}), bf16[32,33,16,128]{3,2,1,0:T(8,128)(2,1)}, u32[]{:S(2)}, u32[]{:S(2)}) %all-to-all-start) | async-done | bytes 4325408 | tf_op jit(solution)/shard_map/all_to_all | solution.py:224
  69.7 7.3 %shrink.1 = bf16[32,32,128]{2,1,0:T(8,128)(2,1)} custom-call(bf16[32,33,16,128]{3,2,1,0:T(8,128)(2,1)} %all-to-all-done.names_ref.x_ref, bf16[32,33,16,128]{3,2,1,0:T(8,128)(2,1)} %all-to-all-done.names_ref.x_ref, bf16[1024,1024]{1,0:T(8,128)(2,1)S(1)} %bitcast.77), custom_call_target="tpu_custom_call" | custom-call | flops 4294967296 | bytes 6422528 | tf_op jit(solution)/shard_map/shrink/pallas_call | solution.py:101
  76.9 8.2 %all-to-all-start.1 = ((bf16[8,128,128]{2,1,0:T(8,128)(2,1)}), bf16[8,128,128]{2,1,0:T(8,128)(2,1)S(1)}, u32[]{:S(2)}, u32[]{:S(2)}) async-start(bf16[8,128,128]{2,1,0:T(8,128)(2,1)} %bitcast.5), calls=%async_computation.1 | async-start | bytes 524288 | tf_op jit(solution)/shard_map/all_to_all | solution.py:204
  85.1 0.0 copy-start.7
  85.1 0.0 collective-permute-done.1
  85.1 0.0 collective-permute-done.4
  85.2 2.3 %fusion.5 = (bf16[512,512]{1,0:T(8,128)(2,1)S(1)}, bf16[512,512]{1,0:T(8,128)(2,1)S(1)}) fusion(f32[8,512,512]{2,1,0:T(8,128)} %copy-done, bf16[512,512]{1,0:T(8,128)(2,1)} %collective-permute-done.4, bf16[512,512]{1,0:T(8,128)(2,1)} %collective-permute-done.1), kind=kLoop, calls=%fused_computation.8 | loop fusion | flops 1572864 | bytes 4194304 | tf_op jit(solution)/shard_map/convert_element_type | solution.py:234
  87.4 2.7 %collective-permute-start.5 = (bf16[512,512]{1,0:T(8,128)(2,1)S(1)}, bf16[512,512]{1,0:T(8,128)(2,1)S(1)}, u32[]{:S(2)}, u32[]{:S(2)}) collective-permute-start(bf16[512,512]{1,0:T(8,128)(2,1)S(1)} %get-tuple-element.19), channel_id=1, source_target_pairs={{0,7},{1,0},{2,1},{3,2},{4,3},{5,4},{6,5},{7,6},{8,15},{9,8},{10,9... | collective-permute-start | bytes 1572872 | tf_op jit(solution)/shard_map/ppermute | solution.py:234
  90.2 0.0 collective-permute-start.2
  90.2 5.2 %all-to-all-done.1 = bf16[8,128,128]{2,1,0:T(8,128)(2,1)S(1)} async-done(((bf16[8,128,128]{2,1,0:T(8,128)(2,1)}), bf16[8,128,128]{2,1,0:T(8,128)(2,1)S(1)}, u32[]{:S(2)}, u32[]{:S(2)}) %all-to-all-start.1) | async-done | bytes 262176 | tf_op jit(solution)/shard_map/all_to_all | solution.py:204
  95.4 0.7 broadcast_in_dim.10
  96.1 3.4 %all-to-all-start.2 = ((bf16[8,128,128]{2,1,0:T(8,128)(2,1)}), bf16[8,128,128]{2,1,0:T(8,128)(2,1)S(1)}, u32[]{:S(2)}, u32[]{:S(2)}) async-start(bf16[8,128,128]{2,1,0:T(8,128)(2,1)} %broadcast_in_dim.10), calls=%async_computation.2 | async-start | bytes 524288 | tf_op jit(solution)/shard_map/all_to_all | solution.py:207
  99.6 4.1 %collective-permute-done.5 = bf16[512,512]{1,0:T(8,128)(2,1)S(1)} collective-permute-done((bf16[512,512]{1,0:T(8,128)(2,1)S(1)}, bf16[512,512]{1,0:T(8,128)(2,1)S(1)}, u32[]{:S(2)}, u32[]{:S(2)}) %collective-permute-start.5) | collective-permute-done | bytes 524320 | tf_op jit(solution)/shard_map/ppermute | solution.py:234
  103.7 1.3 collective-permute-done.2
  105.0 2.0 %fusion.3 = (bf16[512,512]{1,0:T(8,128)(2,1)S(1)}, bf16[512,512]{1,0:T(8,128)(2,1)S(1)}) fusion(f32[8,512,512]{2,1,0:T(8,128)} %copy-done, bf16[512,512]{1,0:T(8,128)(2,1)S(1)} %collective-permute-done.5, bf16[512,512]{1,0:T(8,128)(2,1)} %collective-permute-done.2), kind=kLoop, calls=%fused_computation.5 | loop fusion | flops 1572864 | bytes 4194304 | tf_op jit(solution)/shard_map/convert_element_type | solution.py:235
  107.0 5.4 %all-to-all-done.2 = bf16[8,128,128]{2,1,0:T(8,128)(2,1)S(1)} async-done(((bf16[8,128,128]{2,1,0:T(8,128)(2,1)}), bf16[8,128,128]{2,1,0:T(8,128)(2,1)S(1)}, u32[]{:S(2)}, u32[]{:S(2)}) %all-to-all-start.2) | async-done | bytes 262176 | tf_op jit(solution)/shard_map/all_to_all | solution.py:207
  112.4 0.0 copy-done.7
  112.4 0.0 copy-start.5
  112.4 5.2 %expand.1 = bf16[32,2,32,512]{3,2,1,0:T(8,128)(2,1)} custom-call(bf16[32,33,16,128]{3,2,1,0:T(8,128)(2,1)} %all-to-all-done.names_ref.x_ref, bf16[32,32,128]{2,1,0:T(8,128)(2,1)S(1)} %bitcast.78, bf16[1024,512]{1,0:T(8,128)(2,1)S(1)} %bitcast.80), custom_call_target="tpu_custom_call" | custom-call | flops 2147483648 | bytes 3407872 | tf_op jit(solution)/shard_map/expand/pallas_call | solution.py:148
  117.7 8.7 %all-to-all-start.3 = ((bf16[32,2,32,512]{3,2,1,0:T(8,128)(2,1)}), bf16[32,2,32,512]{3,2,1,0:T(8,128)(2,1)S(1)}, u32[]{:S(2)}, u32[]{:S(2)}) async-start(bf16[32,2,32,512]{3,2,1,0:T(8,128)(2,1)} %expand.1), calls=%async_computation.3 | async-start | bytes 4194304 | tf_op jit(solution)/shard_map/all_to_all | solution.py:241
  126.4 0.1 broadcast_bitcast_fusion
  126.5 0.0 copy-done.5
  126.5 0.1 convert_reduce_fusion
  126.6 0.4 collective-permute-start.6
  127.0 2.4 %collective-permute-start.7 = (bf16[512,512]{1,0:T(8,128)(2,1)S(1)}, bf16[512,512]{1,0:T(8,128)(2,1)}, u32[]{:S(2)}, u32[]{:S(2)}) collective-permute-start(bf16[512,512]{1,0:T(8,128)(2,1)S(1)} %get-tuple-element.14), channel_id=1, source_target_pairs={{0,7},{1,0},{2,1},{3,2},{4,3},{5,4},{6,5},{7,6},{8,15},{9,8},{10,9... | collective-permute-start | bytes 1572872 | tf_op jit(solution)/shard_map/ppermute | solution.py:243
  129.4 0.1 select_reduce_fusion
  129.5 11.7 %collective-permute-done.6 = bf16[512,512]{1,0:T(8,128)(2,1)S(1)} collective-permute-done((bf16[512,512]{1,0:T(8,128)(2,1)S(1)}, bf16[512,512]{1,0:T(8,128)(2,1)S(1)}, u32[]{:S(2)}, u32[]{:S(2)}) %collective-permute-start.6) | collective-permute-done | bytes 524320 | tf_op jit(solution)/shard_map/ppermute | solution.py:242
  141.2 0.0 copy-start.8
  141.2 0.8 copy-done.8
  142.0 0.0 collective-permute-done.7
  142.0 12.7 %all-to-all-done.3 = bf16[32,2,32,512]{3,2,1,0:T(8,128)(2,1)S(1)} async-done(((bf16[32,2,32,512]{3,2,1,0:T(8,128)(2,1)}), bf16[32,2,32,512]{3,2,1,0:T(8,128)(2,1)S(1)}, u32[]{:S(2)}, u32[]{:S(2)}) %all-to-all-start.3) | async-done | bytes 2097184 | tf_op jit(solution)/shard_map/all_to_all | solution.py:241
  154.7 3.6 %fusion.13 = bf16[512,512]{1,0:T(8,128)(2,1)} fusion(f32[8,512,512]{2,1,0:T(8,128)} %copy-done, bf16[512,512]{1,0:T(8,128)(2,1)} %collective-permute-done.7, bf16[512,512]{1,0:T(8,128)(2,1)} %copy-done.8, bf16[2048,512]{1,0:T(8,128)(2,1)S(1)} %bitcast.82, s32[512]{0:T(512)S(1)} %add_subtract_fusion), kind=kOutput, calls=%fused_computation.19 | convolution fusion | flops 1076363264 | bytes 4720640 | tf_op jit(solution)/shard_map/dot_general | solution.py:258
  (13 shorter events, 0.2 us)
Async XLA Ops:
  0.0 1.2 copy-start.2
  1.2 0.7 copy-start.4
  1.9 0.7 copy-start.6
  5.1 2.0 %copy-start.1 = (bf16[32,33,16,128]{3,2,1,0:T(8,128)(2,1)}, bf16[32,33,16,128]{3,2,1,0:T(8,128)(2,1)S(1)}, u32[]{:S(2)}) copy-start(bf16[32,33,16,128]{3,2,1,0:T(8,128)(2,1)S(1)} %pack.1) | copy-start | bytes 12976132
  7.1 8.8 %copy-start.3 = (bf16[2,256,1024]{2,1,0:T(8,128)(2,1)S(1)}, bf16[2,256,1024]{2,1,0:T(8,128)(2,1)}, u32[]{:S(2)}) copy-start(bf16[2,256,1024]{2,1,0:T(8,128)(2,1)} %tokens_ref.1) | copy-start | bytes 3145732
  7.1 62.6 %all-to-all-start = ((bf16[32,33,16,128]{3,2,1,0:T(8,128)(2,1)}), bf16[32,33,16,128]{3,2,1,0:T(8,128)(2,1)}, u32[]{:S(2)}, u32[]{:S(2)}) async-start(bf16[32,33,16,128]{3,2,1,0:T(8,128)(2,1)} %copy-done.1), calls=%async_computation | async-start | bytes 8650752 | tf_op jit(solution)/shard_map/all_to_all | solution.py:224
  25.2 14.9 %copy-start = (f32[8,512,512]{2,1,0:T(8,128)}, f32[8,512,512]{2,1,0:T(8,128)S(1)}, u32[]{:S(2)}) copy-start(f32[8,512,512]{2,1,0:T(8,128)S(1)} %shares.1) | copy-start | bytes 25165828
  25.8 11.0 %collective-permute-start.3 = (bf16[256,512]{1,0:T(8,128)(2,1)S(1)}, bf16[256,512]{1,0:T(8,128)(2,1)S(1)}, u32[]{:S(2)}, u32[]{:S(2)}) collective-permute-start(bf16[256,512]{1,0:T(8,128)(2,1)S(1)} %get-tuple-element.24), channel_id=1, source_target_pairs={{0,7},{1,0},{2,1},{3,2},{4,3},{5,4},{6,5},{7,6},{8,15},{9,8},{10,9... | collective-permute-start | bytes 786440 | tf_op jit(solution)/shard_map/ppermute | solution.py:229
  31.5 8.6 %collective-permute-start = (bf16[256,512]{1,0:T(8,128)(2,1)S(1)}, bf16[256,512]{1,0:T(8,128)(2,1)S(1)}, u32[]{:S(2)}, u32[]{:S(2)}) collective-permute-start(bf16[256,512]{1,0:T(8,128)(2,1)S(1)} %get-tuple-element.26), channel_id=1, source_target_pairs={{0,1},{1,2},{2,3},{3,4},{4,5},{5,6},{6,7},{7,0},{8,9},{9,10},{10,1... | collective-permute-start | bytes 786440 | tf_op jit(solution)/shard_map/ppermute | solution.py:228
  40.3 44.8 %collective-permute-start.1 = (bf16[512,512]{1,0:T(8,128)(2,1)S(1)}, bf16[512,512]{1,0:T(8,128)(2,1)}, u32[]{:S(2)}, u32[]{:S(2)}) collective-permute-start(bf16[512,512]{1,0:T(8,128)(2,1)S(1)} %pad_maximum_fusion), channel_id=1, source_target_pairs={{0,1},{1,2},{2,3},{3,4},{4,5},{5,6},{6,7},{7,0},{8,9},{9,10},{10,1... | collective-permute-start | bytes 1572872 | tf_op jit(solution)/shard_map/ppermute | solution.py:233
  40.5 44.7 %collective-permute-start.4 = (bf16[512,512]{1,0:T(8,128)(2,1)S(1)}, bf16[512,512]{1,0:T(8,128)(2,1)}, u32[]{:S(2)}, u32[]{:S(2)}) collective-permute-start(bf16[512,512]{1,0:T(8,128)(2,1)S(1)} %pad_maximum_fusion.1), channel_id=1, source_target_pairs={{0,7},{1,0},{2,1},{3,2},{4,3},{5,4},{6,5},{7,6},{8,15},{9,8},{10,9... | collective-permute-start | bytes 1572872 | tf_op jit(solution)/shard_map/ppermute | solution.py:234
  76.9 18.4 %all-to-all-start.1 = ((bf16[8,128,128]{2,1,0:T(8,128)(2,1)}), bf16[8,128,128]{2,1,0:T(8,128)(2,1)S(1)}, u32[]{:S(2)}, u32[]{:S(2)}) async-start(bf16[8,128,128]{2,1,0:T(8,128)(2,1)} %bitcast.5), calls=%async_computation.1 | async-start | bytes 524288 | tf_op jit(solution)/shard_map/all_to_all | solution.py:204
  85.1 27.3 %copy-start.7 = (bf16[16,64,512]{2,1,0:T(8,128)(2,1)S(1)}, bf16[16,64,512]{2,1,0:T(8,128)(2,1)}, u32[]{:S(2)}) copy-start(bf16[16,64,512]{2,1,0:T(8,128)(2,1)} %param.9) | copy-start | bytes 3145732
  87.4 16.2 %collective-permute-start.5 = (bf16[512,512]{1,0:T(8,128)(2,1)S(1)}, bf16[512,512]{1,0:T(8,128)(2,1)S(1)}, u32[]{:S(2)}, u32[]{:S(2)}) collective-permute-start(bf16[512,512]{1,0:T(8,128)(2,1)S(1)} %get-tuple-element.19), channel_id=1, source_target_pairs={{0,7},{1,0},{2,1},{3,2},{4,3},{5,4},{6,5},{7,6},{8,15},{9,8},{10,9... | collective-permute-start | bytes 1572872 | tf_op jit(solution)/shard_map/ppermute | solution.py:234
  90.2 14.8 %collective-permute-start.2 = (bf16[512,512]{1,0:T(8,128)(2,1)S(1)}, bf16[512,512]{1,0:T(8,128)(2,1)}, u32[]{:S(2)}, u32[]{:S(2)}) collective-permute-start(bf16[512,512]{1,0:T(8,128)(2,1)S(1)} %get-tuple-element.20), channel_id=1, source_target_pairs={{0,1},{1,2},{2,3},{3,4},{4,5},{5,6},{6,7},{7,0},{8,9},{9,10},{10,1... | collective-permute-start | bytes 1572872 | tf_op jit(solution)/shard_map/ppermute | solution.py:233
  96.1 16.3 %all-to-all-start.2 = ((bf16[8,128,128]{2,1,0:T(8,128)(2,1)}), bf16[8,128,128]{2,1,0:T(8,128)(2,1)S(1)}, u32[]{:S(2)}, u32[]{:S(2)}) async-start(bf16[8,128,128]{2,1,0:T(8,128)(2,1)} %broadcast_in_dim.10), calls=%async_computation.2 | async-start | bytes 524288 | tf_op jit(solution)/shard_map/all_to_all | solution.py:207
  112.4 14.1 %copy-start.5 = (s32[2,1,256]{2,1,0:T(1,128)S(1)}, s32[2,1,256]{2,1,0:T(1,128)}, u32[]{:S(2)}) copy-start(s32[2,1,256]{2,1,0:T(1,128)} %slots_ref.1) | copy-start | bytes 6148
  117.7 37.0 %all-to-all-start.3 = ((bf16[32,2,32,512]{3,2,1,0:T(8,128)(2,1)}), bf16[32,2,32,512]{3,2,1,0:T(8,128)(2,1)S(1)}, u32[]{:S(2)}, u32[]{:S(2)}) async-start(bf16[32,2,32,512]{3,2,1,0:T(8,128)(2,1)} %expand.1), calls=%async_computation.3 | async-start | bytes 4194304 | tf_op jit(solution)/shard_map/all_to_all | solution.py:241
  126.6 14.6 %collective-permute-start.6 = (bf16[512,512]{1,0:T(8,128)(2,1)S(1)}, bf16[512,512]{1,0:T(8,128)(2,1)S(1)}, u32[]{:S(2)}, u32[]{:S(2)}) collective-permute-start(bf16[512,512]{1,0:T(8,128)(2,1)S(1)} %get-tuple-element.13), channel_id=1, source_target_pairs={{0,1},{1,2},{2,3},{3,4},{4,5},{5,6},{6,7},{7,0},{8,9},{9,10},{10,1... | collective-permute-start | bytes 1572872 | tf_op jit(solution)/shard_map/ppermute | solution.py:242
  127.0 15.0 %collective-permute-start.7 = (bf16[512,512]{1,0:T(8,128)(2,1)S(1)}, bf16[512,512]{1,0:T(8,128)(2,1)}, u32[]{:S(2)}, u32[]{:S(2)}) collective-permute-start(bf16[512,512]{1,0:T(8,128)(2,1)S(1)} %get-tuple-element.14), channel_id=1, source_target_pairs={{0,7},{1,0},{2,1},{3,2},{4,3},{5,4},{6,5},{7,6},{8,15},{9,8},{10,9... | collective-permute-start | bytes 1572872 | tf_op jit(solution)/shard_map/ppermute | solution.py:243
  141.2 0.8 copy-start.8

commit v3 on v2

--- a/solution.py
+++ b/solution.py
@@ -11,7 +11,8 @@
 F32 = jnp.float32
 LANES = 128
 TILE = 16
-VMEM = 40 << 20
+VMEM = 24 << 20
+FULL = 62 << 20
 
 
 def pack_kernel(asked_ref, slots_ref, tokens_ref, out_ref):
@@ -41,7 +42,7 @@
         out_ref[s, tiles] = names.astype(F32).astype(BF16)
 
 
-def pack(asked, slots, tokens, most, block=8):
+def pack(asked, slots, tokens, most, block=16):
     steps, rows, width = tokens.shape
     count = asked.shape[1]
     tiles = steps * (most // TILE) * (width // LANES)
@@ -57,7 +58,7 @@
             ],
             out_specs=pl.BlockSpec((block, tiles + 1, TILE, LANES), lambda i, asked: (i, 0, 0, 0)),
         ),
-        compiler_params=pltpu.CompilerParams(vmem_limit_bytes=VMEM),
+        compiler_params=pltpu.CompilerParams(vmem_limit_bytes=FULL),
         cost_estimate=pl.CostEstimate(
             flops=2 * count * steps * most * rows * width,
             bytes_accessed=2 * (tokens.size + count * (tiles + 1) * TILE * LANES),
@@ -95,7 +96,7 @@
     out_ref[...] = out.astype(BF16).reshape(out_ref.shape)
 
 
-def shrink_rows(x, down_t, steps, most, rank, block=8):
+def shrink_rows(x, down_t, steps, most, rank, block=16):
     groups, tiles = x.shape[0], x.shape[1] - 1
     width, held = down_t.shape
     return pl.pallas_call(
@@ -156,7 +157,7 @@
         ],
         out_specs=pl.BlockSpec((block, steps, most, features), lambda i: (i, 0, 0, 0)),
         scratch_shapes=[pltpu.VMEM((block, steps, most, held), BF16)],
-        compiler_params=pltpu.CompilerParams(vmem_limit_bytes=VMEM),
+        compiler_params=pltpu.CompilerParams(vmem_limit_bytes=FULL),
         cost_estimate=pl.CostEstimate(
             flops=2 * groups * steps * most * held * features,
             bytes_accessed=2 * (s.size + up.size + groups * steps * most * features),
@@ -170,17 +171,18 @@
     out_ref[0] = jnp.dot(tokens_ref[...], weight_ref[...], preferred_element_type=F32)
 
 
-def base_shares(flat_tokens, query_weight):
+def base_shares(flat_tokens, query_weight, distances):
     size = lax.axis_size("tp")
     rows, width = flat_tokens.shape
     columns = query_weight.shape[1] // size
-    order = lax.rem(lax.axis_index("tp") + jnp.arange(size, dtype=jnp.int32), size)
+    order = lax.rem(lax.axis_index("tp") + jnp.array(distances, jnp.int32), size)
+    amount = len(distances)
     return pl.pallas_call(
         shares_kernel,
-        out_shape=jax.ShapeDtypeStruct((size, rows, columns), F32),
+        out_shape=jax.ShapeDtypeStruct((amount, rows, columns), F32),
         grid_spec=pltpu.PrefetchScalarGridSpec(
             num_scalar_prefetch=1,
-            grid=(size,),
+            grid=(amount,),
             in_specs=[
                 pl.BlockSpec((rows, width), lambda k, order: (0, 0)),
                 pl.BlockSpec((width, columns), lambda k, order: (0, order[k])),
@@ -189,12 +191,64 @@
         ),
         compiler_params=pltpu.CompilerParams(vmem_limit_bytes=VMEM),
         cost_estimate=pl.CostEstimate(
-            flops=2 * rows * width * columns * size,
-            bytes_accessed=2 * query_weight.size + 4 * rows * columns * size,
+            flops=2 * rows * width * columns * amount,
+            bytes_accessed=2 * width * columns * amount + 4 * rows * columns * amount,
             transcendentals=0,
         ),
         name="shares",
     )(order, flat_tokens, query_weight)
+
+
+def first_sums_kernel(shares_ref, top_ref, low_ref, right_ref, left_ref):
+    middle = top_ref.shape[0]
+    right_ref[:middle] = (shares_ref[0, :middle] + top_ref[...].astype(F32)).astype(BF16)
+    right_ref[middle:] = shares_ref[0, middle:].astype(BF16)
+    left_ref[:middle] = shares_ref[1, :middle].astype(BF16)
+    left_ref[middle:] = (shares_ref[1, middle:] + low_ref[...].astype(F32)).astype(BF16)
+
+
+def first_sums(shares, top, low):
+    _, rows, columns = shares.shape
+    out = jax.ShapeDtypeStruct((rows, columns), BF16)
+    return pl.pallas_call(
+        first_sums_kernel,
+        out_shape=(out, out),
+        compiler_params=pltpu.CompilerParams(vmem_limit_bytes=VMEM),
+        cost_estimate=pl.CostEstimate(
+            flops=2 * rows * columns, bytes_accessed=14 * rows * columns, transcendentals=0
+        ),
+        name="first_sums",
+    )(shares, top, low)
+
+
+def join_kernel(spread_ref, back_ref, base_ref, out_ref):
+    groups, _, most, features = back_ref.shape
+    back = back_ref[...].reshape(groups * most, features)
+    delta = jnp.dot(spread_ref[0], back, preferred_element_type=F32)
+    out_ref[0] = (base_ref[0] + delta).astype(BF16)
+
+
+def join(spread, back, base):
+    steps, rows, places = spread.shape
+    groups, _, most, features = back.shape
+    return pl.pallas_call(
+        join_kernel,
+        out_shape=jax.ShapeDtypeStruct((steps, rows, features), BF16),
+        grid=(steps,),
+        in_specs=[
+            pl.BlockSpec((1, rows, places), lambda t: (t, 0, 0)),
+            pl.BlockSpec((groups, 1, most, features), lambda t: (0, t, 0, 0)),
+            pl.BlockSpec((1, rows, features), lambda t: (t, 0, 0)),
+        ],
+        out_specs=pl.BlockSpec((1, rows, features), lambda t: (t, 0, 0)),
+        compiler_params=pltpu.CompilerParams(vmem_limit_bytes=FULL),
+        cost_estimate=pl.CostEstimate(
+            flops=2 * steps * rows * places * features,
+            bytes_accessed=2 * (spread.size + back.size) + 6 * base.size,
+            transcendentals=0,
+        ),
+        name="join",
+    )(spread, back, base)
 
 
 def sum_over_tp(partial_value):
@@ -223,16 +277,22 @@
     sent, late_tokens, late_slots = lax.optimization_barrier((sent, tokens, row_slot_index))
     x = lax.all_to_all(sent, "pool", split_axis=0, concat_axis=0, tiled=True)
 
-    shares = base_shares(late_tokens.reshape(steps * rows, width), query_weight)
+    late_tokens = late_tokens.reshape(steps * rows, width)
     far = size // 2
-    top = lax.ppermute(shares[far, :middle].astype(BF16), "tp", right).astype(F32)
-    low = lax.ppermute(shares[far, middle:].astype(BF16), "tp", left).astype(F32)
-    going_right = jnp.concatenate([shares[far - 1, :middle] + top, shares[far - 1, middle:]], 0)
-    going_left = jnp.concatenate([shares[far + 1, :middle], shares[far + 1, middle:] + low], 0)
-    for ahead in range(far - 2, 0, -1):
-        going_right = lax.ppermute(going_right.astype(BF16), "tp", right).astype(F32) + shares[ahead]
-        going_left = lax.ppermute(going_left.astype(BF16), "tp", left).astype(F32) + shares[size - ahead]
-    going_right, going_left = going_right.astype(BF16), going_left.astype(BF16)
+    farthest = base_shares(late_tokens, query_weight, [far])[0].astype(BF16)
+    top = lax.ppermute(farthest[:middle], "tp", right)
+    low = lax.ppermute(farthest[middle:], "tp", left)
+    late_tokens, _ = lax.optimization_barrier((late_tokens, farthest))
+    near = [d for ahead in range(far - 2, 0, -1) for d in (ahead, size - ahead)] + [0]
+    first = base_shares(late_tokens, query_weight, [far - 1, far + 1])
+    late_tokens, first = lax.optimization_barrier((late_tokens, first))
+    going_right, going_left = first_sums(first, top, low)
+    shares = base_shares(late_tokens, query_weight, near)
+    for hop in range(far - 2):
+        going_right = lax.ppermute(going_right, "tp", right).astype(F32) + shares[2 * hop]
+        going_left = lax.ppermute(going_left, "tp", left).astype(F32) + shares[2 * hop + 1]
+        going_right, going_left = going_right.astype(BF16), going_left.astype(BF16)
+    x, going_right, going_left = lax.optimization_barrier((x, going_right, going_left))
 
     down_t = down_weight.reshape(adapters * rank, width).T
     shrink = sum_over_tp(shrink_rows(x, down_t, steps, most, rank))
@@ -241,24 +301,16 @@
     back = lax.all_to_all(delta, "pool", split_axis=0, concat_axis=0, tiled=True)
     from_left = lax.ppermute(going_right, "tp", right).astype(F32)
     from_right = lax.ppermute(going_left, "tp", left).astype(F32)
-    base = shares[0] + from_left + from_right
+    base = (shares[-1] + from_left + from_right).reshape(steps, rows, features)
 
     slots = late_slots[:, 0, :]
     before = slots[:, None, :] < jnp.arange(count, dtype=jnp.int32)[None, :, None]
     start = jnp.minimum(jnp.sum(before.astype(jnp.int32), axis=2), rows - most)
     mine = slots[:, :, None] == jnp.arange(count, dtype=jnp.int32)[None, None, :]
     own_start = jnp.sum(jnp.where(mine, start[:, None, :], 0), axis=2)
-    place = (
-        slots * (steps * most)
-        + jnp.arange(steps, dtype=jnp.int32)[:, None] * most
-        + jnp.arange(rows, dtype=jnp.int32)[None, :]
-        - own_start
-    ).reshape(steps * rows)
-    spread = (place[:, None] == jnp.arange(count * steps * most, dtype=jnp.int32)[None, :]).astype(BF16)
-    delta_rows = jnp.dot(
-        spread, back.reshape(count * steps * most, features), preferred_element_type=F32
-    )
-    return (base + delta_rows).astype(BF16).reshape(steps, rows, features)
+    place = slots * most + jnp.arange(rows, dtype=jnp.int32)[None, :] - own_start
+    spread = (place[:, :, None] == jnp.arange(count * most, dtype=jnp.int32)[None, None, :]).astype(BF16)
+    return join(spread, back, base)
 
 
 def solution(mesh):

time: 159 us -> 153 us (0.962)
  blocking collectives: 0 us -> 30.6 us
  waiting for transfers between devices: 72.6 us -> 48.6 us
  starting transfers between devices: 43.1 us -> 30.2 us
  Pallas kernels: 24.3 us -> 28.1 us
  matrix products: 3.61 us -> 0 us
  other arithmetic: 5.39 us -> 7.49 us
  local copies, waits for them, and re-layouts: 9.11 us -> 7.13 us
    all_to_all x0 -> x2, blocking collectives: none -> 30.6 us  [the longest x1 18.2 us: sum_over_tp(): got = lax.all_to_all(flat, 'tp', split_axis=0, concat_axis=0, tiled=True)]
    all_to_all x1, waiting for transfers between devices: 23.6 us -> 4.93 us  [body(): x = lax.all_to_all(sent, 'pool', split_axis=0, concat_axis=0, tiled=True)]
    all_to_all x2 -> x0, starting transfers between devices: 11.6 us -> none  [the longest x1 8.19 us: sum_over_tp(): got = lax.all_to_all(flat, 'tp', split_axis=0, concat_axis=0, tiled=True)]
    all_to_all x2 -> x0, waiting for transfers between devices: 10.6 us -> none  [the longest x1 5.43 us: sum_over_tp(): full = lax.all_to_all(copies, 'tp', split_axis=0, concat_axis=0, tiled=True)]
    ppermute x1, waiting for transfers between devices: 11.7 us -> 1.1 us  [body(): from_left = lax.ppermute(going_right, 'tp', right).astype(F32)]
    ppermute x1, waiting for transfers between devices: 0.01 us -> 10.5 us  [body(): from_right = lax.ppermute(going_left, 'tp', left).astype(F32)]
    ppermute x6, waiting for transfers between devices: 14 us -> 20.9 us  [the longest x2 13.1 us: body(): lax.ppermute(going_left, 'tp', left).astype(F32) + shares[2 * hop + 1]]
    dot_general x1 -> x0, matrix products: 3.61 us -> none  [body(): jnp.dot(spread, back.reshape(count * steps * most, features), preferred_e...]
  transfers between devices with their start and end apart: 12 -> 10, of which waited for: 9 -> 9; matrix products, arithmetic and copies ran while one was open for 6% -> 7% of each run, Pallas kernels for 10% -> 5%
where the time goes in v3:
time: 153 us; the launch traced here: 152 us
  waiting for transfers between devices  48.6 us (32%)
  blocking collectives  30.6 us (20%)
  starting transfers between devices  30.2 us (20%)
  Pallas kernels  28.1 us (18%)
  other arithmetic  7.49 us (5%)
  local copies, waits for them, and re-layouts  7.13 us (5%)
    all_to_all x1, blocking collectives, sum_over_tp(): got = lax.all_to_all(flat, 'tp', split_axis=0, concat_axis=0, tiled=True)  18.2 us
    ppermute x2, waiting for transfers between devices, body(): lax.ppermute(going_left, 'tp', left).astype(F32) + shares[2 * hop + 1]  13.1 us
    all_to_all x1, blocking collectives, sum_over_tp(): full = lax.all_to_all(copies, 'tp', split_axis=0, concat_axis=0, tiled=True)  12.5 us
    all_to_all x1, waiting for transfers between devices, body(): lax.all_to_all(delta, 'pool', split_axis=0, concat_axis=0, tiled=True)  11.2 us
    ppermute x1, waiting for transfers between devices, body(): from_right = lax.ppermute(going_left, 'tp', left).astype(F32)  10.5 us
    all_to_all x1, starting transfers between devices, body(): lax.all_to_all(delta, 'pool', split_axis=0, concat_axis=0, tiled=True)  10.1 us
    all_to_all x1, starting transfers between devices, body(): x = lax.all_to_all(sent, 'pool', split_axis=0, concat_axis=0, tiled=True)  8.77 us
    pallas_call x3, Pallas kernels, base_shares(): pl.pallas_call(shares_kernel, out_shape=jax.ShapeDtypeStruct((amount, row...  7.43 us
  transfers between devices with their start and end apart: 10, of which 9 were waited for; matrix products, arithmetic and copies ran while one was open for 7% of the time, Pallas kernels for 5%

profile of v3, /device:TPU:1, one launch (start us, length us, event | category | flops | bytes accessed | tf_op | source)
XLA Modules:
  0.0 152.3 jit_solution(11443035979400045339)
XLA Ops:
  0.0 4.9 %pack.1 = bf16[32,33,16,128]{3,2,1,0:T(8,128)(2,1)} custom-call(s32[2,32]{1,0:T(2,128)} %bitcast.60, s32[2,1,256]{2,1,0:T(1,128)} %slots_ref.1, bf16[2,256,1024]{2,1,0:T(8,128)(2,1)} %tokens_ref.1), custom_call_target="tpu_custom_call" | custom-call | flops 1073741824 | bytes 5373952 | tf_op jit(solution)/shard_map/pack/pallas_call | solution.py:49
  4.9 0.0 copy-start.2
  4.9 8.8 %all-to-all-start = ((bf16[32,33,16,128]{3,2,1,0:T(8,128)(2,1)}), bf16[32,33,16,128]{3,2,1,0:T(8,128)(2,1)}, u32[]{:S(2)}, u32[]{:S(2)}) async-start(bf16[32,33,16,128]{3,2,1,0:T(8,128)(2,1)} %pack.1), calls=%async_computation | async-start | bytes 8650752 | tf_op jit(solution)/shard_map/all_to_all | solution.py:278
  13.7 0.0 copy-done.2
  13.7 0.0 copy-start
  13.7 3.4 %copy-done = bf16[1024,4096]{1,0:T(8,128)(2,1)S(1)} copy-done((bf16[1024,4096]{1,0:T(8,128)(2,1)S(1)}, bf16[1024,4096]{1,0:T(8,128)(2,1)}, u32[]{:S(2)}) %copy-start) | copy-done | bytes 8388632
  17.1 0.0 copy-start.6
  17.1 0.7 shares.4
  17.8 0.1 convert_element_type.44
  17.9 0.0 slice-start
  18.0 1.7 %collective-permute-start = (bf16[256,512]{1,0:T(8,128)(2,1)S(1)}, bf16[256,512]{1,0:T(8,128)(2,1)S(1)}, u32[]{:S(2)}, u32[]{:S(2)}) collective-permute-start(bf16[256,512]{1,0:T(8,128)(2,1)S(1)} %get-tuple-element.36), channel_id=1, source_target_pairs={{0,1},{1,2},{2,3},{3,4},{4,5},{5,6},{6,7},{7,0},{8,9},{9,10},{10,1... | collective-permute-start | bytes 786440 | tf_op jit(solution)/shard_map/ppermute | solution.py:283
  19.7 4.0 %collective-permute-start.1 = (bf16[256,512]{1,0:T(8,128)(2,1)S(1)}, bf16[256,512]{1,0:T(8,128)(2,1)S(1)}, u32[]{:S(2)}, u32[]{:S(2)}) collective-permute-start(bf16[256,512]{1,0:T(8,128)(2,1)S(1)} %get-tuple-element.35), channel_id=1, source_target_pairs={{0,7},{1,0},{2,1},{3,2},{4,3},{5,4},{6,5},{7,6},{8,15},{9,8},{10,9... | collective-permute-start | bytes 786440 | tf_op jit(solution)/shard_map/ppermute | solution.py:284
  23.7 0.0 copy-done.6
  23.7 0.0 copy-start.5
  23.7 0.0 slice-start.1
  23.7 2.2 %shares.3.shares_ref = f32[2,512,512]{2,1,0:T(8,128)S(1)} custom-call(s32[2]{0:T(128)S(1)} %compare_select_fusion.2.order_ref, bf16[512,1024]{1,0:T(8,128)(2,1)S(1)} %bitcast.51, bf16[1024,4096]{1,0:T(8,128)(2,1)S(1)} %copy-done), custom_call_target="tpu_custom_call" | custom-call | flops 1073741824 | bytes 4194304 | tf_op jit(solution)/shard_map/shares/pallas_call | solution.py:180
  25.9 4.3 %collective-permute-done.top_ref = bf16[256,512]{1,0:T(8,128)(2,1)S(1)} collective-permute-done((bf16[256,512]{1,0:T(8,128)(2,1)S(1)}, bf16[256,512]{1,0:T(8,128)(2,1)S(1)}, u32[]{:S(2)}, u32[]{:S(2)}) %collective-permute-start) | collective-permute-done | bytes 262176 | tf_op jit(solution)/shard_map/ppermute | solution.py:283
  30.2 0.0 collective-permute-done.1.low_ref
  30.2 0.1 first_sums.1
  30.3 2.5 %collective-permute-start.4 = (bf16[512,512]{1,0:T(8,128)(2,1)S(1)}, bf16[512,512]{1,0:T(8,128)(2,1)S(1)}, u32[]{:S(2)}, u32[]{:S(2)}) collective-permute-start(bf16[512,512]{1,0:T(8,128)(2,1)S(1)} %get-tuple-element.24), channel_id=1, source_target_pairs={{0,7},{1,0},{2,1},{3,2},{4,3},{5,4},{6,5},{7,6},{8,15},{9,8},{10,9... | collective-permute-start | bytes 1572872 | tf_op jit(solution)/shard_map/ppermute | solution.py:293
  32.8 0.0 collective-permute-start.2
  32.8 0.0 copy-done.5
  32.8 0.0 slice-done
  32.9 0.0 slice-done.1
  32.9 4.6 %shares.5 = f32[5,512,512]{2,1,0:T(8,128)S(1)} custom-call(s32[5]{0:T(128)S(1)} %compare_select_fusion.order_ref, bf16[512,1024]{1,0:T(8,128)(2,1)S(1)} %bitcast.52, bf16[1024,4096]{1,0:T(8,128)(2,1)S(1)} %bitcast.49), custom_call_target="tpu_custom_call" | custom-call | flops 2684354560 | bytes 10485760 | tf_op jit(solution)/shard_map/shares/pallas_call | solution.py:180
  37.4 0.0 copy-start.1
  37.5 5.8 %collective-permute-done.4 = bf16[512,512]{1,0:T(8,128)(2,1)S(1)} collective-permute-done((bf16[512,512]{1,0:T(8,128)(2,1)S(1)}, bf16[512,512]{1,0:T(8,128)(2,1)S(1)}, u32[]{:S(2)}, u32[]{:S(2)}) %collective-permute-start.4) | collective-permute-done | bytes 524320 | tf_op jit(solution)/shard_map/ppermute | solution.py:293
  43.3 3.0 %collective-permute-done.2 = bf16[512,512]{1,0:T(8,128)(2,1)S(1)} collective-permute-done((bf16[512,512]{1,0:T(8,128)(2,1)S(1)}, bf16[512,512]{1,0:T(8,128)(2,1)S(1)}, u32[]{:S(2)}, u32[]{:S(2)}) %collective-permute-start.2) | collective-permute-done | bytes 524320 | tf_op jit(solution)/shard_map/ppermute | solution.py:292
  46.3 0.0 copy-done.1
  46.3 1.2 fusion.6
  47.5 0.3 collective-permute-start.5
  47.8 1.2 collective-permute-start.3
  49.0 2.9 %copy.12 = bf16[1024,1024]{0,1:T(8,128)(2,1)S(1)} copy(bf16[1024,1024]{1,0:T(8,128)(2,1)} %bitcast.56) | data formatting | bytes 4194304 | tf_op jit(solution)/shard_map/reshape | solution.py:297
  51.8 7.3 %collective-permute-done.5 = bf16[512,512]{1,0:T(8,128)(2,1)S(1)} collective-permute-done((bf16[512,512]{1,0:T(8,128)(2,1)}, bf16[512,512]{1,0:T(8,128)(2,1)S(1)}, u32[]{:S(2)}, u32[]{:S(2)}) %collective-permute-start.5) | collective-permute-done | bytes 524320 | tf_op jit(solution)/shard_map/ppermute | solution.py:293
  59.1 0.0 copy-start.3
  59.1 0.8 copy-done.3
  59.9 0.5 collective-permute-done.3
  60.4 2.2 %fusion.4 = (bf16[512,512]{1,0:T(8,128)(2,1)S(1)}, bf16[512,512]{1,0:T(8,128)(2,1)S(1)}) fusion(f32[5,512,512]{2,1,0:T(8,128)} %copy-done.1, bf16[512,512]{1,0:T(8,128)(2,1)} %copy-done.3, bf16[512,512]{1,0:T(8,128)(2,1)} %collective-permute-done.3), kind=kLoop, calls=%fused_computation.7 | loop fusion | flops 1572864 | bytes 4194304 | tf_op jit(solution)/shard_map/convert_element_type | solution.py:294
  62.6 4.9 %all-to-all-done.names_ref.x_ref = bf16[32,33,16,128]{3,2,1,0:T(8,128)(2,1)} async-done(((bf16[32,33,16,128]{3,2,1,0:T(8,128)(2,1)}), bf16[32,33,16,128]{3,2,1,0:T(8,128)(2,1)}, u32[]{:S(2)}, u32[]{:S(2)}) %all-to-all-start) | async-done | bytes 4325408 | tf_op jit(solution)/shard_map/all_to_all | solution.py:278
  67.5 6.5 %shrink.1 = bf16[32,32,128]{2,1,0:T(8,128)(2,1)S(1)} custom-call(bf16[32,33,16,128]{3,2,1,0:T(8,128)(2,1)} %all-to-all-done.names_ref.x_ref, bf16[32,33,16,128]{3,2,1,0:T(8,128)(2,1)} %all-to-all-done.names_ref.x_ref, bf16[1024,1024]{1,0:T(8,128)(2,1)S(1)} %bitcast.53), custom_call_target="tpu_custom_call" | custom-call | flops 4294967296 | bytes 6422528 | tf_op jit(solution)/shard_map/shrink/pallas_call | solution.py:102
  74.0 18.2 %all_to_all.25 = bf16[8,128,128]{2,1,0:T(8,128)(2,1)S(1)} all-to-all(bf16[8,128,128]{2,1,0:T(8,128)(2,1)S(1)} %bitcast.54), channel_id=1, replica_groups=mesh['pool'=32,'tp'=8] {'tp'}, dimensions={0} | all-to-all | bytes 524288 | tf_op jit(solution)/shard_map/all_to_all | solution.py:258
  92.3 12.5 %all_to_all.26 = bf16[8,128,128]{2,1,0:T(8,128)(2,1)} all-to-all(bf16[8,128,128]{2,1,0:T(8,128)(2,1)S(1)} %broadcast_in_dim.16), channel_id=1, replica_groups=mesh['pool'=32,'tp'=8] {'tp'}, dimensions={0} | all-to-all | bytes 524288 | tf_op jit(solution)/shard_map/all_to_all | solution.py:261
  104.7 0.0 copy-start.4
  104.7 5.8 %expand.1 = bf16[32,2,32,512]{3,2,1,0:T(8,128)(2,1)} custom-call(bf16[32,33,16,128]{3,2,1,0:T(8,128)(2,1)} %all-to-all-done.names_ref.x_ref, bf16[32,32,128]{2,1,0:T(8,128)(2,1)} %bitcast.57, bf16[1024,512]{1,0:T(8,128)(2,1)} %bitcast.61), custom_call_target="tpu_custom_call" | custom-call | flops 2147483648 | bytes 3407872 | tf_op jit(solution)/shard_map/expand/pallas_call | solution.py:149
  110.5 10.1 %all-to-all-start.3 = ((bf16[32,2,32,512]{3,2,1,0:T(8,128)(2,1)}), bf16[32,2,32,512]{3,2,1,0:T(8,128)(2,1)}, u32[]{:S(2)}, u32[]{:S(2)}) async-start(bf16[32,2,32,512]{3,2,1,0:T(8,128)(2,1)} %expand.1), calls=%async_computation.3 | async-start | bytes 4194304 | tf_op jit(solution)/shard_map/all_to_all | solution.py:301
  120.7 0.0 copy-done.4
  120.7 0.1 convert_reduce_fusion
  120.8 0.1 collective-permute-start.7
  120.9 1.5 collective-permute-start.6
  122.4 0.1 select_reduce_fusion
  122.5 1.3 fusion.spread_ref
  123.8 10.5 %collective-permute-done.7 = bf16[512,512]{1,0:T(8,128)(2,1)S(1)} collective-permute-done((bf16[512,512]{1,0:T(8,128)(2,1)S(1)}, bf16[512,512]{1,0:T(8,128)(2,1)S(1)}, u32[]{:S(2)}, u32[]{:S(2)}) %collective-permute-start.7) | collective-permute-done | bytes 524320 | tf_op jit(solution)/shard_map/ppermute | solution.py:303
  134.2 1.1 collective-permute-done.6
  135.3 2.5 %fusion.2 = f32[512,512]{1,0:T(8,128)} fusion(f32[5,512,512]{2,1,0:T(8,128)} %copy-done.1, bf16[512,512]{1,0:T(8,128)(2,1)S(1)} %collective-permute-done.7, bf16[512,512]{1,0:T(8,128)(2,1)S(1)} %collective-permute-done.6), kind=kLoop, calls=%fused_computation.4 | loop fusion | flops 1048576 | bytes 3145728 | tf_op jit(solution)/shard_map/add | solution.py:304
  137.8 11.2 %all-to-all-done.3.back_ref = bf16[32,2,32,512]{3,2,1,0:T(8,128)(2,1)} async-done(((bf16[32,2,32,512]{3,2,1,0:T(8,128)(2,1)}), bf16[32,2,32,512]{3,2,1,0:T(8,128)(2,1)}, u32[]{:S(2)}, u32[]{:S(2)}) %all-to-all-start.3) | async-done | bytes 2097184 | tf_op jit(solution)/shard_map/all_to_all | solution.py:301
  149.0 3.3 %join.1 = bf16[2,256,512]{2,1,0:T(8,128)(2,1)} custom-call(bf16[2,256,1024]{2,1,0:T(8,128)(2,1)} %fusion.spread_ref, bf16[32,2,32,512]{3,2,1,0:T(8,128)(2,1)} %all-to-all-done.3.back_ref, f32[2,256,512]{2,1,0:T(8,128)} %bitcast.55), custom_call_target="tpu_custom_call" | custom-call | flops 536870912 | bytes 4718592 | tf_op jit(solution)/shard_map/join/pallas_call | solution.py:234
  (9 shorter events, 0.1 us)
Async XLA Ops:
  4.9 8.8 %copy-start.2 = (bf16[2,256,1024]{2,1,0:T(8,128)(2,1)S(1)}, bf16[2,256,1024]{2,1,0:T(8,128)(2,1)}, u32[]{:S(2)}) copy-start(bf16[2,256,1024]{2,1,0:T(8,128)(2,1)} %tokens_ref.1) | copy-start | bytes 3145732
  4.9 62.6 %all-to-all-start = ((bf16[32,33,16,128]{3,2,1,0:T(8,128)(2,1)}), bf16[32,33,16,128]{3,2,1,0:T(8,128)(2,1)}, u32[]{:S(2)}, u32[]{:S(2)}) async-start(bf16[32,33,16,128]{3,2,1,0:T(8,128)(2,1)} %pack.1), calls=%async_computation | async-start | bytes 8650752 | tf_op jit(solution)/shard_map/all_to_all | solution.py:278
  13.7 3.4 %copy-start = (bf16[1024,4096]{1,0:T(8,128)(2,1)S(1)}, bf16[1024,4096]{1,0:T(8,128)(2,1)}, u32[]{:S(2)}) copy-start(bf16[1024,4096]{1,0:T(8,128)(2,1)} %weight_ref.5) | copy-start | bytes 25165828
  17.1 6.6 %copy-start.6 = (s32[2]{0:T(128)S(1)}, s32[2]{0:T(128)}, u32[]{:S(2)}) copy-start(s32[2]{0:T(128)} %constant.34.clone) | copy-start | bytes 28
  17.9 14.9 %slice-start = ((s8[8388608]{0:T(1024)(128)(4,1)}), s8[4194304]{0:T(1024)(128)(4,1)S(1)}, s32[]{:S(2)}) async-start(s8[8388608]{0:T(1024)(128)(4,1)} %bitcast.48), calls=%async_computation.4 | async-start | bytes 8388608
  18.0 12.2 %collective-permute-start = (bf16[256,512]{1,0:T(8,128)(2,1)S(1)}, bf16[256,512]{1,0:T(8,128)(2,1)S(1)}, u32[]{:S(2)}, u32[]{:S(2)}) collective-permute-start(bf16[256,512]{1,0:T(8,128)(2,1)S(1)} %get-tuple-element.36), channel_id=1, source_target_pairs={{0,1},{1,2},{2,3},{3,4},{4,5},{5,6},{6,7},{7,0},{8,9},{9,10},{10,1... | collective-permute-start | bytes 786440 | tf_op jit(solution)/shard_map/ppermute | solution.py:283
  19.7 10.5 %collective-permute-start.1 = (bf16[256,512]{1,0:T(8,128)(2,1)S(1)}, bf16[256,512]{1,0:T(8,128)(2,1)S(1)}, u32[]{:S(2)}, u32[]{:S(2)}) collective-permute-start(bf16[256,512]{1,0:T(8,128)(2,1)S(1)} %get-tuple-element.35), channel_id=1, source_target_pairs={{0,7},{1,0},{2,1},{3,2},{4,3},{5,4},{6,5},{7,6},{8,15},{9,8},{10,9... | collective-permute-start | bytes 786440 | tf_op jit(solution)/shard_map/ppermute | solution.py:284
  23.7 9.1 %copy-start.5 = (s32[5]{0:T(128)S(1)}, s32[5]{0:T(128)}, u32[]{:S(2)}) copy-start(s32[5]{0:T(128)} %constant.35.clone) | copy-start | bytes 64
  23.7 9.1 %slice-start.1 = ((s8[8388608]{0:T(1024)(128)(4,1)}), s8[4194304]{0:T(1024)(128)(4,1)S(1)}, s32[]{:S(2)}) async-start(s8[8388608]{0:T(1024)(128)(4,1)} %bitcast.48), calls=%async_computation.5 | async-start | bytes 8388608
  30.3 12.9 %collective-permute-start.4 = (bf16[512,512]{1,0:T(8,128)(2,1)S(1)}, bf16[512,512]{1,0:T(8,128)(2,1)S(1)}, u32[]{:S(2)}, u32[]{:S(2)}) collective-permute-start(bf16[512,512]{1,0:T(8,128)(2,1)S(1)} %get-tuple-element.24), channel_id=1, source_target_pairs={{0,7},{1,0},{2,1},{3,2},{4,3},{5,4},{6,5},{7,6},{8,15},{9,8},{10,9... | collective-permute-start | bytes 1572872 | tf_op jit(solution)/shard_map/ppermute | solution.py:293
  32.8 13.4 %collective-permute-start.2 = (bf16[512,512]{1,0:T(8,128)(2,1)S(1)}, bf16[512,512]{1,0:T(8,128)(2,1)S(1)}, u32[]{:S(2)}, u32[]{:S(2)}) collective-permute-start(bf16[512,512]{1,0:T(8,128)(2,1)S(1)} %get-tuple-element.22), channel_id=1, source_target_pairs={{0,1},{1,2},{2,3},{3,4},{4,5},{5,6},{6,7},{7,0},{8,9},{9,10},{10,1... | collective-permute-start | bytes 1572872 | tf_op jit(solution)/shard_map/ppermute | solution.py:292
  37.4 8.8 %copy-start.1 = (f32[5,512,512]{2,1,0:T(8,128)}, f32[5,512,512]{2,1,0:T(8,128)S(1)}, u32[]{:S(2)}) copy-start(f32[5,512,512]{2,1,0:T(8,128)S(1)} %shares.5) | copy-start | bytes 15728644
  47.5 11.6 %collective-permute-start.5 = (bf16[512,512]{1,0:T(8,128)(2,1)}, bf16[512,512]{1,0:T(8,128)(2,1)S(1)}, u32[]{:S(2)}, u32[]{:S(2)}) collective-permute-start(bf16[512,512]{1,0:T(8,128)(2,1)} %get-tuple-element.33), channel_id=1, source_target_pairs={{0,7},{1,0},{2,1},{3,2},{4,3},{5,4},{6,5},{7,6},{8,15},{9,8},{10,9... | collective-permute-start | bytes 1572872 | tf_op jit(solution)/shard_map/ppermute | solution.py:293
  47.8 12.6 %collective-permute-start.3 = (bf16[512,512]{1,0:T(8,128)(2,1)S(1)}, bf16[512,512]{1,0:T(8,128)(2,1)}, u32[]{:S(2)}, u32[]{:S(2)}) collective-permute-start(bf16[512,512]{1,0:T(8,128)(2,1)S(1)} %get-tuple-element.34), channel_id=1, source_target_pairs={{0,1},{1,2},{2,3},{3,4},{4,5},{5,6},{6,7},{7,0},{8,9},{9,10},{10,1... | collective-permute-start | bytes 1572872 | tf_op jit(solution)/shard_map/ppermute | solution.py:292
  59.1 0.8 copy-start.3
  104.7 16.0 %copy-start.4 = (s32[2,1,256]{2,1,0:T(1,128)S(1)}, s32[2,1,256]{2,1,0:T(1,128)}, u32[]{:S(2)}) copy-start(s32[2,1,256]{2,1,0:T(1,128)} %slots_ref.1) | copy-start | bytes 6148
  110.5 38.5 %all-to-all-start.3 = ((bf16[32,2,32,512]{3,2,1,0:T(8,128)(2,1)}), bf16[32,2,32,512]{3,2,1,0:T(8,128)(2,1)}, u32[]{:S(2)}, u32[]{:S(2)}) async-start(bf16[32,2,32,512]{3,2,1,0:T(8,128)(2,1)} %expand.1), calls=%async_computation.3 | async-start | bytes 4194304 | tf_op jit(solution)/shard_map/all_to_all | solution.py:301
  120.8 13.4 %collective-permute-start.7 = (bf16[512,512]{1,0:T(8,128)(2,1)S(1)}, bf16[512,512]{1,0:T(8,128)(2,1)S(1)}, u32[]{:S(2)}, u32[]{:S(2)}) collective-permute-start(bf16[512,512]{1,0:T(8,128)(2,1)S(1)} %get-tuple-element.30), channel_id=1, source_target_pairs={{0,7},{1,0},{2,1},{3,2},{4,3},{5,4},{6,5},{7,6},{8,15},{9,8},{10,9... | collective-permute-start | bytes 1572872 | tf_op jit(solution)/shard_map/ppermute | solution.py:303
  120.9 14.4 %collective-permute-start.6 = (bf16[512,512]{1,0:T(8,128)(2,1)S(1)}, bf16[512,512]{1,0:T(8,128)(2,1)S(1)}, u32[]{:S(2)}, u32[]{:S(2)}) collective-permute-start(bf16[512,512]{1,0:T(8,128)(2,1)S(1)} %get-tuple-element.29), channel_id=1, source_target_pairs={{0,1},{1,2},{2,3},{3,4},{4,5},{5,6},{6,7},{7,0},{8,9},{9,10},{10,1... | collective-permute-start | bytes 1572872 | tf_op jit(solution)/shard_map/ppermute | solution.py:302

commit v4 on v3

v4 whole, which is shorter than its diff:
```python
import functools

import jax
import jax.numpy as jnp
from jax import lax
from jax.experimental import pallas as pl
from jax.experimental.pallas import tpu as pltpu
from jax.sharding import PartitionSpec as P

BF16 = jnp.bfloat16
F32 = jnp.float32
LANES = 128
TILE = 16
VMEM = 18 << 20
FULL = 62 << 20


def pack_kernel(step, asked_ref, slots_ref, tokens_ref, out_ref):
    rows, width = tokens_ref.shape[1:]
    block = out_ref.shape[0]
    across = width // LANES
    most = out_ref.shape[1] // across * TILE
    first = pl.program_id(0) * block
    shape = (block, most, rows)
    slot = lax.broadcasted_iota(jnp.int32, shape, 0) + first
    ahead = lax.broadcasted_iota(jnp.int32, shape, 1)
    position = lax.broadcasted_iota(jnp.int32, shape, 2)
    held = jnp.broadcast_to(slots_ref[0].reshape(1, 1, rows), shape)
    before = jnp.where(held < slot, 1.0, 0.0)
    start = jnp.minimum(jnp.sum(before, axis=2, keepdims=True).astype(jnp.int32), rows - most)
    pick = jnp.where(position == start + ahead, 1.0, 0.0).astype(BF16)
    value = jnp.dot(pick.reshape(block * most, rows), tokens_ref[0], preferred_element_type=F32)
    value = value.astype(BF16).reshape(block, most // TILE, TILE, width)
    for down in range(most // TILE):
        for c in range(across):
            out_ref[:, down * across + c] = value[:, down, :, c * LANES : (c + 1) * LANES]
    if step == 0:
        line = lax.broadcasted_iota(jnp.int32, (TILE, LANES), 0)
        for s in range(block):
            names = jnp.where(line < TILE // 2, asked_ref[0, first + s], asked_ref[1, first + s])
            out_ref[s, most // TILE * across] = names.astype(F32).astype(BF16)


def pack(step, asked, slots, tokens, most, block=16):
    _, rows, width = tokens.shape
    count = asked.shape[1]
    tiles = (most // TILE) * (width // LANES) + (1 if step == 0 else 0)
    return pl.pallas_call(
        functools.partial(pack_kernel, step),
        out_shape=jax.ShapeDtypeStruct((count, tiles, TILE, LANES), BF16),
        grid_spec=pltpu.PrefetchScalarGridSpec(
            num_scalar_prefetch=1,
            grid=(count // block,),
            in_specs=[
                pl.BlockSpec((1, 1, rows), lambda i, asked: (step, 0, 0)),
                pl.BlockSpec((1, rows, width), lambda i, asked: (step, 0, 0)),
            ],
            out_specs=pl.BlockSpec((block, tiles, TILE, LANES), lambda i, asked: (i, 0, 0, 0)),
        ),
        compiler_params=pltpu.CompilerParams(vmem_limit_bytes=FULL if step == 0 else VMEM),
        cost_estimate=pl.CostEstimate(
            flops=2 * count * most * rows * width,
            bytes_accessed=2 * (rows * width + count * tiles * TILE * LANES),
            transcendentals=0,
        ),
        name="pack",
    )(asked, slots, tokens)


def named(names_ref, step, half, block, most):
    line = step * (TILE // 2)
    return jnp.broadcast_to(
        names_ref[half, :, 0].astype(F32)[:, line : line + 1, :], (block, most, LANES)
    )


def shrink_kernel(step, rank, names_ref, x_ref, down_ref, out_ref, rows_ref, acc_ref):
    halves, block, most, held = acc_ref.shape
    width = rows_ref.shape[-1]
    across = width // LANES
    for d in range(rows_ref.shape[2]):
        for c in range(across):
            rows_ref[:, :, d, :, c * LANES : (c + 1) * LANES] = x_ref[:, :, d * across + c]
    acc = lax.dot_general(
        rows_ref[...].reshape(halves * block * most, width),
        down_ref[...],
        (((1,), (1,)), ((), ())),
        preferred_element_type=F32,
    )
    acc_ref[...] = acc.reshape(acc_ref.shape)
    lane = lax.broadcasted_iota(jnp.int32, (block * most, LANES), 1)
    parts = []
    for h in range(halves):
        wanted = named(names_ref, step, h, block, most)
        value = jnp.zeros((block, most, LANES), F32)
        odd = jnp.zeros((block, most, LANES), F32)
        for c in range(held // LANES):
            here = acc_ref[h, :, :, c * LANES : (c + 1) * LANES]
            value = jnp.where((wanted == 2.0 * c) | (wanted == 2.0 * c + 1.0), here, value)
            odd = jnp.where(wanted == 2.0 * c + 1.0, 1.0, odd)
        value = value.reshape(block * most, LANES)
        odd = odd.reshape(block * most, LANES)
        parts.append(jnp.where(odd == 1.0 * h, value, pltpu.roll(value, rank, 1)))
    out = jnp.where(lane < rank, parts[0], parts[1])
    out_ref[...] = out.astype(BF16).reshape(out_ref.shape)


def shrink_rows(step, names, x, down, most, rank, block=8):
    half = x.shape[0] // 2
    held, width = down.shape
    tiles = (most // TILE) * (width // LANES)
    names = names.reshape((2, half) + names.shape[1:])
    x = x.reshape((2, half) + x.shape[1:])
    return pl.pallas_call(
        functools.partial(shrink_kernel, step, rank),
        out_shape=jax.ShapeDtypeStruct((half, most, LANES), BF16),
        grid=(half // block,),
        in_specs=[
            pl.BlockSpec((2, block, 1, TILE, LANES), lambda i: (0, i, tiles, 0, 0)),
            pl.BlockSpec((2, block, tiles, TILE, LANES), lambda i: (0, i, 0, 0, 0)),
            pl.BlockSpec((held, width), lambda i: (0, 0)),
        ],
        out_specs=pl.BlockSpec((block, most, LANES), lambda i: (i, 0, 0)),
        scratch_shapes=[
            pltpu.VMEM((2, block, most // TILE, TILE, width), BF16),
            pltpu.VMEM((2, block, most, held), F32),
        ],
        compiler_params=pltpu.CompilerParams(vmem_limit_bytes=VMEM),
        cost_estimate=pl.CostEstimate(
            flops=4 * half * most * width * held,
            bytes_accessed=2 * (x.size + down.size),
            transcendentals=0,
        ),
        name="shrink",
    )(names, x, down)


def expand_kernel(step, rank, names_ref, a_ref, b_ref, c_ref, d_ref, e_ref, up_ref, out_ref, wide_ref):
    halves, block, most, held = wide_ref.shape
    both = a_ref[...].astype(F32)
    for ref in (b_ref, c_ref, d_ref, e_ref):
        both = both + ref[...].astype(F32)
    swapped = pltpu.roll(both.reshape(block * most, LANES), rank, 1).reshape(block, most, LANES)
    high = jnp.where(lax.broadcasted_iota(jnp.int32, (block, most, LANES), 2) < rank, 0.0, 1.0)
    for h in range(halves):
        wanted = named(names_ref, step, h, block, most)
        chosen = jnp.where(high == 1.0 * h, both, swapped)
        for c in range(held // LANES):
            value = jnp.where(wanted == 2.0 * c + high, chosen, 0.0)
            wide_ref[h, :, :, c * LANES : (c + 1) * LANES] = value.astype(BF16)
    wide = wide_ref[...].reshape(halves * block * most, held)
    out = jnp.dot(wide, up_ref[...], preferred_element_type=F32)
    out_ref[...] = out.astype(BF16).reshape(out_ref.shape)


def expand_rows(step, names, parts, up, rank, block=8):
    half, most, _ = parts[0].shape
    tiles = names.shape[1] - 1
    held, features = up.shape
    names = names.reshape((2, half) + names.shape[1:])
    delta = pl.pallas_call(
        functools.partial(expand_kernel, step, rank),
        out_shape=pltpu.HBM((2, half, most, features), BF16),
        grid=(half // block,),
        in_specs=[pl.BlockSpec((2, block, 1, TILE, LANES), lambda i: (0, i, tiles, 0, 0))]
        + [pl.BlockSpec((block, most, LANES), lambda i: (i, 0, 0))] * len(parts)
        + [pl.BlockSpec((held, features), lambda i: (0, 0))],
        out_specs=pl.BlockSpec((2, block, most, features), lambda i: (0, i, 0, 0)),
        scratch_shapes=[pltpu.VMEM((2, block, most, held), BF16)],
        compiler_params=pltpu.CompilerParams(vmem_limit_bytes=VMEM),
        cost_estimate=pl.CostEstimate(
            flops=4 * half * most * held * features,
            bytes_accessed=2 * (5 * half * most * LANES + up.size + 2 * half * most * features),
            transcendentals=0,
        ),
        name="expand",
    )(names, *parts, up)
    return delta.reshape(2 * half, most, features)


def shares_kernel(order_ref, tokens_ref, weight_ref, out_ref):
    out_ref[0] = jnp.dot(tokens_ref[...], weight_ref[...], preferred_element_type=F32)


def base_shares(flat_tokens, query_weight, distances):
    size = lax.axis_size("tp")
    rows, width = flat_tokens.shape
    columns = query_weight.shape[1] // size
    order = lax.rem(lax.axis_index("tp") + jnp.array(distances, jnp.int32), size)
    amount = len(distances)
    return pl.pallas_call(
        shares_kernel,
        out_shape=jax.ShapeDtypeStruct((amount, rows, columns), F32),
        grid_spec=pltpu.PrefetchScalarGridSpec(
            num_scalar_prefetch=1,
            grid=(amount,),
            in_specs=[
                pl.BlockSpec((rows, width), lambda k, order: (0, 0)),
                pl.BlockSpec((width, columns), lambda k, order: (0, order[k])),
            ],
            out_specs=pl.BlockSpec((1, rows, columns), lambda k, order: (k, 0, 0)),
        ),
        compiler_params=pltpu.CompilerParams(vmem_limit_bytes=VMEM),
        cost_estimate=pl.CostEstimate(
            flops=2 * rows * width * columns * amount,
            bytes_accessed=2 * width * columns * amount + 4 * rows * columns * amount,
            transcendentals=0,
        ),
        name="shares",
    )(order, flat_tokens, query_weight)


def first_sums_kernel(shares_ref, top_ref, low_ref, right_ref, left_ref):
    middle = top_ref.shape[0]
    right_ref[:middle] = (shares_ref[0, :middle] + top_ref[...].astype(F32)).astype(BF16)
    right_ref[middle:] = shares_ref[0, middle:].astype(BF16)
    left_ref[:middle] = shares_ref[1, :middle].astype(BF16)
    left_ref[middle:] = (shares_ref[1, middle:] + low_ref[...].astype(F32)).astype(BF16)


def first_sums(shares, top, low):
    _, rows, columns = shares.shape
    out = jax.ShapeDtypeStruct((rows, columns), BF16)
    return pl.pallas_call(
        first_sums_kernel,
        out_shape=(out, out),
        compiler_params=pltpu.CompilerParams(vmem_limit_bytes=VMEM),
        cost_estimate=pl.CostEstimate(
            flops=2 * rows * columns, bytes_accessed=14 * rows * columns, transcendentals=0
        ),
        name="first_sums",
    )(shares, top, low)


def join_kernel(spread_ref, back_ref, base_ref, earlier_ref, out_ref):
    groups, most, features = back_ref.shape
    back = back_ref[...].reshape(groups * most, features)
    delta = jnp.dot(spread_ref[...], back, preferred_element_type=F32)
    out_ref[0] = (base_ref[...] + delta).astype(BF16)


def join(step, spread, back, base, earlier):
    rows, places = spread.shape
    groups, most, features = back.shape
    return pl.pallas_call(
        join_kernel,
        out_shape=jax.ShapeDtypeStruct(earlier.shape, BF16),
        grid=(1,),
        in_specs=[
            pl.BlockSpec((rows, places), lambda i: (0, 0)),
            pl.BlockSpec((groups, most, features), lambda i: (0, 0, 0)),
            pl.BlockSpec((rows, features), lambda i: (0, 0)),
            pl.BlockSpec(memory_space=pl.ANY),
        ],
        out_specs=pl.BlockSpec((1, rows, features), lambda i: (step, 0, 0)),
        input_output_aliases={3: 0},
        compiler_params=pltpu.CompilerParams(vmem_limit_bytes=VMEM),
        cost_estimate=pl.CostEstimate(
            flops=2 * rows * places * features,
            bytes_accessed=2 * (spread.size + back.size) + 6 * base.size,
            transcendentals=0,
        ),
        name="join",
    )(spread, back, base, earlier)


def parts_over_tp(value):
    size = lax.axis_size("tp")
    assert size == 8

    def fetch(value, ahead):
        return lax.ppermute(value, "tp", [((i + ahead) % size, i) for i in range(size)])

    after, before = fetch(value, 1), fetch(value, -1)
    two = value.astype(F32) + after.astype(F32)
    three = two + before.astype(F32)
    return value, after, before, fetch(three.astype(BF16), 3), fetch(two.astype(BF16), -3)


def body(tokens, query_weight, down_weight, up_weight, requests, row_slot_index):
    count = lax.axis_size("pool")
    size = lax.axis_size("tp")
    steps, rows, width = tokens.shape
    most = 4 * rows // count
    adapters, rank, _ = down_weight.shape
    features = up_weight.shape[-1]
    middle = steps * rows // 2
    right = [(i, (i + 1) % size) for i in range(size)]
    left = [(i, (i - 1) % size) for i in range(size)]

    def swap(value):
        return lax.all_to_all(value, "pool", split_axis=0, concat_axis=0, tiled=True)

    asked = requests[:, 0, :]
    sent = pack(0, asked, row_slot_index, tokens, most)
    sent, late_tokens, late_slots = lax.optimization_barrier((sent, tokens, row_slot_index))
    x = [swap(sent)]
    sent = pack(1, asked, late_slots, late_tokens, most)

    late_tokens = late_tokens.reshape(steps * rows, width)
    far = size // 2
    far_weight = pltpu.with_memory_space_constraint(query_weight, pltpu.HBM)
    farthest = base_shares(late_tokens, far_weight, [far])[0].astype(BF16)
    top = lax.ppermute(farthest[:middle], "tp", right)
    low = lax.ppermute(farthest[middle:], "tp", left)
    late_tokens, _ = lax.optimization_barrier((late_tokens, farthest))
    near = [d for ahead in range(far - 2, 0, -1) for d in (ahead, size - ahead)] + [0]
    first = base_shares(late_tokens, query_weight, [far - 1, far + 1])
    late_tokens, first = lax.optimization_barrier((late_tokens, first))
    going_right, going_left = first_sums(first, top, low)
    late_tokens, _ = lax.optimization_barrier((late_tokens, going_right))
    shares = base_shares(late_tokens, query_weight, near)
    for hop in range(far - 2):
        going_right = lax.ppermute(going_right, "tp", right).astype(F32) + shares[2 * hop]
        going_left = lax.ppermute(going_left, "tp", left).astype(F32) + shares[2 * hop + 1]
        going_right, going_left = going_right.astype(BF16), going_left.astype(BF16)
        if hop == 0:
            sent, going_right, going_left = lax.optimization_barrier((sent, going_right, going_left))
            x.append(swap(sent))

    down = down_weight.reshape(adapters * rank, width)
    down = pltpu.with_memory_space_constraint(down, pltpu.HBM)
    up = up_weight.reshape(adapters * rank, features)
    names = x[0]
    back = []
    for t in range(steps):
        parts = parts_over_tp(shrink_rows(t, names, x[t], down, most, rank))
        delta = expand_rows(t, names, parts, up, rank)
        if t == steps - 1:
            delta, going_right, going_left = lax.optimization_barrier((delta, going_right, going_left))
        back.append(swap(delta))
    from_left = lax.ppermute(going_right, "tp", right).astype(F32)
    from_right = lax.ppermute(going_left, "tp", left).astype(F32)
    base = (shares[-1] + from_left + from_right).reshape(steps, rows, features)

    slots = late_slots[:, 0, :]
    before = slots[:, None, :] < jnp.arange(count, dtype=jnp.int32)[None, :, None]
    start = jnp.minimum(jnp.sum(before.astype(jnp.int32), axis=2), rows - most)
    mine = slots[:, :, None] == jnp.arange(count, dtype=jnp.int32)[None, None, :]
    own_start = jnp.sum(jnp.where(mine, start[:, None, :], 0), axis=2)
    place = slots * most + jnp.arange(rows, dtype=jnp.int32)[None, :] - own_start
    spread = (place[:, :, None] == jnp.arange(count * most, dtype=jnp.int32)[None, None, :]).astype(BF16)
    out = jnp.zeros((steps, rows, features), BF16)
    for t in range(steps):
        out = join(t, spread[t], back[t], base[t], out)
    return out


def solution(mesh):
    placed = (
        P(None, "pool", "tp"),
        P("tp", None),
        P("pool", None, "tp"),
        P("pool", None, "tp"),
        P(None, "pool", None),
        P(None, "pool", None),
    )
    return jax.shard_map(
        body, mesh=mesh, in_specs=placed, out_specs=P(None, "pool", "tp"), check_vma=False
    )
```

time: 153 us -> 149 us (0.974)
  starting transfers between devices: 30.2 us -> 62.5 us
  blocking collectives: 30.6 us -> 0 us
  waiting for transfers between devices: 48.6 us -> 40.6 us
  Pallas kernels: 28.1 us -> 32.4 us
    all_to_all x2 -> x0, blocking collectives: 30.6 us -> none  [the longest x1 18.2 us: sum_over_tp(): got = lax.all_to_all(flat, 'tp', split_axis=0, concat_axis=0, tiled=True)]
    ppermute x0 -> x8, waiting for transfers between devices: none -> 24.2 us  [fetch(): lax.ppermute(value, 'tp', [((i + ahead) % size, i) for i in range(size)])]
    all_to_all x2 -> x4, starting transfers between devices: 18.9 us -> 37.6 us  [swap(): lax.all_to_all(value, 'pool', split_axis=0, concat_axis=0, tiled=True)]
    ppermute x2, waiting for transfers between devices: 13.1 us -> 0.01 us  [body(): lax.ppermute(going_left, 'tp', left).astype(F32) + shares[2 * hop + 1]]
    ppermute x0 -> x8, starting transfers between devices: none -> 11 us  [fetch(): lax.ppermute(value, 'tp', [((i + ahead) % size, i) for i in range(size)])]
    ppermute x1, waiting for transfers between devices: 10.5 us -> 0.01 us  [body(): from_right = lax.ppermute(going_left, 'tp', left).astype(F32)]
    all_to_all x2 -> x4, waiting for transfers between devices: 16.2 us -> 8.5 us  [swap(): lax.all_to_all(value, 'pool', split_axis=0, concat_axis=0, tiled=True)]
    ppermute x1, waiting for transfers between devices: 4.27 us -> 0.85 us  [body(): top = lax.ppermute(farthest[:middle], 'tp', right)]
  transfers between devices with their start and end apart: 10 -> 20, of which waited for: 9 -> 11; matrix products, arithmetic and copies ran while one was open for 7% -> 5% of each run, Pallas kernels for 5% -> 19%
where the time goes in v4:
time: 149 us; the launch traced here: 148 us
  starting transfers between devices  62.5 us (42%)
  waiting for transfers between devices  40.6 us (27%)
  Pallas kernels  32.4 us (22%)
  other arithmetic  6.64 us (4%)
  local copies, waits for them, and re-layouts  5.82 us (4%)
    all_to_all x4, starting transfers between devices, swap(): lax.all_to_all(value, 'pool', split_axis=0, concat_axis=0, tiled=True)  37.6 us
    ppermute x8, waiting for transfers between devices, fetch(): lax.ppermute(value, 'tp', [((i + ahead) % size, i) for i in range(size)])  24.2 us
    ppermute x8, starting transfers between devices, fetch(): lax.ppermute(value, 'tp', [((i + ahead) % size, i) for i in range(size)])  11 us
    pallas_call x2, Pallas kernels, shrink_rows(): pl.pallas_call(functools.partial(shrink_kernel, step, rank), out_shape=ja...  9.22 us
    pallas_call x3, Pallas kernels, base_shares(): pl.pallas_call(shares_kernel, out_shape=jax.ShapeDtypeStruct((amount, row...  8.8 us
    all_to_all x4, waiting for transfers between devices, swap(): lax.all_to_all(value, 'pool', split_axis=0, concat_axis=0, tiled=True)  8.5 us
    pallas_call x2, Pallas kernels, expand_rows(): pl.pallas_call(functools.partial(expand_kernel, step, rank), out_shape=pl...  5.37 us
    pallas_call x2, Pallas kernels, pack(): pl.pallas_call(functools.partial(pack_kernel, step), out_shape=jax.ShapeD...  5.29 us
  transfers between devices with their start and end apart: 20, of which 11 were waited for; matrix products, arithmetic and copies ran while one was open for 5% of the time, Pallas kernels for 19%

profile of v4, /device:TPU:1, one launch (start us, length us, event | category | flops | bytes accessed | tf_op | source)
XLA Modules:
  0.0 148.2 jit_solution(12865622336473352592)
XLA Ops:
  0.0 3.7 %pack.2 = bf16[32,17,16,128]{3,2,1,0:T(8,128)(2,1)} custom-call(s32[2,32]{1,0:T(2,128)} %bitcast.64, s32[2,1,256]{2,1,0:T(1,128)} %slots_ref.2, bf16[2,256,1024]{2,1,0:T(8,128)(2,1)} %tokens_ref.2), custom_call_target="tpu_custom_call" | custom-call | flops 536870912 | bytes 2752512 | tf_op jit(solution)/shard_map/pack/pallas_call | solution.py:48
  3.7 8.7 %all-to-all-start = ((bf16[32,17,16,128]{3,2,1,0:T(8,128)(2,1)}), bf16[32,17,16,128]{3,2,1,0:T(8,128)(2,1)S(1)}, u32[]{:S(2)}, u32[]{:S(2)}) async-start(bf16[32,17,16,128]{3,2,1,0:T(8,128)(2,1)} %pack.2), calls=%async_computation | async-start | bytes 4456448 | tf_op jit(solution)/shard_map/all_to_all | solution.py:292
  12.5 0.0 slice-start
  12.5 2.1 %shares.4 = f32[1,512,512]{2,1,0:T(8,128)S(1)} custom-call(s32[1]{0:T(128)S(6)} %rem.55.order_ref, bf16[512,1024]{1,0:T(8,128)(2,1)S(1)} %bitcast.54, bf16[1024,4096]{1,0:T(8,128)(2,1)} %weight_ref.5), custom_call_target="tpu_custom_call" | custom-call | flops 536870912 | bytes 2097152 | tf_op jit(solution)/shard_map/shares/pallas_call | solution.py:191
  14.6 0.0 copy-start.8
  14.6 0.1 convert_element_type.72
  14.7 1.7 %collective-permute-start = (bf16[256,512]{1,0:T(8,128)(2,1)S(1)}, bf16[256,512]{1,0:T(8,128)(2,1)S(1)}, u32[]{:S(2)}, u32[]{:S(2)}) collective-permute-start(bf16[256,512]{1,0:T(8,128)(2,1)S(1)} %get-tuple-element.42), channel_id=1, source_target_pairs={{0,1},{1,2},{2,3},{3,4},{4,5},{5,6},{6,7},{7,0},{8,9},{9,10},{10,1... | collective-permute-start | bytes 786440 | tf_op jit(solution)/shard_map/ppermute | solution.py:304
  16.4 4.0 %collective-permute-start.1 = (bf16[256,512]{1,0:T(8,128)(2,1)S(1)}, bf16[256,512]{1,0:T(8,128)(2,1)S(1)}, u32[]{:S(2)}, u32[]{:S(2)}) collective-permute-start(bf16[256,512]{1,0:T(8,128)(2,1)S(1)} %get-tuple-element.41), channel_id=1, source_target_pairs={{0,7},{1,0},{2,1},{3,2},{4,3},{5,4},{6,5},{7,6},{8,15},{9,8},{10,9... | collective-permute-start | bytes 786440 | tf_op jit(solution)/shard_map/ppermute | solution.py:305
  20.5 3.4 %copy-done = bf16[1024,4096]{1,0:T(8,128)(2,1)S(1)} copy-done((bf16[1024,4096]{1,0:T(8,128)(2,1)S(1)}, bf16[1024,4096]{1,0:T(8,128)(2,1)}, u32[]{:S(2)}) %copy-start) | copy-done | bytes 8388632
  23.8 2.2 %shares.3.shares_ref = f32[2,512,512]{2,1,0:T(8,128)S(1)} custom-call(s32[2]{0:T(128)S(1)} %compare_select_fusion.2.order_ref, bf16[512,1024]{1,0:T(8,128)(2,1)S(1)} %bitcast.55, bf16[1024,4096]{1,0:T(8,128)(2,1)S(1)} %copy-done), custom_call_target="tpu_custom_call" | custom-call | flops 1073741824 | bytes 4194304 | tf_op jit(solution)/shard_map/shares/pallas_call | solution.py:191
  26.0 0.0 copy-start.5
  26.0 0.0 copy-start.6
  26.0 0.8 collective-permute-done.top_ref
  26.9 0.0 collective-permute-done.1.low_ref
  26.9 0.2 first_sums.1
  27.1 0.0 copy-start.7
  27.1 0.1 collective-permute-start.2
  27.2 2.7 %collective-permute-start.3 = (bf16[512,512]{1,0:T(8,128)(2,1)S(1)}, bf16[512,512]{1,0:T(8,128)(2,1)S(1)}, u32[]{:S(2)}, u32[]{:S(2)}) collective-permute-start(bf16[512,512]{1,0:T(8,128)(2,1)S(1)} %get-tuple-element.26), channel_id=1, source_target_pairs={{0,7},{1,0},{2,1},{3,2},{4,3},{5,4},{6,5},{7,6},{8,15},{9,8},{10,9... | collective-permute-start | bytes 1572872 | tf_op jit(solution)/shard_map/ppermute | solution.py:315
  29.9 1.6 %pack.3 = bf16[32,16,16,128]{3,2,1,0:T(8,128)(2,1)S(1)} custom-call(s32[2,32]{1,0:T(2,128)S(1)} %bitcast.65, s32[2,1,256]{2,1,0:T(1,128)S(1)} %copy-done.5, bf16[2,256,1024]{2,1,0:T(8,128)(2,1)S(1)} %copy-done.1), custom_call_target="tpu_custom_call" | custom-call | flops 536870912 | bytes 2621440 | tf_op jit(solution)/shard_map/pack/pallas_call | solution.py:48
  31.4 1.4 copy-done.3
  32.8 4.6 %shares.5 = f32[5,512,512]{2,1,0:T(8,128)S(1)} custom-call(s32[5]{0:T(128)S(1)} %compare_select_fusion.order_ref, bf16[512,1024]{1,0:T(8,128)(2,1)S(1)} %bitcast.56, bf16[1024,4096]{1,0:T(8,128)(2,1)S(1)} %bitcast.53), custom_call_target="tpu_custom_call" | custom-call | flops 2684354560 | bytes 10485760 | tf_op jit(solution)/shard_map/shares/pallas_call | solution.py:191
  37.4 3.7 %collective-permute-done.2 = bf16[512,512]{1,0:T(8,128)(2,1)S(1)} collective-permute-done((bf16[512,512]{1,0:T(8,128)(2,1)S(1)}, bf16[512,512]{1,0:T(8,128)(2,1)S(1)}, u32[]{:S(2)}, u32[]{:S(2)}) %collective-permute-start.2) | collective-permute-done | bytes 524320 | tf_op jit(solution)/shard_map/ppermute | solution.py:314
  41.1 0.0 collective-permute-done.3
  41.1 1.4 fusion.8
  42.5 0.0 all-to-all-done
  42.5 8.5 %all-to-all-start.1 = ((bf16[32,16,16,128]{3,2,1,0:T(8,128)(2,1)}), bf16[32,16,16,128]{3,2,1,0:T(8,128)(2,1)}, u32[]{:S(2)}, u32[]{:S(2)}) async-start(bf16[32,16,16,128]{3,2,1,0:T(8,128)(2,1)} %copy-done.3), calls=%async_computation.1 | async-start | bytes 4194304 | tf_op jit(solution)/shard_map/all_to_all | solution.py:292
  51.1 0.0 copy-start.4
  51.1 4.5 %shrink.3.a_ref = bf16[16,32,128]{2,1,0:T(8,128)(2,1)S(1)} custom-call(bf16[2,16,17,16,128]{4,3,2,1,0:T(8,128)(2,1)S(1)} %bitcast.57, bf16[2,16,17,16,128]{4,3,2,1,0:T(8,128)(2,1)S(1)} %bitcast.58, bf16[1024,1024]{1,0:T(8,128)(2,1)} %bitcast.70), custom_call_target="tpu_custom_call" | custom-call | flops 2147483648 | bytes 4325376 | tf_op jit(solution)/shard_map/shrink/pallas_call | solution.py:114
  55.6 2.7 %collective-permute-start.12 = (bf16[16,32,128]{2,1,0:T(8,128)(2,1)S(1)}, bf16[16,32,128]{2,1,0:T(8,128)(2,1)S(1)}, u32[]{:S(2)}, u32[]{:S(2)}) collective-permute-start(bf16[16,32,128]{2,1,0:T(8,128)(2,1)S(1)} %shrink.3.a_ref), channel_id=1, source_target_pairs={{1,0},{2,1},{3,2},{4,3},{5,4},{6,5},{7,6},{0,7},{9,8},{10,9},{11,1... | collective-permute-start | bytes 393224 | tf_op jit(solution)/shard_map/ppermute | solution.py:272
  58.4 2.6 %collective-permute-done.12.b_ref = bf16[16,32,128]{2,1,0:T(8,128)(2,1)S(1)} collective-permute-done((bf16[16,32,128]{2,1,0:T(8,128)(2,1)S(1)}, bf16[16,32,128]{2,1,0:T(8,128)(2,1)S(1)}, u32[]{:S(2)}, u32[]{:S(2)}) %collective-permute-start.12) | collective-permute-done | bytes 131104 | tf_op jit(solution)/shard_map/ppermute | solution.py:272
  60.9 3.2 %collective-permute-done.13.c_ref = bf16[16,32,128]{2,1,0:T(8,128)(2,1)S(1)} collective-permute-done((bf16[16,32,128]{2,1,0:T(8,128)(2,1)S(1)}, bf16[16,32,128]{2,1,0:T(8,128)(2,1)S(1)}, u32[]{:S(2)}, u32[]{:S(2)}) %collective-permute-start.13) | collective-permute-done | bytes 131104 | tf_op jit(solution)/shard_map/ppermute | solution.py:272
  64.1 0.1 fusion.12
  64.2 1.7 %collective-permute-start.14 = (bf16[16,32,128]{2,1,0:T(8,128)(2,1)S(1)}, bf16[16,32,128]{2,1,0:T(8,128)(2,1)S(1)}, u32[]{:S(2)}, u32[]{:S(2)}) collective-permute-start(bf16[16,32,128]{2,1,0:T(8,128)(2,1)S(1)} %get-tuple-element.44), channel_id=1, source_target_pairs={{3,0},{4,1},{5,2},{6,3},{7,4},{0,5},{1,6},{2,7},{11,8},{12,9},{13,... | collective-permute-start | bytes 393224 | tf_op jit(solution)/shard_map/ppermute | solution.py:272
  65.9 1.6 %collective-permute-start.15 = (bf16[16,32,128]{2,1,0:T(8,128)(2,1)S(1)}, bf16[16,32,128]{2,1,0:T(8,128)(2,1)S(1)}, u32[]{:S(2)}, u32[]{:S(2)}) collective-permute-start(bf16[16,32,128]{2,1,0:T(8,128)(2,1)S(1)} %get-tuple-element.43), channel_id=1, source_target_pairs={{5,0},{6,1},{7,2},{0,3},{1,4},{2,5},{3,6},{4,7},{13,8},{14,9},{15,... | collective-permute-start | bytes 393224 | tf_op jit(solution)/shard_map/ppermute | solution.py:272
  67.5 0.1 convert_reduce_fusion
  67.7 0.9 collective-permute-start.8
  68.5 1.9 %collective-permute-start.9 = (bf16[512,512]{1,0:T(8,128)(2,1)}, bf16[512,512]{1,0:T(8,128)(2,1)}, u32[]{:S(2)}, u32[]{:S(2)}) collective-permute-start(bf16[512,512]{1,0:T(8,128)(2,1)} %get-tuple-element.29), channel_id=1, source_target_pairs={{0,7},{1,0},{2,1},{3,2},{4,3},{5,4},{6,5},{7,6},{8,15},{9,8},{10,9... | collective-permute-start | bytes 1572872 | tf_op jit(solution)/shard_map/ppermute | solution.py:315
  70.4 6.6 %collective-permute-done.14.d_ref = bf16[16,32,128]{2,1,0:T(8,128)(2,1)S(1)} collective-permute-done((bf16[16,32,128]{2,1,0:T(8,128)(2,1)S(1)}, bf16[16,32,128]{2,1,0:T(8,128)(2,1)S(1)}, u32[]{:S(2)}, u32[]{:S(2)}) %collective-permute-start.14) | collective-permute-done | bytes 131104 | tf_op jit(solution)/shard_map/ppermute | solution.py:272
  77.0 2.7 %expand.3 = bf16[2,16,32,512]{3,2,1,0:T(8,128)(2,1)} custom-call(bf16[2,16,17,16,128]{4,3,2,1,0:T(8,128)(2,1)S(1)} %bitcast.59, bf16[16,32,128]{2,1,0:T(8,128)(2,1)S(1)} %shrink.3.a_ref, bf16[16,32,128]{2,1,0:T(8,128)(2,1)S(1)} %collective-permute-done.12.b_ref, bf16[16,32,128]{2,1,0:T(8,128)(2,1)S(1)} %collective-permute-done.13.c_ref, ...), custom_call_target="tpu_custom_call" | custom-call | flops 1073741824 | bytes 2752512 | tf_op jit(solution)/shard_map/expand/pallas_call | solution.py:161
  79.7 12.3 %all-to-all-start.3 = ((bf16[32,32,512]{2,1,0:T(8,128)(2,1)}), bf16[32,32,512]{2,1,0:T(8,128)(2,1)}, u32[]{:S(2)}, u32[]{:S(2)}) async-start(bf16[32,32,512]{2,1,0:T(8,128)(2,1)} %bitcast.66), calls=%async_computation.3 | async-start | bytes 2097152 | tf_op jit(solution)/shard_map/all_to_all | solution.py:292
  92.0 4.7 %shrink.2.a_ref = bf16[16,32,128]{2,1,0:T(8,128)(2,1)S(1)} custom-call(bf16[2,16,17,16,128]{4,3,2,1,0:T(8,128)(2,1)S(1)} %bitcast.60, bf16[2,16,16,16,128]{4,3,2,1,0:T(8,128)(2,1)} %bitcast.9.x_ref, bf16[1024,1024]{1,0:T(8,128)(2,1)} %bitcast.71), custom_call_target="tpu_custom_call" | custom-call | flops 2147483648 | bytes 4194304 | tf_op jit(solution)/shard_map/shrink/pallas_call | solution.py:114
  96.7 0.1 collective-permute-start.4
  96.8 1.5 collective-permute-start.5
  98.3 0.1 select_reduce_fusion
  98.4 3.2 %collective-permute-done.4.b_ref = bf16[16,32,128]{2,1,0:T(8,128)(2,1)S(1)} collective-permute-done((bf16[16,32,128]{2,1,0:T(8,128)(2,1)S(1)}, bf16[16,32,128]{2,1,0:T(8,128)(2,1)S(1)}, u32[]{:S(2)}, u32[]{:S(2)}) %collective-permute-start.4) | collective-permute-done | bytes 131104 | tf_op jit(solution)/shard_map/ppermute | solution.py:272
  101.6 1.4 collective-permute-done.5.c_ref
  103.0 0.1 fusion.11
  103.0 0.5 collective-permute-start.6
  103.5 2.9 %collective-permute-start.7 = (bf16[16,32,128]{2,1,0:T(8,128)(2,1)S(1)}, bf16[16,32,128]{2,1,0:T(8,128)(2,1)S(1)}, u32[]{:S(2)}, u32[]{:S(2)}) collective-permute-start(bf16[16,32,128]{2,1,0:T(8,128)(2,1)S(1)} %get-tuple-element.45), channel_id=1, source_target_pairs={{5,0},{6,1},{7,2},{0,3},{1,4},{2,5},{3,6},{4,7},{13,8},{14,9},{15,... | collective-permute-start | bytes 393224 | tf_op jit(solution)/shard_map/ppermute | solution.py:272
  106.4 3.1 %fusion.4 = (bf16[512,512]{1,0:T(8,128)(2,1)}, bf16[512,512]{1,0:T(8,128)(2,1)}) fusion(f32[5,512,512]{2,1,0:T(8,128)} %copy-done.2, bf16[512,512]{1,0:T(8,128)(2,1)} %collective-permute-done.9, bf16[512,512]{1,0:T(8,128)(2,1)} %collective-permute-done.8), kind=kLoop, calls=%fused_computation.7 | loop fusion | flops 1572864 | bytes 4194304 | tf_op jit(solution)/shard_map/convert_element_type | solution.py:316
  109.5 0.9 collective-permute-done.6.d_ref
  110.4 6.4 %collective-permute-done.7.e_ref = bf16[16,32,128]{2,1,0:T(8,128)(2,1)S(1)} collective-permute-done((bf16[16,32,128]{2,1,0:T(8,128)(2,1)S(1)}, bf16[16,32,128]{2,1,0:T(8,128)(2,1)S(1)}, u32[]{:S(2)}, u32[]{:S(2)}) %collective-permute-start.7) | collective-permute-done | bytes 131104 | tf_op jit(solution)/shard_map/ppermute | solution.py:272
  116.8 2.7 %expand.2 = bf16[2,16,32,512]{3,2,1,0:T(8,128)(2,1)} custom-call(bf16[2,16,17,16,128]{4,3,2,1,0:T(8,128)(2,1)S(1)} %bitcast.61, bf16[16,32,128]{2,1,0:T(8,128)(2,1)S(1)} %shrink.2.a_ref, bf16[16,32,128]{2,1,0:T(8,128)(2,1)S(1)} %collective-permute-done.4.b_ref, bf16[16,32,128]{2,1,0:T(8,128)(2,1)S(1)} %collective-permute-done.5.c_ref, ...), custom_call_target="tpu_custom_call" | custom-call | flops 1073741824 | bytes 2752512 | tf_op jit(solution)/shard_map/expand/pallas_call | solution.py:161
  119.4 2.7 %collective-permute-start.11 = (bf16[512,512]{1,0:T(8,128)(2,1)}, bf16[512,512]{1,0:T(8,128)(2,1)S(1)}, u32[]{:S(2)}, u32[]{:S(2)}) collective-permute-start(bf16[512,512]{1,0:T(8,128)(2,1)} %get-tuple-element.32), channel_id=1, source_target_pairs={{0,7},{1,0},{2,1},{3,2},{4,3},{5,4},{6,5},{7,6},{8,15},{9,8},{10,9... | collective-permute-start | bytes 1572872 | tf_op jit(solution)/shard_map/ppermute | solution.py:333
  122.1 8.0 %all-to-all-start.2 = ((bf16[32,32,512]{2,1,0:T(8,128)(2,1)}), bf16[32,32,512]{2,1,0:T(8,128)(2,1)S(1)}, u32[]{:S(2)}, u32[]{:S(2)}) async-start(bf16[32,32,512]{2,1,0:T(8,128)(2,1)} %bitcast.67), calls=%async_computation.2 | async-start | bytes 2097152 | tf_op jit(solution)/shard_map/all_to_all | solution.py:292
  130.1 0.2 fusion
  130.4 0.1 slice_bitcast_fusion.5
  130.5 3.4 %collective-permute-done.10 = bf16[512,512]{1,0:T(8,128)(2,1)S(1)} collective-permute-done((bf16[512,512]{1,0:T(8,128)(2,1)}, bf16[512,512]{1,0:T(8,128)(2,1)S(1)}, u32[]{:S(2)}, u32[]{:S(2)}) %collective-permute-start.10) | collective-permute-done | bytes 524320 | tf_op jit(solution)/shard_map/ppermute | solution.py:332
  133.8 1.4 fusion.2
  135.3 0.1 fusion.15
  135.4 0.8 broadcast_in_dim.23.earlier_ref
  136.2 2.4 %join.2.earlier_ref = bf16[2,256,512]{2,1,0:T(8,128)(2,1)} custom-call(bf16[256,1024]{1,0:T(8,128)(2,1)S(1)} %get-tuple-element.39.spread_ref, bf16[32,32,512]{2,1,0:T(8,128)(2,1)} %all-to-all-done.3.back_ref, f32[256,512]{1,0:T(8,128)S(1)} %get-tuple-element.37.base_ref, ...), custom_call_target="tpu_custom_call", output_to_operand_aliasing={{}: (3, {})} | custom-call | flops 268435456 | bytes 2359296 | tf_op jit(solution)/shard_map/join/pallas_call | solution.py:245
  138.6 8.5 %all-to-all-done.2.back_ref = bf16[32,32,512]{2,1,0:T(8,128)(2,1)S(1)} async-done(((bf16[32,32,512]{2,1,0:T(8,128)(2,1)}), bf16[32,32,512]{2,1,0:T(8,128)(2,1)S(1)}, u32[]{:S(2)}, u32[]{:S(2)}) %all-to-all-start.2) | async-done | bytes 1048608 | tf_op jit(solution)/shard_map/all_to_all | solution.py:292
  147.1 1.2 join.3
  (29 shorter events, 0.1 us)
Async XLA Ops:
  3.7 8.7 %copy-start.1 = (bf16[2,256,1024]{2,1,0:T(8,128)(2,1)S(1)}, bf16[2,256,1024]{2,1,0:T(8,128)(2,1)}, u32[]{:S(2)}) copy-start(bf16[2,256,1024]{2,1,0:T(8,128)(2,1)} %tokens_ref.2) | copy-start | bytes 3145732
  3.7 38.8 %all-to-all-start = ((bf16[32,17,16,128]{3,2,1,0:T(8,128)(2,1)}), bf16[32,17,16,128]{3,2,1,0:T(8,128)(2,1)S(1)}, u32[]{:S(2)}, u32[]{:S(2)}) async-start(bf16[32,17,16,128]{3,2,1,0:T(8,128)(2,1)} %pack.2), calls=%async_computation | async-start | bytes 4456448 | tf_op jit(solution)/shard_map/all_to_all | solution.py:292
  12.5 20.3 %slice-start = ((s8[8388608]{0:T(1024)(128)(4,1)}), s8[4194304]{0:T(1024)(128)(4,1)S(1)}, s32[]{:S(2)}) async-start(s8[8388608]{0:T(1024)(128)(4,1)} %bitcast.52), calls=%async_computation.4 | async-start | bytes 8388608
  14.6 5.9 %copy-start.8 = (s32[2]{0:T(128)S(1)}, s32[2]{0:T(128)}, u32[]{:S(2)}) copy-start(s32[2]{0:T(128)} %constant.33.clone) | copy-start | bytes 28
  14.7 12.2 %collective-permute-start = (bf16[256,512]{1,0:T(8,128)(2,1)S(1)}, bf16[256,512]{1,0:T(8,128)(2,1)S(1)}, u32[]{:S(2)}, u32[]{:S(2)}) collective-permute-start(bf16[256,512]{1,0:T(8,128)(2,1)S(1)} %get-tuple-element.42), channel_id=1, source_target_pairs={{0,1},{1,2},{2,3},{3,4},{4,5},{5,6},{6,7},{7,0},{8,9},{9,10},{10,1... | collective-permute-start | bytes 786440 | tf_op jit(solution)/shard_map/ppermute | solution.py:304
  16.4 10.5 %collective-permute-start.1 = (bf16[256,512]{1,0:T(8,128)(2,1)S(1)}, bf16[256,512]{1,0:T(8,128)(2,1)S(1)}, u32[]{:S(2)}, u32[]{:S(2)}) collective-permute-start(bf16[256,512]{1,0:T(8,128)(2,1)S(1)} %get-tuple-element.41), channel_id=1, source_target_pairs={{0,7},{1,0},{2,1},{3,2},{4,3},{5,4},{6,5},{7,6},{8,15},{9,8},{10,9... | collective-permute-start | bytes 786440 | tf_op jit(solution)/shard_map/ppermute | solution.py:305
  20.5 3.4 %copy-start = (bf16[1024,4096]{1,0:T(8,128)(2,1)S(1)}, bf16[1024,4096]{1,0:T(8,128)(2,1)}, u32[]{:S(2)}) copy-start(bf16[1024,4096]{1,0:T(8,128)(2,1)} %weight_ref.5) | copy-start | bytes 25165828
  23.8 9.0 %slice-start.1 = ((s8[8388608]{0:T(1024)(128)(4,1)}), s8[4194304]{0:T(1024)(128)(4,1)S(1)}, s32[]{:S(2)}) async-start(s8[8388608]{0:T(1024)(128)(4,1)} %bitcast.52), calls=%async_computation.5 | async-start | bytes 8388608
  26.0 3.8 %copy-start.5 = (s32[2,1,256]{2,1,0:T(1,128)S(1)}, s32[2,1,256]{2,1,0:T(1,128)}, u32[]{:S(2)}) copy-start(s32[2,1,256]{2,1,0:T(1,128)} %slots_ref.2) | copy-start | bytes 6148
  26.0 3.8 %copy-start.6 = (s32[2,1,32]{2,1,0:T(1,128)S(1)}, s32[2,1,32]{2,1,0:T(1,128)}, u32[]{:S(2)}) copy-start(s32[2,1,32]{2,1,0:T(1,128)} %param.13) | copy-start | bytes 772
  27.1 5.7 %copy-start.7 = (s32[5]{0:T(128)S(1)}, s32[5]{0:T(128)}, u32[]{:S(2)}) copy-start(s32[5]{0:T(128)} %constant.34.clone) | copy-start | bytes 64
  27.1 14.0 %collective-permute-start.2 = (bf16[512,512]{1,0:T(8,128)(2,1)S(1)}, bf16[512,512]{1,0:T(8,128)(2,1)S(1)}, u32[]{:S(2)}, u32[]{:S(2)}) collective-permute-start(bf16[512,512]{1,0:T(8,128)(2,1)S(1)} %get-tuple-element.23), channel_id=1, source_target_pairs={{0,1},{1,2},{2,3},{3,4},{4,5},{5,6},{6,7},{7,0},{8,9},{9,10},{10,1... | collective-permute-start | bytes 1572872 | tf_op jit(solution)/shard_map/ppermute | solution.py:314
  27.2 13.9 %collective-permute-start.3 = (bf16[512,512]{1,0:T(8,128)(2,1)S(1)}, bf16[512,512]{1,0:T(8,128)(2,1)S(1)}, u32[]{:S(2)}, u32[]{:S(2)}) collective-permute-start(bf16[512,512]{1,0:T(8,128)(2,1)S(1)} %get-tuple-element.26), channel_id=1, source_target_pairs={{0,7},{1,0},{2,1},{3,2},{4,3},{5,4},{6,5},{7,6},{8,15},{9,8},{10,9... | collective-permute-start | bytes 1572872 | tf_op jit(solution)/shard_map/ppermute | solution.py:315
  31.4 1.4 copy-start.3
  37.4 3.7 %copy-start.2 = (f32[5,512,512]{2,1,0:T(8,128)}, f32[5,512,512]{2,1,0:T(8,128)S(1)}, u32[]{:S(2)}) copy-start(f32[5,512,512]{2,1,0:T(8,128)S(1)} %shares.5) | copy-start | bytes 15728644
  42.5 37.2 %all-to-all-start.1 = ((bf16[32,16,16,128]{3,2,1,0:T(8,128)(2,1)}), bf16[32,16,16,128]{3,2,1,0:T(8,128)(2,1)}, u32[]{:S(2)}, u32[]{:S(2)}) async-start(bf16[32,16,16,128]{3,2,1,0:T(8,128)(2,1)} %copy-done.3), calls=%async_computation.1 | async-start | bytes 4194304 | tf_op jit(solution)/shard_map/all_to_all | solution.py:292
  51.1 25.9 %copy-start.4 = (bf16[16,64,512]{2,1,0:T(8,128)(2,1)S(1)}, bf16[16,64,512]{2,1,0:T(8,128)(2,1)}, u32[]{:S(2)}) copy-start(bf16[16,64,512]{2,1,0:T(8,128)(2,1)} %param.12) | copy-start | bytes 3145732
  55.6 5.3 %collective-permute-start.12 = (bf16[16,32,128]{2,1,0:T(8,128)(2,1)S(1)}, bf16[16,32,128]{2,1,0:T(8,128)(2,1)S(1)}, u32[]{:S(2)}, u32[]{:S(2)}) collective-permute-start(bf16[16,32,128]{2,1,0:T(8,128)(2,1)S(1)} %shrink.3.a_ref), channel_id=1, source_target_pairs={{1,0},{2,1},{3,2},{4,3},{5,4},{6,5},{7,6},{0,7},{9,8},{10,9},{11,1... | collective-permute-start | bytes 393224 | tf_op jit(solution)/shard_map/ppermute | solution.py:272
  58.4 5.8 %collective-permute-start.13 = (bf16[16,32,128]{2,1,0:T(8,128)(2,1)S(1)}, bf16[16,32,128]{2,1,0:T(8,128)(2,1)S(1)}, u32[]{:S(2)}, u32[]{:S(2)}) collective-permute-start(bf16[16,32,128]{2,1,0:T(8,128)(2,1)S(1)} %shrink.3.a_ref), channel_id=1, source_target_pairs={{7,0},{0,1},{1,2},{2,3},{3,4},{4,5},{5,6},{6,7},{15,8},{8,9},{9,10... | collective-permute-start | bytes 393224 | tf_op jit(solution)/shard_map/ppermute | solution.py:272
  64.2 12.8 %collective-permute-start.14 = (bf16[16,32,128]{2,1,0:T(8,128)(2,1)S(1)}, bf16[16,32,128]{2,1,0:T(8,128)(2,1)S(1)}, u32[]{:S(2)}, u32[]{:S(2)}) collective-permute-start(bf16[16,32,128]{2,1,0:T(8,128)(2,1)S(1)} %get-tuple-element.44), channel_id=1, source_target_pairs={{3,0},{4,1},{5,2},{6,3},{7,4},{0,5},{1,6},{2,7},{11,8},{12,9},{13,... | collective-permute-start | bytes 393224 | tf_op jit(solution)/shard_map/ppermute | solution.py:272
  65.9 11.1 %collective-permute-start.15 = (bf16[16,32,128]{2,1,0:T(8,128)(2,1)S(1)}, bf16[16,32,128]{2,1,0:T(8,128)(2,1)S(1)}, u32[]{:S(2)}, u32[]{:S(2)}) collective-permute-start(bf16[16,32,128]{2,1,0:T(8,128)(2,1)S(1)} %get-tuple-element.43), channel_id=1, source_target_pairs={{5,0},{6,1},{7,2},{0,3},{1,4},{2,5},{3,6},{4,7},{13,8},{14,9},{15,... | collective-permute-start | bytes 393224 | tf_op jit(solution)/shard_map/ppermute | solution.py:272
  67.7 38.7 %collective-permute-start.8 = (bf16[512,512]{1,0:T(8,128)(2,1)}, bf16[512,512]{1,0:T(8,128)(2,1)}, u32[]{:S(2)}, u32[]{:S(2)}) collective-permute-start(bf16[512,512]{1,0:T(8,128)(2,1)} %get-tuple-element.28), channel_id=1, source_target_pairs={{0,1},{1,2},{2,3},{3,4},{4,5},{5,6},{6,7},{7,0},{8,9},{9,10},{10,1... | collective-permute-start | bytes 1572872 | tf_op jit(solution)/shard_map/ppermute | solution.py:314
  68.5 37.8 %collective-permute-start.9 = (bf16[512,512]{1,0:T(8,128)(2,1)}, bf16[512,512]{1,0:T(8,128)(2,1)}, u32[]{:S(2)}, u32[]{:S(2)}) collective-permute-start(bf16[512,512]{1,0:T(8,128)(2,1)} %get-tuple-element.29), channel_id=1, source_target_pairs={{0,7},{1,0},{2,1},{3,2},{4,3},{5,4},{6,5},{7,6},{8,15},{9,8},{10,9... | collective-permute-start | bytes 1572872 | tf_op jit(solution)/shard_map/ppermute | solution.py:315
  79.7 42.4 %all-to-all-start.3 = ((bf16[32,32,512]{2,1,0:T(8,128)(2,1)}), bf16[32,32,512]{2,1,0:T(8,128)(2,1)}, u32[]{:S(2)}, u32[]{:S(2)}) async-start(bf16[32,32,512]{2,1,0:T(8,128)(2,1)} %bitcast.66), calls=%async_computation.3 | async-start | bytes 2097152 | tf_op jit(solution)/shard_map/all_to_all | solution.py:292
  96.7 4.9 %collective-permute-start.4 = (bf16[16,32,128]{2,1,0:T(8,128)(2,1)S(1)}, bf16[16,32,128]{2,1,0:T(8,128)(2,1)S(1)}, u32[]{:S(2)}, u32[]{:S(2)}) collective-permute-start(bf16[16,32,128]{2,1,0:T(8,128)(2,1)S(1)} %shrink.2.a_ref), channel_id=1, source_target_pairs={{1,0},{2,1},{3,2},{4,3},{5,4},{6,5},{7,6},{0,7},{9,8},{10,9},{11,1... | collective-permute-start | bytes 393224 | tf_op jit(solution)/shard_map/ppermute | solution.py:272
  96.8 6.2 %collective-permute-start.5 = (bf16[16,32,128]{2,1,0:T(8,128)(2,1)S(1)}, bf16[16,32,128]{2,1,0:T(8,128)(2,1)S(1)}, u32[]{:S(2)}, u32[]{:S(2)}) collective-permute-start(bf16[16,32,128]{2,1,0:T(8,128)(2,1)S(1)} %shrink.2.a_ref), channel_id=1, source_target_pairs={{7,0},{0,1},{1,2},{2,3},{3,4},{4,5},{5,6},{6,7},{15,8},{8,9},{9,10... | collective-permute-start | bytes 393224 | tf_op jit(solution)/shard_map/ppermute | solution.py:272
  103.0 7.4 %collective-permute-start.6 = (bf16[16,32,128]{2,1,0:T(8,128)(2,1)S(1)}, bf16[16,32,128]{2,1,0:T(8,128)(2,1)S(1)}, u32[]{:S(2)}, u32[]{:S(2)}) collective-permute-start(bf16[16,32,128]{2,1,0:T(8,128)(2,1)S(1)} %get-tuple-element.46), channel_id=1, source_target_pairs={{3,0},{4,1},{5,2},{6,3},{7,4},{0,5},{1,6},{2,7},{11,8},{12,9},{13,... | collective-permute-start | bytes 393224 | tf_op jit(solution)/shard_map/ppermute | solution.py:272
  103.5 13.2 %collective-permute-start.7 = (bf16[16,32,128]{2,1,0:T(8,128)(2,1)S(1)}, bf16[16,32,128]{2,1,0:T(8,128)(2,1)S(1)}, u32[]{:S(2)}, u32[]{:S(2)}) collective-permute-start(bf16[16,32,128]{2,1,0:T(8,128)(2,1)S(1)} %get-tuple-element.45), channel_id=1, source_target_pairs={{5,0},{6,1},{7,2},{0,3},{1,4},{2,5},{3,6},{4,7},{13,8},{14,9},{15,... | collective-permute-start | bytes 393224 | tf_op jit(solution)/shard_map/ppermute | solution.py:272
  119.4 14.4 %collective-permute-start.10 = (bf16[512,512]{1,0:T(8,128)(2,1)}, bf16[512,512]{1,0:T(8,128)(2,1)S(1)}, u32[]{:S(2)}, u32[]{:S(2)}) collective-permute-start(bf16[512,512]{1,0:T(8,128)(2,1)} %get-tuple-element.31), channel_id=1, source_target_pairs={{0,1},{1,2},{2,3},{3,4},{4,5},{5,6},{6,7},{7,0},{8,9},{9,10},{10,1... | collective-permute-start | bytes 1572872 | tf_op jit(solution)/shard_map/ppermute | solution.py:332
  119.4 14.4 %collective-permute-start.11 = (bf16[512,512]{1,0:T(8,128)(2,1)}, bf16[512,512]{1,0:T(8,128)(2,1)S(1)}, u32[]{:S(2)}, u32[]{:S(2)}) collective-permute-start(bf16[512,512]{1,0:T(8,128)(2,1)} %get-tuple-element.32), channel_id=1, source_target_pairs={{0,7},{1,0},{2,1},{3,2},{4,3},{5,4},{6,5},{7,6},{8,15},{9,8},{10,9... | collective-permute-start | bytes 1572872 | tf_op jit(solution)/shard_map/ppermute | solution.py:333
  122.1 24.9 %all-to-all-start.2 = ((bf16[32,32,512]{2,1,0:T(8,128)(2,1)}), bf16[32,32,512]{2,1,0:T(8,128)(2,1)S(1)}, u32[]{:S(2)}, u32[]{:S(2)}) async-start(bf16[32,32,512]{2,1,0:T(8,128)(2,1)} %bitcast.67), calls=%async_computation.2 | async-start | bytes 2097152 | tf_op jit(solution)/shard_map/all_to_all | solution.py:292

commit v5 on v4

--- a/solution.py
+++ b/solution.py
@@ -310,25 +310,28 @@
     going_right, going_left = first_sums(first, top, low)
     late_tokens, _ = lax.optimization_barrier((late_tokens, going_right))
     shares = base_shares(late_tokens, query_weight, near)
-    for hop in range(far - 2):
-        going_right = lax.ppermute(going_right, "tp", right).astype(F32) + shares[2 * hop]
-        going_left = lax.ppermute(going_left, "tp", left).astype(F32) + shares[2 * hop + 1]
-        going_right, going_left = going_right.astype(BF16), going_left.astype(BF16)
-        if hop == 0:
-            sent, going_right, going_left = lax.optimization_barrier((sent, going_right, going_left))
-            x.append(swap(sent))
-
-    down = down_weight.reshape(adapters * rank, width)
-    down = pltpu.with_memory_space_constraint(down, pltpu.HBM)
+    down = pltpu.with_memory_space_constraint(down_weight.reshape(adapters * rank, width), pltpu.HBM)
+    going_right = lax.ppermute(going_right, "tp", right).astype(F32) + shares[0]
+    going_left = lax.ppermute(going_left, "tp", left).astype(F32) + shares[1]
+    going_right, going_left = going_right.astype(BF16), going_left.astype(BF16)
+    names = x[0]
+    shrunk = shrink_rows(0, names, x[0], down, most, rank)
+    sent, going_right, going_left = lax.optimization_barrier((sent, going_right, going_left))
+    x.append(swap(sent))
+
     up = up_weight.reshape(adapters * rank, features)
-    names = x[0]
     back = []
-    for t in range(steps):
-        parts = parts_over_tp(shrink_rows(t, names, x[t], down, most, rank))
-        delta = expand_rows(t, names, parts, up, rank)
-        if t == steps - 1:
-            delta, going_right, going_left = lax.optimization_barrier((delta, going_right, going_left))
-        back.append(swap(delta))
+    delta = expand_rows(0, names, parts_over_tp(shrunk), up, rank)
+    going_right = lax.ppermute(going_right, "tp", right)
+    going_left = lax.ppermute(going_left, "tp", left)
+    shrunk = shrink_rows(1, names, x[1], down, most, rank)
+    delta, shrunk = lax.optimization_barrier((delta, shrunk))
+    back.append(swap(delta))
+    delta = expand_rows(1, names, parts_over_tp(shrunk), up, rank)
+    going_right = (going_right.astype(F32) + shares[2]).astype(BF16)
+    going_left = (going_left.astype(F32) + shares[3]).astype(BF16)
+    delta, going_right, going_left = lax.optimization_barrier((delta, going_right, going_left))
+    back.append(swap(delta))
     from_left = lax.ppermute(going_right, "tp", right).astype(F32)
     from_right = lax.ppermute(going_left, "tp", left).astype(F32)
     base = (shares[-1] + from_left + from_right).reshape(steps, rows, features)

time: 149 us -> 145 us (0.973)
  waiting for transfers between devices: 40.6 us -> 34.3 us
    ppermute x8, waiting for transfers between devices: 24.2 us -> 17.9 us  [fetch(): lax.ppermute(value, 'tp', [((i + ahead) % size, i) for i in range(size)])]
    convert_element_type x2 -> x1, other arithmetic: 4.54 us -> 1.32 us  [body(): going_left.astype(BF16)]
    convert_element_type x0 -> x1, other arithmetic: none -> 3.15 us  [body(): going_left = (going_left.astype(F32) + shares[3]).astype(BF16)]
  transfers between devices with their start and end apart: 20 -> 20, of which waited for: 11 -> 9; matrix products, arithmetic and copies ran while one was open for 5% -> 6% of each run, Pallas kernels for 19% -> 20%
where the time goes in v5:
time: 145 us
  starting transfers between devices  63.4 us (44%)
  waiting for transfers between devices  34.3 us (24%)
  Pallas kernels  33.3 us (23%)
  other arithmetic  7.47 us (5%)
  local copies, waits for them, and re-layouts  5.82 us (4%)
    all_to_all x4, starting transfers between devices, swap(): lax.all_to_all(value, 'pool', split_axis=0, concat_axis=0, tiled=True)  37.3 us
    ppermute x8, waiting for transfers between devices, fetch(): lax.ppermute(value, 'tp', [((i + ahead) % size, i) for i in range(size)])  17.9 us
    ppermute x8, starting transfers between devices, fetch(): lax.ppermute(value, 'tp', [((i + ahead) % size, i) for i in range(size)])  12.1 us
    pallas_call x2, Pallas kernels, shrink_rows(): pl.pallas_call(functools.partial(shrink_kernel, step, rank), out_shape=ja...  9.2 us
    all_to_all x4, waiting for transfers between devices, swap(): lax.all_to_all(value, 'pool', split_axis=0, concat_axis=0, tiled=True)  9.11 us
    pallas_call x3, Pallas kernels, base_shares(): pl.pallas_call(shares_kernel, out_shape=jax.ShapeDtypeStruct((amount, row...  8.8 us
    pallas_call x2, Pallas kernels, expand_rows(): pl.pallas_call(functools.partial(expand_kernel, step, rank), out_shape=pl...  6.28 us
    pallas_call x2, Pallas kernels, pack(): pl.pallas_call(functools.partial(pack_kernel, step), out_shape=jax.ShapeD...  5.29 us
  transfers between devices with their start and end apart: 20, of which 9 were waited for; matrix products, arithmetic and copies ran while one was open for 6% of the time, Pallas kernels for 20%

profile of v5, /device:TPU:1, one launch (start us, length us, event | category | flops | bytes accessed | tf_op | source)
XLA Modules:
  0.0 144.6 jit_solution(228135753590695938)
XLA Ops:
  0.0 3.7 %pack.2 = bf16[32,17,16,128]{3,2,1,0:T(8,128)(2,1)} custom-call(s32[2,32]{1,0:T(2,128)} %bitcast.64, s32[2,1,256]{2,1,0:T(1,128)} %slots_ref.2, bf16[2,256,1024]{2,1,0:T(8,128)(2,1)} %tokens_ref.2), custom_call_target="tpu_custom_call" | custom-call | flops 536870912 | bytes 2752512 | tf_op jit(solution)/shard_map/pack/pallas_call | solution.py:48
  3.7 8.7 %all-to-all-start = ((bf16[32,17,16,128]{3,2,1,0:T(8,128)(2,1)}), bf16[32,17,16,128]{3,2,1,0:T(8,128)(2,1)S(1)}, u32[]{:S(2)}, u32[]{:S(2)}) async-start(bf16[32,17,16,128]{3,2,1,0:T(8,128)(2,1)} %pack.2), calls=%async_computation | async-start | bytes 4456448 | tf_op jit(solution)/shard_map/all_to_all | solution.py:292
  12.5 0.0 slice-start
  12.5 2.1 %shares.4 = f32[1,512,512]{2,1,0:T(8,128)S(1)} custom-call(s32[1]{0:T(128)S(6)} %rem.55.order_ref, bf16[512,1024]{1,0:T(8,128)(2,1)S(1)} %bitcast.54, bf16[1024,4096]{1,0:T(8,128)(2,1)} %weight_ref.5), custom_call_target="tpu_custom_call" | custom-call | flops 536870912 | bytes 2097152 | tf_op jit(solution)/shard_map/shares/pallas_call | solution.py:191
  14.6 0.0 copy-start.8
  14.6 0.1 convert_element_type.77
  14.7 1.7 %collective-permute-start.4 = (bf16[256,512]{1,0:T(8,128)(2,1)S(1)}, bf16[256,512]{1,0:T(8,128)(2,1)S(1)}, u32[]{:S(2)}, u32[]{:S(2)}) collective-permute-start(bf16[256,512]{1,0:T(8,128)(2,1)S(1)} %get-tuple-element.46), channel_id=1, source_target_pairs={{0,1},{1,2},{2,3},{3,4},{4,5},{5,6},{6,7},{7,0},{8,9},{9,10},{10,1... | collective-permute-start | bytes 786440 | tf_op jit(solution)/shard_map/ppermute | solution.py:304
  16.4 4.0 %collective-permute-start.5 = (bf16[256,512]{1,0:T(8,128)(2,1)S(1)}, bf16[256,512]{1,0:T(8,128)(2,1)S(1)}, u32[]{:S(2)}, u32[]{:S(2)}) collective-permute-start(bf16[256,512]{1,0:T(8,128)(2,1)S(1)} %get-tuple-element.45), channel_id=1, source_target_pairs={{0,7},{1,0},{2,1},{3,2},{4,3},{5,4},{6,5},{7,6},{8,15},{9,8},{10,9... | collective-permute-start | bytes 786440 | tf_op jit(solution)/shard_map/ppermute | solution.py:305
  20.5 3.4 %copy-done = bf16[1024,4096]{1,0:T(8,128)(2,1)S(1)} copy-done((bf16[1024,4096]{1,0:T(8,128)(2,1)S(1)}, bf16[1024,4096]{1,0:T(8,128)(2,1)}, u32[]{:S(2)}) %copy-start) | copy-done | bytes 8388632
  23.8 2.2 %shares.3.shares_ref = f32[2,512,512]{2,1,0:T(8,128)S(1)} custom-call(s32[2]{0:T(128)S(1)} %compare_select_fusion.2.order_ref, bf16[512,1024]{1,0:T(8,128)(2,1)S(1)} %bitcast.55, bf16[1024,4096]{1,0:T(8,128)(2,1)S(1)} %copy-done), custom_call_target="tpu_custom_call" | custom-call | flops 1073741824 | bytes 4194304 | tf_op jit(solution)/shard_map/shares/pallas_call | solution.py:191
  26.0 0.0 copy-start.5
  26.0 0.0 copy-start.6
  26.0 0.8 collective-permute-done.4.top_ref
  26.9 0.2 first_sums.1
  27.1 0.0 copy-start.7
  27.1 0.1 collective-permute-start.6
  27.2 2.7 %collective-permute-start.7 = (bf16[512,512]{1,0:T(8,128)(2,1)S(1)}, bf16[512,512]{1,0:T(8,128)(2,1)S(1)}, u32[]{:S(2)}, u32[]{:S(2)}) collective-permute-start(bf16[512,512]{1,0:T(8,128)(2,1)S(1)} %get-tuple-element.28), channel_id=1, source_target_pairs={{0,7},{1,0},{2,1},{3,2},{4,3},{5,4},{6,5},{7,6},{8,15},{9,8},{10,9... | collective-permute-start | bytes 1572872 | tf_op jit(solution)/shard_map/ppermute | solution.py:315
  29.9 1.6 %pack.3 = bf16[32,16,16,128]{3,2,1,0:T(8,128)(2,1)S(1)} custom-call(s32[2,32]{1,0:T(2,128)S(1)} %bitcast.65, s32[2,1,256]{2,1,0:T(1,128)S(1)} %copy-done.5, bf16[2,256,1024]{2,1,0:T(8,128)(2,1)S(1)} %copy-done.1), custom_call_target="tpu_custom_call" | custom-call | flops 536870912 | bytes 2621440 | tf_op jit(solution)/shard_map/pack/pallas_call | solution.py:48
  31.4 1.4 copy-done.3
  32.8 4.6 %shares.5 = f32[5,512,512]{2,1,0:T(8,128)S(1)} custom-call(s32[5]{0:T(128)S(1)} %compare_select_fusion.order_ref, bf16[512,1024]{1,0:T(8,128)(2,1)S(1)} %bitcast.56, bf16[1024,4096]{1,0:T(8,128)(2,1)S(1)} %bitcast.53), custom_call_target="tpu_custom_call" | custom-call | flops 2684354560 | bytes 10485760 | tf_op jit(solution)/shard_map/shares/pallas_call | solution.py:191
  37.4 3.7 %collective-permute-done.6 = bf16[512,512]{1,0:T(8,128)(2,1)S(1)} collective-permute-done((bf16[512,512]{1,0:T(8,128)(2,1)S(1)}, bf16[512,512]{1,0:T(8,128)(2,1)S(1)}, u32[]{:S(2)}, u32[]{:S(2)}) %collective-permute-start.6) | collective-permute-done | bytes 524320 | tf_op jit(solution)/shard_map/ppermute | solution.py:314
  41.1 1.3 fusion.8
  42.4 0.0 all-to-all-done
  42.4 8.5 %all-to-all-start.1 = ((bf16[32,16,16,128]{3,2,1,0:T(8,128)(2,1)}), bf16[32,16,16,128]{3,2,1,0:T(8,128)(2,1)}, u32[]{:S(2)}, u32[]{:S(2)}) async-start(bf16[32,16,16,128]{3,2,1,0:T(8,128)(2,1)} %copy-done.3), calls=%async_computation.1 | async-start | bytes 4194304 | tf_op jit(solution)/shard_map/all_to_all | solution.py:292
  51.0 0.0 copy-start.4
  51.0 4.5 %shrink.2.a_ref = bf16[16,32,128]{2,1,0:T(8,128)(2,1)S(1)} custom-call(bf16[2,16,17,16,128]{4,3,2,1,0:T(8,128)(2,1)S(1)} %bitcast.57, bf16[2,16,17,16,128]{4,3,2,1,0:T(8,128)(2,1)S(1)} %bitcast.58, bf16[1024,1024]{1,0:T(8,128)(2,1)} %bitcast.70), custom_call_target="tpu_custom_call" | custom-call | flops 2147483648 | bytes 4325376 | tf_op jit(solution)/shard_map/shrink/pallas_call | solution.py:114
  55.5 2.7 %collective-permute-start = (bf16[16,32,128]{2,1,0:T(8,128)(2,1)S(1)}, bf16[16,32,128]{2,1,0:T(8,128)(2,1)S(1)}, u32[]{:S(2)}, u32[]{:S(2)}) collective-permute-start(bf16[16,32,128]{2,1,0:T(8,128)(2,1)S(1)} %shrink.2.a_ref), channel_id=1, source_target_pairs={{1,0},{2,1},{3,2},{4,3},{5,4},{6,5},{7,6},{0,7},{9,8},{10,9},{11,1... | collective-permute-start | bytes 393224 | tf_op jit(solution)/shard_map/ppermute | solution.py:272
  58.3 2.6 %collective-permute-done.b_ref = bf16[16,32,128]{2,1,0:T(8,128)(2,1)S(1)} collective-permute-done((bf16[16,32,128]{2,1,0:T(8,128)(2,1)S(1)}, bf16[16,32,128]{2,1,0:T(8,128)(2,1)S(1)}, u32[]{:S(2)}, u32[]{:S(2)}) %collective-permute-start) | collective-permute-done | bytes 131104 | tf_op jit(solution)/shard_map/ppermute | solution.py:272
  60.9 3.2 %collective-permute-done.1.c_ref = bf16[16,32,128]{2,1,0:T(8,128)(2,1)S(1)} collective-permute-done((bf16[16,32,128]{2,1,0:T(8,128)(2,1)S(1)}, bf16[16,32,128]{2,1,0:T(8,128)(2,1)S(1)}, u32[]{:S(2)}, u32[]{:S(2)}) %collective-permute-start.1) | collective-permute-done | bytes 131104 | tf_op jit(solution)/shard_map/ppermute | solution.py:272
  64.1 0.1 fusion.11
  64.1 1.7 %collective-permute-start.2 = (bf16[16,32,128]{2,1,0:T(8,128)(2,1)S(1)}, bf16[16,32,128]{2,1,0:T(8,128)(2,1)S(1)}, u32[]{:S(2)}, u32[]{:S(2)}) collective-permute-start(bf16[16,32,128]{2,1,0:T(8,128)(2,1)S(1)} %get-tuple-element.50), channel_id=1, source_target_pairs={{3,0},{4,1},{5,2},{6,3},{7,4},{0,5},{1,6},{2,7},{11,8},{12,9},{13,... | collective-permute-start | bytes 393224 | tf_op jit(solution)/shard_map/ppermute | solution.py:272
  65.8 1.7 %collective-permute-start.3 = (bf16[16,32,128]{2,1,0:T(8,128)(2,1)S(1)}, bf16[16,32,128]{2,1,0:T(8,128)(2,1)S(1)}, u32[]{:S(2)}, u32[]{:S(2)}) collective-permute-start(bf16[16,32,128]{2,1,0:T(8,128)(2,1)S(1)} %get-tuple-element.49), channel_id=1, source_target_pairs={{5,0},{6,1},{7,2},{0,3},{1,4},{2,5},{3,6},{4,7},{13,8},{14,9},{15,... | collective-permute-start | bytes 393224 | tf_op jit(solution)/shard_map/ppermute | solution.py:272
  67.5 0.1 convert_reduce_fusion
  67.6 0.9 collective-permute-start.12
  68.5 1.9 %collective-permute-start.13 = (bf16[512,512]{1,0:T(8,128)(2,1)}, bf16[512,512]{1,0:T(8,128)(2,1)}, u32[]{:S(2)}, u32[]{:S(2)}) collective-permute-start(bf16[512,512]{1,0:T(8,128)(2,1)} %get-tuple-element.32), channel_id=1, source_target_pairs={{0,7},{1,0},{2,1},{3,2},{4,3},{5,4},{6,5},{7,6},{8,15},{9,8},{10,9... | collective-permute-start | bytes 1572872 | tf_op jit(solution)/shard_map/ppermute | solution.py:326
  70.3 6.6 %collective-permute-done.2.d_ref = bf16[16,32,128]{2,1,0:T(8,128)(2,1)S(1)} collective-permute-done((bf16[16,32,128]{2,1,0:T(8,128)(2,1)S(1)}, bf16[16,32,128]{2,1,0:T(8,128)(2,1)S(1)}, u32[]{:S(2)}, u32[]{:S(2)}) %collective-permute-start.2) | collective-permute-done | bytes 131104 | tf_op jit(solution)/shard_map/ppermute | solution.py:272
  76.9 2.7 %expand.2 = bf16[2,16,32,512]{3,2,1,0:T(8,128)(2,1)} custom-call(bf16[2,16,17,16,128]{4,3,2,1,0:T(8,128)(2,1)S(1)} %bitcast.59, bf16[16,32,128]{2,1,0:T(8,128)(2,1)S(1)} %shrink.2.a_ref, bf16[16,32,128]{2,1,0:T(8,128)(2,1)S(1)} %collective-permute-done.b_ref, bf16[16,32,128]{2,1,0:T(8,128)(2,1)S(1)} %collective-permute-done.1.c_ref, ...), custom_call_target="tpu_custom_call" | custom-call | flops 1073741824 | bytes 2752512 | tf_op jit(solution)/shard_map/expand/pallas_call | solution.py:161
  79.6 0.0 all-to-all-done.1
  79.6 4.7 %shrink.3.a_ref = bf16[16,32,128]{2,1,0:T(8,128)(2,1)S(1)} custom-call(bf16[2,16,17,16,128]{4,3,2,1,0:T(8,128)(2,1)S(1)} %bitcast.60, bf16[2,16,16,16,128]{4,3,2,1,0:T(8,128)(2,1)} %bitcast.12.x_ref, bf16[1024,1024]{1,0:T(8,128)(2,1)} %bitcast.71), custom_call_target="tpu_custom_call" | custom-call | flops 2147483648 | bytes 4194304 | tf_op jit(solution)/shard_map/shrink/pallas_call | solution.py:114
  84.3 2.7 %collective-permute-start.8 = (bf16[16,32,128]{2,1,0:T(8,128)(2,1)S(1)}, bf16[16,32,128]{2,1,0:T(8,128)(2,1)S(1)}, u32[]{:S(2)}, u32[]{:S(2)}) collective-permute-start(bf16[16,32,128]{2,1,0:T(8,128)(2,1)S(1)} %shrink.3.a_ref), channel_id=1, source_target_pairs={{1,0},{2,1},{3,2},{4,3},{5,4},{6,5},{7,6},{0,7},{9,8},{10,9},{11,1... | collective-permute-start | bytes 393224 | tf_op jit(solution)/shard_map/ppermute | solution.py:272
  87.0 11.7 %all-to-all-start.3 = ((bf16[32,32,512]{2,1,0:T(8,128)(2,1)}), bf16[32,32,512]{2,1,0:T(8,128)(2,1)}, u32[]{:S(2)}, u32[]{:S(2)}) async-start(bf16[32,32,512]{2,1,0:T(8,128)(2,1)} %bitcast.66), calls=%async_computation.3 | async-start | bytes 2097152 | tf_op jit(solution)/shard_map/all_to_all | solution.py:292
  98.7 0.1 select_reduce_fusion
  98.8 0.0 collective-permute-done.8.b_ref
  98.8 0.0 collective-permute-done.9.c_ref
  98.8 1.0 fusion.12
  99.8 0.3 collective-permute-start.10
  100.1 3.0 %collective-permute-start.11 = (bf16[16,32,128]{2,1,0:T(8,128)(2,1)S(1)}, bf16[16,32,128]{2,1,0:T(8,128)(2,1)S(1)}, u32[]{:S(2)}, u32[]{:S(2)}) collective-permute-start(bf16[16,32,128]{2,1,0:T(8,128)(2,1)S(1)} %get-tuple-element.47), channel_id=1, source_target_pairs={{5,0},{6,1},{7,2},{0,3},{1,4},{2,5},{3,6},{4,7},{13,8},{14,9},{15,... | collective-permute-start | bytes 393224 | tf_op jit(solution)/shard_map/ppermute | solution.py:272
  103.2 0.0 collective-permute-done.12
  103.2 3.1 %fusion.4 = (bf16[512,512]{1,0:T(8,128)(2,1)}, bf16[512,512]{1,0:T(8,128)(2,1)}) fusion(f32[5,512,512]{2,1,0:T(8,128)} %copy-done.2, bf16[512,512]{1,0:T(8,128)(2,1)} %collective-permute-done.13, bf16[512,512]{1,0:T(8,128)(2,1)} %collective-permute-done.12), kind=kLoop, calls=%fused_computation.7 | loop fusion | flops 1572864 | bytes 4194304 | tf_op jit(solution)/shard_map/convert_element_type | solution.py:332
  106.3 3.1 %collective-permute-done.10.d_ref = bf16[16,32,128]{2,1,0:T(8,128)(2,1)S(1)} collective-permute-done((bf16[16,32,128]{2,1,0:T(8,128)(2,1)S(1)}, bf16[16,32,128]{2,1,0:T(8,128)(2,1)S(1)}, u32[]{:S(2)}, u32[]{:S(2)}) %collective-permute-start.10) | collective-permute-done | bytes 131104 | tf_op jit(solution)/shard_map/ppermute | solution.py:272
  109.4 2.5 %collective-permute-done.11.e_ref = bf16[16,32,128]{2,1,0:T(8,128)(2,1)S(1)} collective-permute-done((bf16[16,32,128]{2,1,0:T(8,128)(2,1)S(1)}, bf16[16,32,128]{2,1,0:T(8,128)(2,1)S(1)}, u32[]{:S(2)}, u32[]{:S(2)}) %collective-permute-start.11) | collective-permute-done | bytes 131104 | tf_op jit(solution)/shard_map/ppermute | solution.py:272
  111.9 3.6 %expand.3 = bf16[2,16,32,512]{3,2,1,0:T(8,128)(2,1)} custom-call(bf16[2,16,17,16,128]{4,3,2,1,0:T(8,128)(2,1)S(1)} %bitcast.61, bf16[16,32,128]{2,1,0:T(8,128)(2,1)S(1)} %shrink.3.a_ref, bf16[16,32,128]{2,1,0:T(8,128)(2,1)S(1)} %collective-permute-done.8.b_ref, bf16[16,32,128]{2,1,0:T(8,128)(2,1)} %collective-permute-done.9.c_ref, ...), custom_call_target="tpu_custom_call" | custom-call | flops 1073741824 | bytes 2752512 | tf_op jit(solution)/shard_map/expand/pallas_call | solution.py:161
  115.5 1.0 collective-permute-start.14
  116.4 1.7 %collective-permute-start.15 = (bf16[512,512]{1,0:T(8,128)(2,1)}, bf16[512,512]{1,0:T(8,128)(2,1)S(1)}, u32[]{:S(2)}, u32[]{:S(2)}) collective-permute-start(bf16[512,512]{1,0:T(8,128)(2,1)} %get-tuple-element.35), channel_id=1, source_target_pairs={{0,7},{1,0},{2,1},{3,2},{4,3},{5,4},{6,5},{7,6},{8,15},{9,8},{10,9... | collective-permute-start | bytes 1572872 | tf_op jit(solution)/shard_map/ppermute | solution.py:336
  118.1 8.3 %all-to-all-start.2 = ((bf16[32,32,512]{2,1,0:T(8,128)(2,1)}), bf16[32,32,512]{2,1,0:T(8,128)(2,1)S(1)}, u32[]{:S(2)}, u32[]{:S(2)}) async-start(bf16[32,32,512]{2,1,0:T(8,128)(2,1)} %bitcast.67), calls=%async_computation.2 | async-start | bytes 2097152 | tf_op jit(solution)/shard_map/all_to_all | solution.py:292
  126.5 0.2 fusion
  126.7 0.1 slice_bitcast_fusion.5
  126.8 2.8 %collective-permute-done.14 = bf16[512,512]{1,0:T(8,128)(2,1)S(1)} collective-permute-done((bf16[512,512]{1,0:T(8,128)(2,1)}, bf16[512,512]{1,0:T(8,128)(2,1)S(1)}, u32[]{:S(2)}, u32[]{:S(2)}) %collective-permute-start.14) | collective-permute-done | bytes 524320 | tf_op jit(solution)/shard_map/ppermute | solution.py:335
  129.6 1.4 fusion.2
  131.0 0.1 fusion.15
  131.1 0.8 broadcast_in_dim.23.earlier_ref
  131.9 2.4 %join.2.earlier_ref = bf16[2,256,512]{2,1,0:T(8,128)(2,1)} custom-call(bf16[256,1024]{1,0:T(8,128)(2,1)S(1)} %get-tuple-element.43.spread_ref, bf16[32,32,512]{2,1,0:T(8,128)(2,1)} %all-to-all-done.3.back_ref, f32[256,512]{1,0:T(8,128)S(1)} %get-tuple-element.41.base_ref, ...), custom_call_target="tpu_custom_call", output_to_operand_aliasing={{}: (3, {})} | custom-call | flops 268435456 | bytes 2359296 | tf_op jit(solution)/shard_map/join/pallas_call | solution.py:245
  134.3 9.1 %all-to-all-done.2.back_ref = bf16[32,32,512]{2,1,0:T(8,128)(2,1)S(1)} async-done(((bf16[32,32,512]{2,1,0:T(8,128)(2,1)}), bf16[32,32,512]{2,1,0:T(8,128)(2,1)S(1)}, u32[]{:S(2)}, u32[]{:S(2)}) %all-to-all-start.2) | async-done | bytes 1048608 | tf_op jit(solution)/shard_map/all_to_all | solution.py:292
  143.4 1.2 join.3
  (29 shorter events, 0.1 us)
Async XLA Ops:
  3.7 8.7 %copy-start.1 = (bf16[2,256,1024]{2,1,0:T(8,128)(2,1)S(1)}, bf16[2,256,1024]{2,1,0:T(8,128)(2,1)}, u32[]{:S(2)}) copy-start(bf16[2,256,1024]{2,1,0:T(8,128)(2,1)} %tokens_ref.2) | copy-start | bytes 3145732
  3.7 38.7 %all-to-all-start = ((bf16[32,17,16,128]{3,2,1,0:T(8,128)(2,1)}), bf16[32,17,16,128]{3,2,1,0:T(8,128)(2,1)S(1)}, u32[]{:S(2)}, u32[]{:S(2)}) async-start(bf16[32,17,16,128]{3,2,1,0:T(8,128)(2,1)} %pack.2), calls=%async_computation | async-start | bytes 4456448 | tf_op jit(solution)/shard_map/all_to_all | solution.py:292
  12.5 20.3 %slice-start = ((s8[8388608]{0:T(1024)(128)(4,1)}), s8[4194304]{0:T(1024)(128)(4,1)S(1)}, s32[]{:S(2)}) async-start(s8[8388608]{0:T(1024)(128)(4,1)} %bitcast.52), calls=%async_computation.4 | async-start | bytes 8388608
  14.6 5.9 %copy-start.8 = (s32[2]{0:T(128)S(1)}, s32[2]{0:T(128)}, u32[]{:S(2)}) copy-start(s32[2]{0:T(128)} %constant.33.clone) | copy-start | bytes 28
  14.7 12.2 %collective-permute-start.4 = (bf16[256,512]{1,0:T(8,128)(2,1)S(1)}, bf16[256,512]{1,0:T(8,128)(2,1)S(1)}, u32[]{:S(2)}, u32[]{:S(2)}) collective-permute-start(bf16[256,512]{1,0:T(8,128)(2,1)S(1)} %get-tuple-element.46), channel_id=1, source_target_pairs={{0,1},{1,2},{2,3},{3,4},{4,5},{5,6},{6,7},{7,0},{8,9},{9,10},{10,1... | collective-permute-start | bytes 786440 | tf_op jit(solution)/shard_map/ppermute | solution.py:304
  16.4 10.5 %collective-permute-start.5 = (bf16[256,512]{1,0:T(8,128)(2,1)S(1)}, bf16[256,512]{1,0:T(8,128)(2,1)S(1)}, u32[]{:S(2)}, u32[]{:S(2)}) collective-permute-start(bf16[256,512]{1,0:T(8,128)(2,1)S(1)} %get-tuple-element.45), channel_id=1, source_target_pairs={{0,7},{1,0},{2,1},{3,2},{4,3},{5,4},{6,5},{7,6},{8,15},{9,8},{10,9... | collective-permute-start | bytes 786440 | tf_op jit(solution)/shard_map/ppermute | solution.py:305
  20.5 3.4 %copy-start = (bf16[1024,4096]{1,0:T(8,128)(2,1)S(1)}, bf16[1024,4096]{1,0:T(8,128)(2,1)}, u32[]{:S(2)}) copy-start(bf16[1024,4096]{1,0:T(8,128)(2,1)} %weight_ref.5) | copy-start | bytes 25165828
  23.8 9.0 %slice-start.1 = ((s8[8388608]{0:T(1024)(128)(4,1)}), s8[4194304]{0:T(1024)(128)(4,1)S(1)}, s32[]{:S(2)}) async-start(s8[8388608]{0:T(1024)(128)(4,1)} %bitcast.52), calls=%async_computation.5 | async-start | bytes 8388608
  26.0 3.8 %copy-start.5 = (s32[2,1,256]{2,1,0:T(1,128)S(1)}, s32[2,1,256]{2,1,0:T(1,128)}, u32[]{:S(2)}) copy-start(s32[2,1,256]{2,1,0:T(1,128)} %slots_ref.2) | copy-start | bytes 6148
  26.0 3.8 %copy-start.6 = (s32[2,1,32]{2,1,0:T(1,128)S(1)}, s32[2,1,32]{2,1,0:T(1,128)}, u32[]{:S(2)}) copy-start(s32[2,1,32]{2,1,0:T(1,128)} %param.13) | copy-start | bytes 772
  27.1 5.7 %copy-start.7 = (s32[5]{0:T(128)S(1)}, s32[5]{0:T(128)}, u32[]{:S(2)}) copy-start(s32[5]{0:T(128)} %constant.34.clone) | copy-start | bytes 64
  27.1 14.0 %collective-permute-start.6 = (bf16[512,512]{1,0:T(8,128)(2,1)S(1)}, bf16[512,512]{1,0:T(8,128)(2,1)S(1)}, u32[]{:S(2)}, u32[]{:S(2)}) collective-permute-start(bf16[512,512]{1,0:T(8,128)(2,1)S(1)} %get-tuple-element.25), channel_id=1, source_target_pairs={{0,1},{1,2},{2,3},{3,4},{4,5},{5,6},{6,7},{7,0},{8,9},{9,10},{10,1... | collective-permute-start | bytes 1572872 | tf_op jit(solution)/shard_map/ppermute | solution.py:314
  27.2 13.9 %collective-permute-start.7 = (bf16[512,512]{1,0:T(8,128)(2,1)S(1)}, bf16[512,512]{1,0:T(8,128)(2,1)S(1)}, u32[]{:S(2)}, u32[]{:S(2)}) collective-permute-start(bf16[512,512]{1,0:T(8,128)(2,1)S(1)} %get-tuple-element.28), channel_id=1, source_target_pairs={{0,7},{1,0},{2,1},{3,2},{4,3},{5,4},{6,5},{7,6},{8,15},{9,8},{10,9... | collective-permute-start | bytes 1572872 | tf_op jit(solution)/shard_map/ppermute | solution.py:315
  31.4 1.4 copy-start.3
  37.4 3.7 %copy-start.2 = (f32[5,512,512]{2,1,0:T(8,128)}, f32[5,512,512]{2,1,0:T(8,128)S(1)}, u32[]{:S(2)}) copy-start(f32[5,512,512]{2,1,0:T(8,128)S(1)} %shares.5) | copy-start | bytes 15728644
  42.4 37.2 %all-to-all-start.1 = ((bf16[32,16,16,128]{3,2,1,0:T(8,128)(2,1)}), bf16[32,16,16,128]{3,2,1,0:T(8,128)(2,1)}, u32[]{:S(2)}, u32[]{:S(2)}) async-start(bf16[32,16,16,128]{3,2,1,0:T(8,128)(2,1)} %copy-done.3), calls=%async_computation.1 | async-start | bytes 4194304 | tf_op jit(solution)/shard_map/all_to_all | solution.py:292
  51.0 25.9 %copy-start.4 = (bf16[16,64,512]{2,1,0:T(8,128)(2,1)S(1)}, bf16[16,64,512]{2,1,0:T(8,128)(2,1)}, u32[]{:S(2)}) copy-start(bf16[16,64,512]{2,1,0:T(8,128)(2,1)} %param.12) | copy-start | bytes 3145732
  55.5 5.3 %collective-permute-start = (bf16[16,32,128]{2,1,0:T(8,128)(2,1)S(1)}, bf16[16,32,128]{2,1,0:T(8,128)(2,1)S(1)}, u32[]{:S(2)}, u32[]{:S(2)}) collective-permute-start(bf16[16,32,128]{2,1,0:T(8,128)(2,1)S(1)} %shrink.2.a_ref), channel_id=1, source_target_pairs={{1,0},{2,1},{3,2},{4,3},{5,4},{6,5},{7,6},{0,7},{9,8},{10,9},{11,1... | collective-permute-start | bytes 393224 | tf_op jit(solution)/shard_map/ppermute | solution.py:272
  58.3 5.8 %collective-permute-start.1 = (bf16[16,32,128]{2,1,0:T(8,128)(2,1)S(1)}, bf16[16,32,128]{2,1,0:T(8,128)(2,1)S(1)}, u32[]{:S(2)}, u32[]{:S(2)}) collective-permute-start(bf16[16,32,128]{2,1,0:T(8,128)(2,1)S(1)} %shrink.2.a_ref), channel_id=1, source_target_pairs={{7,0},{0,1},{1,2},{2,3},{3,4},{4,5},{5,6},{6,7},{15,8},{8,9},{9,10... | collective-permute-start | bytes 393224 | tf_op jit(solution)/shard_map/ppermute | solution.py:272
  64.1 12.8 %collective-permute-start.2 = (bf16[16,32,128]{2,1,0:T(8,128)(2,1)S(1)}, bf16[16,32,128]{2,1,0:T(8,128)(2,1)S(1)}, u32[]{:S(2)}, u32[]{:S(2)}) collective-permute-start(bf16[16,32,128]{2,1,0:T(8,128)(2,1)S(1)} %get-tuple-element.50), channel_id=1, source_target_pairs={{3,0},{4,1},{5,2},{6,3},{7,4},{0,5},{1,6},{2,7},{11,8},{12,9},{13,... | collective-permute-start | bytes 393224 | tf_op jit(solution)/shard_map/ppermute | solution.py:272
  65.8 11.1 %collective-permute-start.3 = (bf16[16,32,128]{2,1,0:T(8,128)(2,1)S(1)}, bf16[16,32,128]{2,1,0:T(8,128)(2,1)S(1)}, u32[]{:S(2)}, u32[]{:S(2)}) collective-permute-start(bf16[16,32,128]{2,1,0:T(8,128)(2,1)S(1)} %get-tuple-element.49), channel_id=1, source_target_pairs={{5,0},{6,1},{7,2},{0,3},{1,4},{2,5},{3,6},{4,7},{13,8},{14,9},{15,... | collective-permute-start | bytes 393224 | tf_op jit(solution)/shard_map/ppermute | solution.py:272
  67.6 35.6 %collective-permute-start.12 = (bf16[512,512]{1,0:T(8,128)(2,1)}, bf16[512,512]{1,0:T(8,128)(2,1)}, u32[]{:S(2)}, u32[]{:S(2)}) collective-permute-start(bf16[512,512]{1,0:T(8,128)(2,1)} %get-tuple-element.31), channel_id=1, source_target_pairs={{0,1},{1,2},{2,3},{3,4},{4,5},{5,6},{6,7},{7,0},{8,9},{9,10},{10,1... | collective-permute-start | bytes 1572872 | tf_op jit(solution)/shard_map/ppermute | solution.py:325
  68.5 34.7 %collective-permute-start.13 = (bf16[512,512]{1,0:T(8,128)(2,1)}, bf16[512,512]{1,0:T(8,128)(2,1)}, u32[]{:S(2)}, u32[]{:S(2)}) collective-permute-start(bf16[512,512]{1,0:T(8,128)(2,1)} %get-tuple-element.32), channel_id=1, source_target_pairs={{0,7},{1,0},{2,1},{3,2},{4,3},{5,4},{6,5},{7,6},{8,15},{9,8},{10,9... | collective-permute-start | bytes 1572872 | tf_op jit(solution)/shard_map/ppermute | solution.py:326
  84.3 14.5 %collective-permute-start.8 = (bf16[16,32,128]{2,1,0:T(8,128)(2,1)S(1)}, bf16[16,32,128]{2,1,0:T(8,128)(2,1)S(1)}, u32[]{:S(2)}, u32[]{:S(2)}) collective-permute-start(bf16[16,32,128]{2,1,0:T(8,128)(2,1)S(1)} %shrink.3.a_ref), channel_id=1, source_target_pairs={{1,0},{2,1},{3,2},{4,3},{5,4},{6,5},{7,6},{0,7},{9,8},{10,9},{11,1... | collective-permute-start | bytes 393224 | tf_op jit(solution)/shard_map/ppermute | solution.py:272
  87.0 11.8 %collective-permute-start.9 = (bf16[16,32,128]{2,1,0:T(8,128)(2,1)S(1)}, bf16[16,32,128]{2,1,0:T(8,128)(2,1)}, u32[]{:S(2)}, u32[]{:S(2)}) collective-permute-start(bf16[16,32,128]{2,1,0:T(8,128)(2,1)S(1)} %shrink.3.a_ref), channel_id=1, source_target_pairs={{7,0},{0,1},{1,2},{2,3},{3,4},{4,5},{5,6},{6,7},{15,8},{8,9},{9,10... | collective-permute-start | bytes 393224 | tf_op jit(solution)/shard_map/ppermute | solution.py:272
  87.0 31.1 %all-to-all-start.3 = ((bf16[32,32,512]{2,1,0:T(8,128)(2,1)}), bf16[32,32,512]{2,1,0:T(8,128)(2,1)}, u32[]{:S(2)}, u32[]{:S(2)}) async-start(bf16[32,32,512]{2,1,0:T(8,128)(2,1)} %bitcast.66), calls=%async_computation.3 | async-start | bytes 2097152 | tf_op jit(solution)/shard_map/all_to_all | solution.py:292
  99.8 9.6 %collective-permute-start.10 = (bf16[16,32,128]{2,1,0:T(8,128)(2,1)S(1)}, bf16[16,32,128]{2,1,0:T(8,128)(2,1)S(1)}, u32[]{:S(2)}, u32[]{:S(2)}) collective-permute-start(bf16[16,32,128]{2,1,0:T(8,128)(2,1)S(1)} %get-tuple-element.48), channel_id=1, source_target_pairs={{3,0},{4,1},{5,2},{6,3},{7,4},{0,5},{1,6},{2,7},{11,8},{12,9},{13,... | collective-permute-start | bytes 393224 | tf_op jit(solution)/shard_map/ppermute | solution.py:272
  100.1 11.7 %collective-permute-start.11 = (bf16[16,32,128]{2,1,0:T(8,128)(2,1)S(1)}, bf16[16,32,128]{2,1,0:T(8,128)(2,1)S(1)}, u32[]{:S(2)}, u32[]{:S(2)}) collective-permute-start(bf16[16,32,128]{2,1,0:T(8,128)(2,1)S(1)} %get-tuple-element.47), channel_id=1, source_target_pairs={{5,0},{6,1},{7,2},{0,3},{1,4},{2,5},{3,6},{4,7},{13,8},{14,9},{15,... | collective-permute-start | bytes 393224 | tf_op jit(solution)/shard_map/ppermute | solution.py:272
  115.5 14.1 %collective-permute-start.14 = (bf16[512,512]{1,0:T(8,128)(2,1)}, bf16[512,512]{1,0:T(8,128)(2,1)S(1)}, u32[]{:S(2)}, u32[]{:S(2)}) collective-permute-start(bf16[512,512]{1,0:T(8,128)(2,1)} %get-tuple-element.34), channel_id=1, source_target_pairs={{0,1},{1,2},{2,3},{3,4},{4,5},{5,6},{6,7},{7,0},{8,9},{9,10},{10,1... | collective-permute-start | bytes 1572872 | tf_op jit(solution)/shard_map/ppermute | solution.py:335
  116.4 13.1 %collective-permute-start.15 = (bf16[512,512]{1,0:T(8,128)(2,1)}, bf16[512,512]{1,0:T(8,128)(2,1)S(1)}, u32[]{:S(2)}, u32[]{:S(2)}) collective-permute-start(bf16[512,512]{1,0:T(8,128)(2,1)} %get-tuple-element.35), channel_id=1, source_target_pairs={{0,7},{1,0},{2,1},{3,2},{4,3},{5,4},{6,5},{7,6},{8,15},{9,8},{10,9... | collective-permute-start | bytes 1572872 | tf_op jit(solution)/shard_map/ppermute | solution.py:336
  118.1 25.3 %all-to-all-start.2 = ((bf16[32,32,512]{2,1,0:T(8,128)(2,1)}), bf16[32,32,512]{2,1,0:T(8,128)(2,1)S(1)}, u32[]{:S(2)}, u32[]{:S(2)}) async-start(bf16[32,32,512]{2,1,0:T(8,128)(2,1)} %bitcast.67), calls=%async_computation.2 | async-start | bytes 2097152 | tf_op jit(solution)/shard_map/all_to_all | solution.py:292

commit v6 on v5

--- a/solution.py
+++ b/solution.py
@@ -35,10 +35,17 @@
         for c in range(across):
             out_ref[:, down * across + c] = value[:, down, :, c * LANES : (c + 1) * LANES]
     if step == 0:
-        line = lax.broadcasted_iota(jnp.int32, (TILE, LANES), 0)
-        for s in range(block):
-            names = jnp.where(line < TILE // 2, asked_ref[0, first + s], asked_ref[1, first + s])
-            out_ref[s, most // TILE * across] = names.astype(F32).astype(BF16)
+        shape = (block, TILE, asked_ref.shape[1])
+        here = lax.broadcasted_iota(jnp.int32, shape, 2) == lax.broadcasted_iota(jnp.int32, shape, 0) + first
+        line = lax.broadcasted_iota(jnp.int32, shape, 1)
+        asked = jnp.where(
+            line < TILE // 2,
+            jnp.broadcast_to(asked_ref[0:1, :].reshape(1, 1, -1), shape),
+            jnp.broadcast_to(asked_ref[1:2, :].reshape(1, 1, -1), shape),
+        )
+        names = jnp.sum(jnp.where(here, asked.astype(F32), 0.0), axis=2, keepdims=True)
+        names = jnp.broadcast_to(names, (block, TILE, LANES))
+        out_ref[:, most // TILE * across] = names.astype(BF16)
 
 
 def pack(step, asked, slots, tokens, most, block=16):
@@ -48,15 +55,13 @@
     return pl.pallas_call(
         functools.partial(pack_kernel, step),
         out_shape=jax.ShapeDtypeStruct((count, tiles, TILE, LANES), BF16),
-        grid_spec=pltpu.PrefetchScalarGridSpec(
-            num_scalar_prefetch=1,
-            grid=(count // block,),
-            in_specs=[
-                pl.BlockSpec((1, 1, rows), lambda i, asked: (step, 0, 0)),
-                pl.BlockSpec((1, rows, width), lambda i, asked: (step, 0, 0)),
-            ],
-            out_specs=pl.BlockSpec((block, tiles, TILE, LANES), lambda i, asked: (i, 0, 0, 0)),
-        ),
+        grid=(count // block,),
+        in_specs=[
+            pl.BlockSpec(asked.shape, lambda i: (0, 0)),
+            pl.BlockSpec((1, 1, rows), lambda i: (step, 0, 0)),
+            pl.BlockSpec((1, rows, width), lambda i: (step, 0, 0)),
+        ],
+        out_specs=pl.BlockSpec((block, tiles, TILE, LANES), lambda i: (i, 0, 0, 0)),
         compiler_params=pltpu.CompilerParams(vmem_limit_bytes=FULL if step == 0 else VMEM),
         cost_estimate=pl.CostEstimate(
             flops=2 * count * most * rows * width,
@@ -92,12 +97,11 @@
     parts = []
     for h in range(halves):
         wanted = named(names_ref, step, h, block, most)
-        value = jnp.zeros((block, most, LANES), F32)
-        odd = jnp.zeros((block, most, LANES), F32)
-        for c in range(held // LANES):
-            here = acc_ref[h, :, :, c * LANES : (c + 1) * LANES]
-            value = jnp.where((wanted == 2.0 * c) | (wanted == 2.0 * c + 1.0), here, value)
-            odd = jnp.where(wanted == 2.0 * c + 1.0, 1.0, odd)
+        pair = jnp.floor(wanted * 0.5)
+        odd = wanted - 2.0 * pair
+        value = acc_ref[h, :, :, :LANES]
+        for c in range(1, held // LANES):
+            value = jnp.where(pair == 1.0 * c, acc_ref[h, :, :, c * LANES : (c + 1) * LANES], value)
         value = value.reshape(block * most, LANES)
         odd = odd.reshape(block * most, LANES)
         parts.append(jnp.where(odd == 1.0 * h, value, pltpu.roll(value, rank, 1)))
@@ -145,8 +149,9 @@
     for h in range(halves):
         wanted = named(names_ref, step, h, block, most)
         chosen = jnp.where(high == 1.0 * h, both, swapped)
+        place = (wanted - high) * 0.5
         for c in range(held // LANES):
-            value = jnp.where(wanted == 2.0 * c + high, chosen, 0.0)
+            value = jnp.where(place == 1.0 * c, chosen, 0.0)
             wide_ref[h, :, :, c * LANES : (c + 1) * LANES] = value.astype(BF16)
     wide = wide_ref[...].reshape(halves * block * most, held)
     out = jnp.dot(wide, up_ref[...], preferred_element_type=F32)
@@ -311,13 +316,14 @@
     late_tokens, _ = lax.optimization_barrier((late_tokens, going_right))
     shares = base_shares(late_tokens, query_weight, near)
     down = pltpu.with_memory_space_constraint(down_weight.reshape(adapters * rank, width), pltpu.HBM)
-    going_right = lax.ppermute(going_right, "tp", right).astype(F32) + shares[0]
-    going_left = lax.ppermute(going_left, "tp", left).astype(F32) + shares[1]
-    going_right, going_left = going_right.astype(BF16), going_left.astype(BF16)
+    going_right = lax.ppermute(going_right, "tp", right)
+    going_left = lax.ppermute(going_left, "tp", left)
     names = x[0]
     shrunk = shrink_rows(0, names, x[0], down, most, rank)
-    sent, going_right, going_left = lax.optimization_barrier((sent, going_right, going_left))
+    sent, going_right, going_left, shares = lax.optimization_barrier((sent, going_right, going_left, shares))
     x.append(swap(sent))
+    going_right = (going_right.astype(F32) + shares[0]).astype(BF16)
+    going_left = (going_left.astype(F32) + shares[1]).astype(BF16)
 
     up = up_weight.reshape(adapters * rank, features)
     back = []

time: 145 us -> 145 us (level)
  local copies, waits for them, and re-layouts: 5.82 us -> 8.94 us
  starting transfers between devices: 63.4 us -> 61.4 us
  waiting for transfers between devices: 34.3 us -> 32.5 us
  other arithmetic: 7.47 us -> 9.22 us
    ppermute x2 -> x0, waiting for transfers between devices: 3.7 us -> none  [the longest x1 3.7 us: body(): going_right = lax.ppermute(going_right, 'tp', right).astype(F32) + shares[0]]
    unnamed x23 -> x27, local copies, waits for them, and re-layouts: 4.81 us -> 7.94 us
    ppermute x1 -> x2, starting transfers between devices: 1.88 us -> 4.96 us  [body(): going_left = lax.ppermute(going_left, 'tp', left)]
    ppermute x2 -> x0, starting transfers between devices: 2.75 us -> none  [the longest x1 2.66 us: body(): going_left = lax.ppermute(going_left, 'tp', left).astype(F32) + shares[1]]
    ppermute x1 -> x2, waiting for transfers between devices: 0.01 us -> 1.93 us  [body(): going_right = lax.ppermute(going_right, 'tp', right)]
    convert_element_type x1, other arithmetic: 1.32 us -> 3.06 us  [body(): going_left = (going_left.astype(F32) + shares[1]).astype(BF16)]
    all_to_all x4, starting transfers between devices: 37.3 us -> 35.6 us  [swap(): lax.all_to_all(value, 'pool', split_axis=0, concat_axis=0, tiled=True)]
  transfers between devices with their start and end apart: 20 -> 20, of which waited for: 9 -> 10; matrix products, arithmetic and copies ran while one was open for 6% -> 7% of each run, Pallas kernels for 20% -> 19%
where the time goes in v6:
time: 145 us; the launch traced here: 144 us
  starting transfers between devices  61.4 us (42%)
  waiting for transfers between devices  32.5 us (22%)
  Pallas kernels  31.9 us (22%)
  other arithmetic  9.22 us (6%)
  local copies, waits for them, and re-layouts  8.94 us (6%)
    all_to_all x4, starting transfers between devices, swap(): lax.all_to_all(value, 'pool', split_axis=0, concat_axis=0, tiled=True)  35.6 us
    ppermute x8, waiting for transfers between devices, fetch(): lax.ppermute(value, 'tp', [((i + ahead) % size, i) for i in range(size)])  17.6 us
    ppermute x8, starting transfers between devices, fetch(): lax.ppermute(value, 'tp', [((i + ahead) % size, i) for i in range(size)])  12 us
    pallas_call x2, Pallas kernels, shrink_rows(): pl.pallas_call(functools.partial(shrink_kernel, step, rank), out_shape=ja...  9.18 us
    pallas_call x3, Pallas kernels, base_shares(): pl.pallas_call(shares_kernel, out_shape=jax.ShapeDtypeStruct((amount, row...  8.81 us
    all_to_all x4, waiting for transfers between devices, swap(): lax.all_to_all(value, 'pool', split_axis=0, concat_axis=0, tiled=True)  8.59 us
    unnamed x27, local copies, waits for them, and re-layouts  7.94 us
    pallas_call x2, Pallas kernels, expand_rows(): pl.pallas_call(functools.partial(expand_kernel, step, rank), out_shape=pl...  6.21 us
  transfers between devices with their start and end apart: 20, of which 10 were waited for; matrix products, arithmetic and copies ran while one was open for 7% of the time, Pallas kernels for 19%

profile of v6, /device:TPU:1, one launch (start us, length us, event | category | flops | bytes accessed | tf_op | source)
XLA Modules:
  0.0 144.3 jit_solution(3106485902864558930)
XLA Ops:
  0.0 3.1 %pack.2 = bf16[32,17,16,128]{3,2,1,0:T(8,128)(2,1)} custom-call(s32[2,32]{1,0:T(2,128)} %bitcast.54, s32[2,1,256]{2,1,0:T(1,128)} %slots_ref.2, bf16[2,256,1024]{2,1,0:T(8,128)(2,1)} %tokens_ref.2), custom_call_target="tpu_custom_call" | custom-call | flops 536870912 | bytes 2752512 | tf_op jit(solution)/shard_map/pack/pallas_call | solution.py:55
  3.1 8.7 %all-to-all-start = ((bf16[32,17,16,128]{3,2,1,0:T(8,128)(2,1)}), bf16[32,17,16,128]{3,2,1,0:T(8,128)(2,1)S(1)}, u32[]{:S(2)}, u32[]{:S(2)}) async-start(bf16[32,17,16,128]{3,2,1,0:T(8,128)(2,1)} %pack.2), calls=%async_computation | async-start | bytes 4456448 | tf_op jit(solution)/shard_map/all_to_all | solution.py:297
  11.8 0.0 slice-start
  11.8 2.1 %shares.4 = f32[1,512,512]{2,1,0:T(8,128)S(1)} custom-call(s32[1]{0:T(128)S(6)} %rem.55.order_ref, bf16[512,1024]{1,0:T(8,128)(2,1)S(1)} %bitcast.44, bf16[1024,4096]{1,0:T(8,128)(2,1)} %weight_ref.5), custom_call_target="tpu_custom_call" | custom-call | flops 536870912 | bytes 2097152 | tf_op jit(solution)/shard_map/shares/pallas_call | solution.py:196
  13.9 0.0 copy-start.10
  13.9 0.1 convert_element_type.77
  14.0 1.7 %collective-permute-start.4 = (bf16[256,512]{1,0:T(8,128)(2,1)S(1)}, bf16[256,512]{1,0:T(8,128)(2,1)S(1)}, u32[]{:S(2)}, u32[]{:S(2)}) collective-permute-start(bf16[256,512]{1,0:T(8,128)(2,1)S(1)} %get-tuple-element.48), channel_id=1, source_target_pairs={{0,1},{1,2},{2,3},{3,4},{4,5},{5,6},{6,7},{7,0},{8,9},{9,10},{10,1... | collective-permute-start | bytes 786440 | tf_op jit(solution)/shard_map/ppermute | solution.py:309
  15.7 4.0 %collective-permute-start.5 = (bf16[256,512]{1,0:T(8,128)(2,1)S(1)}, bf16[256,512]{1,0:T(8,128)(2,1)S(1)}, u32[]{:S(2)}, u32[]{:S(2)}) collective-permute-start(bf16[256,512]{1,0:T(8,128)(2,1)S(1)} %get-tuple-element.47), channel_id=1, source_target_pairs={{0,7},{1,0},{2,1},{3,2},{4,3},{5,4},{6,5},{7,6},{8,15},{9,8},{10,9... | collective-permute-start | bytes 786440 | tf_op jit(solution)/shard_map/ppermute | solution.py:310
  19.8 3.4 %copy-done = bf16[1024,4096]{1,0:T(8,128)(2,1)S(1)} copy-done((bf16[1024,4096]{1,0:T(8,128)(2,1)S(1)}, bf16[1024,4096]{1,0:T(8,128)(2,1)}, u32[]{:S(2)}) %copy-start) | copy-done | bytes 8388632
  23.2 2.2 %shares.3.shares_ref = f32[2,512,512]{2,1,0:T(8,128)S(1)} custom-call(s32[2]{0:T(128)S(1)} %compare_select_fusion.2.order_ref, bf16[512,1024]{1,0:T(8,128)(2,1)S(1)} %bitcast.45, bf16[1024,4096]{1,0:T(8,128)(2,1)S(1)} %copy-done), custom_call_target="tpu_custom_call" | custom-call | flops 1073741824 | bytes 4194304 | tf_op jit(solution)/shard_map/shares/pallas_call | solution.py:196
  25.3 0.0 copy-start.5
  25.4 0.0 copy-start.6
  25.4 0.8 collective-permute-done.4.top_ref
  26.2 0.2 first_sums.1
  26.4 0.0 copy-start.9
  26.4 0.1 collective-permute-start.6
  26.5 2.7 %collective-permute-start.7 = (bf16[512,512]{1,0:T(8,128)(2,1)S(1)}, bf16[512,512]{1,0:T(8,128)(2,1)}, u32[]{:S(2)}, u32[]{:S(2)}) collective-permute-start(bf16[512,512]{1,0:T(8,128)(2,1)S(1)} %get-tuple-element.27), channel_id=1, source_target_pairs={{0,7},{1,0},{2,1},{3,2},{4,3},{5,4},{6,5},{7,6},{8,15},{9,8},{10,9... | collective-permute-start | bytes 1572872 | tf_op jit(solution)/shard_map/ppermute | solution.py:320
  29.2 1.0 pack.3
  30.2 1.4 copy-done.3
  31.6 4.6 %shares.5 = f32[5,512,512]{2,1,0:T(8,128)S(1)} custom-call(s32[5]{0:T(128)S(1)} %compare_select_fusion.order_ref, bf16[512,1024]{1,0:T(8,128)(2,1)S(1)} %bitcast.46, bf16[1024,4096]{1,0:T(8,128)(2,1)S(1)} %bitcast.43), custom_call_target="tpu_custom_call" | custom-call | flops 2684354560 | bytes 10485760 | tf_op jit(solution)/shard_map/shares/pallas_call | solution.py:196
  36.2 2.3 %copy-done.2 = f32[5,512,512]{2,1,0:T(8,128)} copy-done((f32[5,512,512]{2,1,0:T(8,128)}, f32[5,512,512]{2,1,0:T(8,128)S(1)}, u32[]{:S(2)}) %copy-start.2) | copy-done | bytes 5242904
  38.5 1.9 %collective-permute-done.6 = bf16[512,512]{1,0:T(8,128)(2,1)S(1)} collective-permute-done((bf16[512,512]{1,0:T(8,128)(2,1)S(1)}, bf16[512,512]{1,0:T(8,128)(2,1)S(1)}, u32[]{:S(2)}, u32[]{:S(2)}) %collective-permute-start.6) | collective-permute-done | bytes 524320 | tf_op jit(solution)/shard_map/ppermute | solution.py:319
  40.4 0.8 copy-done.7
  41.2 0.2 all-to-all-done
  41.5 8.3 %all-to-all-start.1 = ((bf16[32,16,16,128]{3,2,1,0:T(8,128)(2,1)}), bf16[32,16,16,128]{3,2,1,0:T(8,128)(2,1)}, u32[]{:S(2)}, u32[]{:S(2)}) async-start(bf16[32,16,16,128]{3,2,1,0:T(8,128)(2,1)} %copy-done.3), calls=%async_computation.1 | async-start | bytes 4194304 | tf_op jit(solution)/shard_map/all_to_all | solution.py:297
  49.8 0.0 copy-start.8
  49.8 4.5 %shrink.2.a_ref = bf16[16,32,128]{2,1,0:T(8,128)(2,1)S(1)} custom-call(bf16[2,16,17,16,128]{4,3,2,1,0:T(8,128)(2,1)S(1)} %bitcast.47, bf16[2,16,17,16,128]{4,3,2,1,0:T(8,128)(2,1)S(1)} %bitcast.48, bf16[1024,1024]{1,0:T(8,128)(2,1)} %bitcast.60), custom_call_target="tpu_custom_call" | custom-call | flops 2147483648 | bytes 4325376 | tf_op jit(solution)/shard_map/shrink/pallas_call | solution.py:118
  54.3 2.6 %collective-permute-start = (bf16[16,32,128]{2,1,0:T(8,128)(2,1)S(1)}, bf16[16,32,128]{2,1,0:T(8,128)(2,1)S(1)}, u32[]{:S(2)}, u32[]{:S(2)}) collective-permute-start(bf16[16,32,128]{2,1,0:T(8,128)(2,1)S(1)} %shrink.2.a_ref), channel_id=1, source_target_pairs={{1,0},{2,1},{3,2},{4,3},{5,4},{6,5},{7,6},{0,7},{9,8},{10,9},{11,1... | collective-permute-start | bytes 393224 | tf_op jit(solution)/shard_map/ppermute | solution.py:277
  56.9 0.1 convert_reduce_fusion
  57.0 2.3 %collective-permute-done.b_ref = bf16[16,32,128]{2,1,0:T(8,128)(2,1)S(1)} collective-permute-done((bf16[16,32,128]{2,1,0:T(8,128)(2,1)S(1)}, bf16[16,32,128]{2,1,0:T(8,128)(2,1)S(1)}, u32[]{:S(2)}, u32[]{:S(2)}) %collective-permute-start) | collective-permute-done | bytes 131104 | tf_op jit(solution)/shard_map/ppermute | solution.py:277
  59.4 3.2 %collective-permute-done.1.c_ref = bf16[16,32,128]{2,1,0:T(8,128)(2,1)S(1)} collective-permute-done((bf16[16,32,128]{2,1,0:T(8,128)(2,1)S(1)}, bf16[16,32,128]{2,1,0:T(8,128)(2,1)S(1)}, u32[]{:S(2)}, u32[]{:S(2)}) %collective-permute-start.1) | collective-permute-done | bytes 131104 | tf_op jit(solution)/shard_map/ppermute | solution.py:277
  62.6 0.1 fusion.6
  62.6 0.0 copy-start.4
  62.6 1.2 collective-permute-start.2
  63.8 2.1 %collective-permute-start.3 = (bf16[16,32,128]{2,1,0:T(8,128)(2,1)S(1)}, bf16[16,32,128]{2,1,0:T(8,128)(2,1)S(1)}, u32[]{:S(2)}, u32[]{:S(2)}) collective-permute-start(bf16[16,32,128]{2,1,0:T(8,128)(2,1)S(1)} %get-tuple-element.51), channel_id=1, source_target_pairs={{5,0},{6,1},{7,2},{0,3},{1,4},{2,5},{3,6},{4,7},{13,8},{14,9},{15,... | collective-permute-start | bytes 393224 | tf_op jit(solution)/shard_map/ppermute | solution.py:277
  66.0 3.1 %fusion.3 = (bf16[512,512]{1,0:T(8,128)(2,1)}, bf16[512,512]{1,0:T(8,128)(2,1)}) fusion(f32[5,512,512]{2,1,0:T(8,128)} %copy-done.2, bf16[512,512]{1,0:T(8,128)(2,1)} %collective-permute-done.7, bf16[512,512]{1,0:T(8,128)(2,1)S(1)} %copy-done.8), kind=kLoop, calls=%fused_computation.7 | loop fusion | flops 1572864 | bytes 4194304 | tf_op jit(solution)/shard_map/convert_element_type | solution.py:326
  69.0 0.4 collective-permute-start.12
  69.4 2.3 %collective-permute-start.13 = (bf16[512,512]{1,0:T(8,128)(2,1)}, bf16[512,512]{1,0:T(8,128)(2,1)}, u32[]{:S(2)}, u32[]{:S(2)}) collective-permute-start(bf16[512,512]{1,0:T(8,128)(2,1)} %get-tuple-element.41), channel_id=1, source_target_pairs={{0,7},{1,0},{2,1},{3,2},{4,3},{5,4},{6,5},{7,6},{8,15},{9,8},{10,9... | collective-permute-start | bytes 1572872 | tf_op jit(solution)/shard_map/ppermute | solution.py:332
  71.7 3.8 %collective-permute-done.2.d_ref = bf16[16,32,128]{2,1,0:T(8,128)(2,1)S(1)} collective-permute-done((bf16[16,32,128]{2,1,0:T(8,128)(2,1)S(1)}, bf16[16,32,128]{2,1,0:T(8,128)(2,1)S(1)}, u32[]{:S(2)}, u32[]{:S(2)}) %collective-permute-start.2) | collective-permute-done | bytes 131104 | tf_op jit(solution)/shard_map/ppermute | solution.py:277
  75.5 2.7 %expand.2 = bf16[2,16,32,512]{3,2,1,0:T(8,128)(2,1)} custom-call(bf16[2,16,17,16,128]{4,3,2,1,0:T(8,128)(2,1)S(1)} %bitcast.49, bf16[16,32,128]{2,1,0:T(8,128)(2,1)S(1)} %shrink.2.a_ref, bf16[16,32,128]{2,1,0:T(8,128)(2,1)S(1)} %collective-permute-done.b_ref, bf16[16,32,128]{2,1,0:T(8,128)(2,1)S(1)} %collective-permute-done.1.c_ref, ...), custom_call_target="tpu_custom_call" | custom-call | flops 1073741824 | bytes 2752512 | tf_op jit(solution)/shard_map/expand/pallas_call | solution.py:166
  78.2 0.0 all-to-all-done.1
  78.2 4.7 %shrink.3.a_ref = bf16[16,32,128]{2,1,0:T(8,128)(2,1)S(1)} custom-call(bf16[2,16,17,16,128]{4,3,2,1,0:T(8,128)(2,1)S(1)} %bitcast.50, bf16[2,16,16,16,128]{4,3,2,1,0:T(8,128)(2,1)} %bitcast.10.x_ref, bf16[1024,1024]{1,0:T(8,128)(2,1)} %bitcast.61), custom_call_target="tpu_custom_call" | custom-call | flops 2147483648 | bytes 4194304 | tf_op jit(solution)/shard_map/shrink/pallas_call | solution.py:118
  82.9 2.7 %collective-permute-start.8 = (bf16[16,32,128]{2,1,0:T(8,128)(2,1)S(1)}, bf16[16,32,128]{2,1,0:T(8,128)(2,1)S(1)}, u32[]{:S(2)}, u32[]{:S(2)}) collective-permute-start(bf16[16,32,128]{2,1,0:T(8,128)(2,1)S(1)} %shrink.3.a_ref), channel_id=1, source_target_pairs={{1,0},{2,1},{3,2},{4,3},{5,4},{6,5},{7,6},{0,7},{9,8},{10,9},{11,1... | collective-permute-start | bytes 393224 | tf_op jit(solution)/shard_map/ppermute | solution.py:277
  85.5 0.0 collective-permute-start.9
  85.5 10.6 %all-to-all-start.3 = ((bf16[32,32,512]{2,1,0:T(8,128)(2,1)}), bf16[32,32,512]{2,1,0:T(8,128)(2,1)}, u32[]{:S(2)}, u32[]{:S(2)}) async-start(bf16[32,32,512]{2,1,0:T(8,128)(2,1)} %bitcast.56), calls=%async_computation.3 | async-start | bytes 2097152 | tf_op jit(solution)/shard_map/all_to_all | solution.py:297
  96.1 0.1 select_reduce_fusion
  96.3 1.0 fusion.7
  97.2 0.7 collective-permute-start.10
  97.9 2.6 %collective-permute-start.11 = (bf16[16,32,128]{2,1,0:T(8,128)(2,1)S(1)}, bf16[16,32,128]{2,1,0:T(8,128)(2,1)S(1)}, u32[]{:S(2)}, u32[]{:S(2)}) collective-permute-start(bf16[16,32,128]{2,1,0:T(8,128)(2,1)S(1)} %get-tuple-element.49), channel_id=1, source_target_pairs={{5,0},{6,1},{7,2},{0,3},{1,4},{2,5},{3,6},{4,7},{13,8},{14,9},{15,... | collective-permute-start | bytes 393224 | tf_op jit(solution)/shard_map/ppermute | solution.py:277
  100.6 3.2 %fusion.2 = (bf16[512,512]{1,0:T(8,128)(2,1)}, bf16[512,512]{1,0:T(8,128)(2,1)}) fusion(f32[5,512,512]{2,1,0:T(8,128)} %copy-done.2, bf16[512,512]{1,0:T(8,128)(2,1)} %collective-permute-done.13, bf16[512,512]{1,0:T(8,128)(2,1)} %collective-permute-done.12), kind=kLoop, calls=%fused_computation.5 | loop fusion | flops 1572864 | bytes 4194304 | tf_op jit(solution)/shard_map/convert_element_type | solution.py:338
  103.7 5.1 %collective-permute-done.10.d_ref = bf16[16,32,128]{2,1,0:T(8,128)(2,1)S(1)} collective-permute-done((bf16[16,32,128]{2,1,0:T(8,128)(2,1)S(1)}, bf16[16,32,128]{2,1,0:T(8,128)(2,1)S(1)}, u32[]{:S(2)}, u32[]{:S(2)}) %collective-permute-start.10) | collective-permute-done | bytes 131104 | tf_op jit(solution)/shard_map/ppermute | solution.py:277
  108.9 3.2 %collective-permute-done.11.e_ref = bf16[16,32,128]{2,1,0:T(8,128)(2,1)S(1)} collective-permute-done((bf16[16,32,128]{2,1,0:T(8,128)(2,1)S(1)}, bf16[16,32,128]{2,1,0:T(8,128)(2,1)S(1)}, u32[]{:S(2)}, u32[]{:S(2)}) %collective-permute-start.11) | collective-permute-done | bytes 131104 | tf_op jit(solution)/shard_map/ppermute | solution.py:277
  112.0 3.5 %expand.3 = bf16[2,16,32,512]{3,2,1,0:T(8,128)(2,1)} custom-call(bf16[2,16,17,16,128]{4,3,2,1,0:T(8,128)(2,1)S(1)} %bitcast.51, bf16[16,32,128]{2,1,0:T(8,128)(2,1)S(1)} %shrink.3.a_ref, bf16[16,32,128]{2,1,0:T(8,128)(2,1)S(1)} %collective-permute-done.8.b_ref, bf16[16,32,128]{2,1,0:T(8,128)(2,1)} %collective-permute-done.9.c_ref, ...), custom_call_target="tpu_custom_call" | custom-call | flops 1073741824 | bytes 2752512 | tf_op jit(solution)/shard_map/expand/pallas_call | solution.py:166
  115.5 2.7 %collective-permute-start.15 = (bf16[512,512]{1,0:T(8,128)(2,1)}, bf16[512,512]{1,0:T(8,128)(2,1)S(1)}, u32[]{:S(2)}, u32[]{:S(2)}) collective-permute-start(bf16[512,512]{1,0:T(8,128)(2,1)} %get-tuple-element.37), channel_id=1, source_target_pairs={{0,7},{1,0},{2,1},{3,2},{4,3},{5,4},{6,5},{7,6},{8,15},{9,8},{10,9... | collective-permute-start | bytes 1572872 | tf_op jit(solution)/shard_map/ppermute | solution.py:342
  118.2 8.0 %all-to-all-start.2 = ((bf16[32,32,512]{2,1,0:T(8,128)(2,1)}), bf16[32,32,512]{2,1,0:T(8,128)(2,1)S(1)}, u32[]{:S(2)}, u32[]{:S(2)}) async-start(bf16[32,32,512]{2,1,0:T(8,128)(2,1)} %bitcast.57), calls=%async_computation.2 | async-start | bytes 2097152 | tf_op jit(solution)/shard_map/all_to_all | solution.py:297
  126.2 0.2 fusion
  126.5 0.1 slice_bitcast_fusion
  126.5 3.5 %collective-permute-done.14 = bf16[512,512]{1,0:T(8,128)(2,1)S(1)} collective-permute-done((bf16[512,512]{1,0:T(8,128)(2,1)}, bf16[512,512]{1,0:T(8,128)(2,1)S(1)}, u32[]{:S(2)}, u32[]{:S(2)}) %collective-permute-start.14) | collective-permute-done | bytes 524320 | tf_op jit(solution)/shard_map/ppermute | solution.py:341
  130.1 1.4 fusion.1
  131.5 0.1 fusion.10
  131.6 0.8 broadcast_in_dim.23.earlier_ref
  132.4 2.4 %join.2.earlier_ref = bf16[2,256,512]{2,1,0:T(8,128)(2,1)} custom-call(bf16[256,1024]{1,0:T(8,128)(2,1)S(1)} %get-tuple-element.45.spread_ref, bf16[32,32,512]{2,1,0:T(8,128)(2,1)} %all-to-all-done.3.back_ref, f32[256,512]{1,0:T(8,128)S(1)} %get-tuple-element.43.base_ref, ...), custom_call_target="tpu_custom_call", output_to_operand_aliasing={{}: (3, {})} | custom-call | flops 268435456 | bytes 2359296 | tf_op jit(solution)/shard_map/join/pallas_call | solution.py:250
  134.8 8.3 %all-to-all-done.2.back_ref = bf16[32,32,512]{2,1,0:T(8,128)(2,1)S(1)} async-done(((bf16[32,32,512]{2,1,0:T(8,128)(2,1)}), bf16[32,32,512]{2,1,0:T(8,128)(2,1)S(1)}, u32[]{:S(2)}, u32[]{:S(2)}) %all-to-all-start.2) | async-done | bytes 1048608 | tf_op jit(solution)/shard_map/all_to_all | solution.py:297
  143.1 1.2 join.3
  (33 shorter events, 0.1 us)
Async XLA Ops:
  3.1 8.7 %copy-start.1 = (bf16[2,256,1024]{2,1,0:T(8,128)(2,1)S(1)}, bf16[2,256,1024]{2,1,0:T(8,128)(2,1)}, u32[]{:S(2)}) copy-start(bf16[2,256,1024]{2,1,0:T(8,128)(2,1)} %tokens_ref.2) | copy-start | bytes 3145732
  3.1 38.4 %all-to-all-start = ((bf16[32,17,16,128]{3,2,1,0:T(8,128)(2,1)}), bf16[32,17,16,128]{3,2,1,0:T(8,128)(2,1)S(1)}, u32[]{:S(2)}, u32[]{:S(2)}) async-start(bf16[32,17,16,128]{3,2,1,0:T(8,128)(2,1)} %pack.2), calls=%async_computation | async-start | bytes 4456448 | tf_op jit(solution)/shard_map/all_to_all | solution.py:297
  11.8 19.8 %slice-start = ((s8[8388608]{0:T(1024)(128)(4,1)}), s8[4194304]{0:T(1024)(128)(4,1)S(1)}, s32[]{:S(2)}) async-start(s8[8388608]{0:T(1024)(128)(4,1)} %bitcast.42), calls=%async_computation.4 | async-start | bytes 8388608
  13.9 5.9 %copy-start.10 = (s32[2]{0:T(128)S(1)}, s32[2]{0:T(128)}, u32[]{:S(2)}) copy-start(s32[2]{0:T(128)} %constant.33.clone) | copy-start | bytes 28
  14.0 12.2 %collective-permute-start.4 = (bf16[256,512]{1,0:T(8,128)(2,1)S(1)}, bf16[256,512]{1,0:T(8,128)(2,1)S(1)}, u32[]{:S(2)}, u32[]{:S(2)}) collective-permute-start(bf16[256,512]{1,0:T(8,128)(2,1)S(1)} %get-tuple-element.48), channel_id=1, source_target_pairs={{0,1},{1,2},{2,3},{3,4},{4,5},{5,6},{6,7},{7,0},{8,9},{9,10},{10,1... | collective-permute-start | bytes 786440 | tf_op jit(solution)/shard_map/ppermute | solution.py:309
  15.7 10.5 %collective-permute-start.5 = (bf16[256,512]{1,0:T(8,128)(2,1)S(1)}, bf16[256,512]{1,0:T(8,128)(2,1)S(1)}, u32[]{:S(2)}, u32[]{:S(2)}) collective-permute-start(bf16[256,512]{1,0:T(8,128)(2,1)S(1)} %get-tuple-element.47), channel_id=1, source_target_pairs={{0,7},{1,0},{2,1},{3,2},{4,3},{5,4},{6,5},{7,6},{8,15},{9,8},{10,9... | collective-permute-start | bytes 786440 | tf_op jit(solution)/shard_map/ppermute | solution.py:310
  19.8 3.4 %copy-start = (bf16[1024,4096]{1,0:T(8,128)(2,1)S(1)}, bf16[1024,4096]{1,0:T(8,128)(2,1)}, u32[]{:S(2)}) copy-start(bf16[1024,4096]{1,0:T(8,128)(2,1)} %weight_ref.5) | copy-start | bytes 25165828
  23.2 8.4 %slice-start.1 = ((s8[8388608]{0:T(1024)(128)(4,1)}), s8[4194304]{0:T(1024)(128)(4,1)S(1)}, s32[]{:S(2)}) async-start(s8[8388608]{0:T(1024)(128)(4,1)} %bitcast.42), calls=%async_computation.5 | async-start | bytes 8388608
  25.3 3.8 %copy-start.5 = (s32[2,1,256]{2,1,0:T(1,128)S(1)}, s32[2,1,256]{2,1,0:T(1,128)}, u32[]{:S(2)}) copy-start(s32[2,1,256]{2,1,0:T(1,128)} %slots_ref.2) | copy-start | bytes 6148
  25.4 3.8 %copy-start.6 = (s32[2,1,32]{2,1,0:T(1,128)S(1)}, s32[2,1,32]{2,1,0:T(1,128)}, u32[]{:S(2)}) copy-start(s32[2,1,32]{2,1,0:T(1,128)} %param.13) | copy-start | bytes 772
  26.4 5.2 %copy-start.9 = (s32[5]{0:T(128)S(1)}, s32[5]{0:T(128)}, u32[]{:S(2)}) copy-start(s32[5]{0:T(128)} %constant.34.clone) | copy-start | bytes 64
  26.4 14.0 %collective-permute-start.6 = (bf16[512,512]{1,0:T(8,128)(2,1)S(1)}, bf16[512,512]{1,0:T(8,128)(2,1)S(1)}, u32[]{:S(2)}, u32[]{:S(2)}) collective-permute-start(bf16[512,512]{1,0:T(8,128)(2,1)S(1)} %get-tuple-element.26), channel_id=1, source_target_pairs={{0,1},{1,2},{2,3},{3,4},{4,5},{5,6},{6,7},{7,0},{8,9},{9,10},{10,1... | collective-permute-start | bytes 1572872 | tf_op jit(solution)/shard_map/ppermute | solution.py:319
  26.5 14.7 %collective-permute-start.7 = (bf16[512,512]{1,0:T(8,128)(2,1)S(1)}, bf16[512,512]{1,0:T(8,128)(2,1)}, u32[]{:S(2)}, u32[]{:S(2)}) collective-permute-start(bf16[512,512]{1,0:T(8,128)(2,1)S(1)} %get-tuple-element.27), channel_id=1, source_target_pairs={{0,7},{1,0},{2,1},{3,2},{4,3},{5,4},{6,5},{7,6},{8,15},{9,8},{10,9... | collective-permute-start | bytes 1572872 | tf_op jit(solution)/shard_map/ppermute | solution.py:320
  30.2 1.4 copy-start.3
  36.2 2.3 %copy-start.2 = (f32[5,512,512]{2,1,0:T(8,128)}, f32[5,512,512]{2,1,0:T(8,128)S(1)}, u32[]{:S(2)}) copy-start(f32[5,512,512]{2,1,0:T(8,128)S(1)} %shares.5) | copy-start | bytes 15728644
  40.4 0.8 copy-start.7
  41.5 36.7 %all-to-all-start.1 = ((bf16[32,16,16,128]{3,2,1,0:T(8,128)(2,1)}), bf16[32,16,16,128]{3,2,1,0:T(8,128)(2,1)}, u32[]{:S(2)}, u32[]{:S(2)}) async-start(bf16[32,16,16,128]{3,2,1,0:T(8,128)(2,1)} %copy-done.3), calls=%async_computation.1 | async-start | bytes 4194304 | tf_op jit(solution)/shard_map/all_to_all | solution.py:297
  49.8 16.2 %copy-start.8 = (bf16[512,512]{1,0:T(8,128)(2,1)S(1)}, bf16[512,512]{1,0:T(8,128)(2,1)}, u32[]{:S(2)}) copy-start(bf16[512,512]{1,0:T(8,128)(2,1)} %copy-done.7) | copy-start | bytes 1572868
  54.3 5.0 %collective-permute-start = (bf16[16,32,128]{2,1,0:T(8,128)(2,1)S(1)}, bf16[16,32,128]{2,1,0:T(8,128)(2,1)S(1)}, u32[]{:S(2)}, u32[]{:S(2)}) collective-permute-start(bf16[16,32,128]{2,1,0:T(8,128)(2,1)S(1)} %shrink.2.a_ref), channel_id=1, source_target_pairs={{1,0},{2,1},{3,2},{4,3},{5,4},{6,5},{7,6},{0,7},{9,8},{10,9},{11,1... | collective-permute-start | bytes 393224 | tf_op jit(solution)/shard_map/ppermute | solution.py:277
  56.9 5.6 %collective-permute-start.1 = (bf16[16,32,128]{2,1,0:T(8,128)(2,1)S(1)}, bf16[16,32,128]{2,1,0:T(8,128)(2,1)S(1)}, u32[]{:S(2)}, u32[]{:S(2)}) collective-permute-start(bf16[16,32,128]{2,1,0:T(8,128)(2,1)S(1)} %shrink.2.a_ref), channel_id=1, source_target_pairs={{7,0},{0,1},{1,2},{2,3},{3,4},{4,5},{5,6},{6,7},{15,8},{8,9},{9,10... | collective-permute-start | bytes 393224 | tf_op jit(solution)/shard_map/ppermute | solution.py:277
  62.6 12.9 %copy-start.4 = (bf16[16,64,512]{2,1,0:T(8,128)(2,1)S(1)}, bf16[16,64,512]{2,1,0:T(8,128)(2,1)}, u32[]{:S(2)}) copy-start(bf16[16,64,512]{2,1,0:T(8,128)(2,1)} %param.12) | copy-start | bytes 3145732
  62.6 12.8 %collective-permute-start.2 = (bf16[16,32,128]{2,1,0:T(8,128)(2,1)S(1)}, bf16[16,32,128]{2,1,0:T(8,128)(2,1)S(1)}, u32[]{:S(2)}, u32[]{:S(2)}) collective-permute-start(bf16[16,32,128]{2,1,0:T(8,128)(2,1)S(1)} %get-tuple-element.52), channel_id=1, source_target_pairs={{3,0},{4,1},{5,2},{6,3},{7,4},{0,5},{1,6},{2,7},{11,8},{12,9},{13,... | collective-permute-start | bytes 393224 | tf_op jit(solution)/shard_map/ppermute | solution.py:277
  63.8 11.6 %collective-permute-start.3 = (bf16[16,32,128]{2,1,0:T(8,128)(2,1)S(1)}, bf16[16,32,128]{2,1,0:T(8,128)(2,1)S(1)}, u32[]{:S(2)}, u32[]{:S(2)}) collective-permute-start(bf16[16,32,128]{2,1,0:T(8,128)(2,1)S(1)} %get-tuple-element.51), channel_id=1, source_target_pairs={{5,0},{6,1},{7,2},{0,3},{1,4},{2,5},{3,6},{4,7},{13,8},{14,9},{15,... | collective-permute-start | bytes 393224 | tf_op jit(solution)/shard_map/ppermute | solution.py:277
  69.0 31.5 %collective-permute-start.12 = (bf16[512,512]{1,0:T(8,128)(2,1)}, bf16[512,512]{1,0:T(8,128)(2,1)}, u32[]{:S(2)}, u32[]{:S(2)}) collective-permute-start(bf16[512,512]{1,0:T(8,128)(2,1)} %get-tuple-element.42), channel_id=1, source_target_pairs={{0,1},{1,2},{2,3},{3,4},{4,5},{5,6},{6,7},{7,0},{8,9},{9,10},{10,1... | collective-permute-start | bytes 1572872 | tf_op jit(solution)/shard_map/ppermute | solution.py:331
  69.4 31.2 %collective-permute-start.13 = (bf16[512,512]{1,0:T(8,128)(2,1)}, bf16[512,512]{1,0:T(8,128)(2,1)}, u32[]{:S(2)}, u32[]{:S(2)}) collective-permute-start(bf16[512,512]{1,0:T(8,128)(2,1)} %get-tuple-element.41), channel_id=1, source_target_pairs={{0,7},{1,0},{2,1},{3,2},{4,3},{5,4},{6,5},{7,6},{8,15},{9,8},{10,9... | collective-permute-start | bytes 1572872 | tf_op jit(solution)/shard_map/ppermute | solution.py:332
  82.9 13.4 %collective-permute-start.8 = (bf16[16,32,128]{2,1,0:T(8,128)(2,1)S(1)}, bf16[16,32,128]{2,1,0:T(8,128)(2,1)S(1)}, u32[]{:S(2)}, u32[]{:S(2)}) collective-permute-start(bf16[16,32,128]{2,1,0:T(8,128)(2,1)S(1)} %shrink.3.a_ref), channel_id=1, source_target_pairs={{1,0},{2,1},{3,2},{4,3},{5,4},{6,5},{7,6},{0,7},{9,8},{10,9},{11,1... | collective-permute-start | bytes 393224 | tf_op jit(solution)/shard_map/ppermute | solution.py:277
  85.5 10.7 %collective-permute-start.9 = (bf16[16,32,128]{2,1,0:T(8,128)(2,1)S(1)}, bf16[16,32,128]{2,1,0:T(8,128)(2,1)}, u32[]{:S(2)}, u32[]{:S(2)}) collective-permute-start(bf16[16,32,128]{2,1,0:T(8,128)(2,1)S(1)} %shrink.3.a_ref), channel_id=1, source_target_pairs={{7,0},{0,1},{1,2},{2,3},{3,4},{4,5},{5,6},{6,7},{15,8},{8,9},{9,10... | collective-permute-start | bytes 393224 | tf_op jit(solution)/shard_map/ppermute | solution.py:277
  85.5 32.7 %all-to-all-start.3 = ((bf16[32,32,512]{2,1,0:T(8,128)(2,1)}), bf16[32,32,512]{2,1,0:T(8,128)(2,1)}, u32[]{:S(2)}, u32[]{:S(2)}) async-start(bf16[32,32,512]{2,1,0:T(8,128)(2,1)} %bitcast.56), calls=%async_computation.3 | async-start | bytes 2097152 | tf_op jit(solution)/shard_map/all_to_all | solution.py:297
  97.2 11.6 %collective-permute-start.10 = (bf16[16,32,128]{2,1,0:T(8,128)(2,1)S(1)}, bf16[16,32,128]{2,1,0:T(8,128)(2,1)S(1)}, u32[]{:S(2)}, u32[]{:S(2)}) collective-permute-start(bf16[16,32,128]{2,1,0:T(8,128)(2,1)S(1)} %get-tuple-element.50), channel_id=1, source_target_pairs={{3,0},{4,1},{5,2},{6,3},{7,4},{0,5},{1,6},{2,7},{11,8},{12,9},{13,... | collective-permute-start | bytes 393224 | tf_op jit(solution)/shard_map/ppermute | solution.py:277
  97.9 14.1 %collective-permute-start.11 = (bf16[16,32,128]{2,1,0:T(8,128)(2,1)S(1)}, bf16[16,32,128]{2,1,0:T(8,128)(2,1)S(1)}, u32[]{:S(2)}, u32[]{:S(2)}) collective-permute-start(bf16[16,32,128]{2,1,0:T(8,128)(2,1)S(1)} %get-tuple-element.49), channel_id=1, source_target_pairs={{5,0},{6,1},{7,2},{0,3},{1,4},{2,5},{3,6},{4,7},{13,8},{14,9},{15,... | collective-permute-start | bytes 393224 | tf_op jit(solution)/shard_map/ppermute | solution.py:277
  115.5 14.5 %collective-permute-start.14 = (bf16[512,512]{1,0:T(8,128)(2,1)}, bf16[512,512]{1,0:T(8,128)(2,1)S(1)}, u32[]{:S(2)}, u32[]{:S(2)}) collective-permute-start(bf16[512,512]{1,0:T(8,128)(2,1)} %get-tuple-element.36), channel_id=1, source_target_pairs={{0,1},{1,2},{2,3},{3,4},{4,5},{5,6},{6,7},{7,0},{8,9},{9,10},{10,1... | collective-permute-start | bytes 1572872 | tf_op jit(solution)/shard_map/ppermute | solution.py:341
  115.5 14.5 %collective-permute-start.15 = (bf16[512,512]{1,0:T(8,128)(2,1)}, bf16[512,512]{1,0:T(8,128)(2,1)S(1)}, u32[]{:S(2)}, u32[]{:S(2)}) collective-permute-start(bf16[512,512]{1,0:T(8,128)(2,1)} %get-tuple-element.37), channel_id=1, source_target_pairs={{0,7},{1,0},{2,1},{3,2},{4,3},{5,4},{6,5},{7,6},{8,15},{9,8},{10,9... | collective-permute-start | bytes 1572872 | tf_op jit(solution)/shard_map/ppermute | solution.py:342
  118.2 24.9 %all-to-all-start.2 = ((bf16[32,32,512]{2,1,0:T(8,128)(2,1)}), bf16[32,32,512]{2,1,0:T(8,128)(2,1)S(1)}, u32[]{:S(2)}, u32[]{:S(2)}) async-start(bf16[32,32,512]{2,1,0:T(8,128)(2,1)} %bitcast.57), calls=%async_computation.2 | async-start | bytes 2097152 | tf_op jit(solution)/shard_map/all_to_all | solution.py:297

commit v7 on v6

--- a/solution.py
+++ b/solution.py
@@ -269,7 +269,7 @@
     )(spread, back, base, earlier)
 
 
-def parts_over_tp(value):
+def parts_over_tp(value, early):
     size = lax.axis_size("tp")
     assert size == 8
 
@@ -277,9 +277,11 @@
         return lax.ppermute(value, "tp", [((i + ahead) % size, i) for i in range(size)])
 
     after, before = fetch(value, 1), fetch(value, -1)
-    two = value.astype(F32) + after.astype(F32)
-    three = two + before.astype(F32)
-    return value, after, before, fetch(three.astype(BF16), 3), fetch(two.astype(BF16), -3)
+    two = (value.astype(F32) + after.astype(F32)).astype(BF16)
+    if early:
+        value, after, two = lax.optimization_barrier((value, after, two))
+    three = value.astype(F32) + after.astype(F32) + before.astype(F32)
+    return value, after, before, fetch(three.astype(BF16), 3), fetch(two, -3)
 
 
 def body(tokens, query_weight, down_weight, up_weight, requests, row_slot_index):
@@ -327,13 +329,13 @@
 
     up = up_weight.reshape(adapters * rank, features)
     back = []
-    delta = expand_rows(0, names, parts_over_tp(shrunk), up, rank)
+    delta = expand_rows(0, names, parts_over_tp(shrunk, True), up, rank)
     going_right = lax.ppermute(going_right, "tp", right)
     going_left = lax.ppermute(going_left, "tp", left)
     shrunk = shrink_rows(1, names, x[1], down, most, rank)
     delta, shrunk = lax.optimization_barrier((delta, shrunk))
     back.append(swap(delta))
-    delta = expand_rows(1, names, parts_over_tp(shrunk), up, rank)
+    delta = expand_rows(1, names, parts_over_tp(shrunk, False), up, rank)
     going_right = (going_right.astype(F32) + shares[2]).astype(BF16)
     going_left = (going_left.astype(F32) + shares[3]).astype(BF16)
     delta, going_right, going_left = lax.optimization_barrier((delta, going_right, going_left))

time: 145 us -> 144 us (level)
  waiting for transfers between devices: 32.5 us -> 30.8 us
    ppermute x8, waiting for transfers between devices: 17.6 us -> 15.9 us  [fetch(): lax.ppermute(value, 'tp', [((i + ahead) % size, i) for i in range(size)])]
where the time goes in v7:
time: 144 us; the launch traced here: 143 us
  starting transfers between devices  62.1 us (43%)
  Pallas kernels  31.9 us (22%)
  waiting for transfers between devices  30.8 us (21%)
  other arithmetic  9.27 us (6%)
  local copies, waits for them, and re-layouts  8.94 us (6%)
    all_to_all x4, starting transfers between devices, swap(): lax.all_to_all(value, 'pool', split_axis=0, concat_axis=0, tiled=True)  36.2 us
    ppermute x8, waiting for transfers between devices, fetch(): lax.ppermute(value, 'tp', [((i + ahead) % size, i) for i in range(size)])  15.9 us
    ppermute x8, starting transfers between devices, fetch(): lax.ppermute(value, 'tp', [((i + ahead) % size, i) for i in range(size)])  12 us
    pallas_call x2, Pallas kernels, shrink_rows(): pl.pallas_call(functools.partial(shrink_kernel, step, rank), out_shape=ja...  9.17 us
    all_to_all x4, waiting for transfers between devices, swap(): lax.all_to_all(value, 'pool', split_axis=0, concat_axis=0, tiled=True)  9.04 us
    pallas_call x3, Pallas kernels, base_shares(): pl.pallas_call(shares_kernel, out_shape=jax.ShapeDtypeStruct((amount, row...  8.8 us
    unnamed x27, local copies, waits for them, and re-layouts  7.93 us
    pallas_call x2, Pallas kernels, expand_rows(): pl.pallas_call(functools.partial(expand_kernel, step, rank), out_shape=pl...  6.2 us
  transfers between devices with their start and end apart: 20, of which 10 were waited for; matrix products, arithmetic and copies ran while one was open for 7% of the time, Pallas kernels for 19%

profile of v7, /device:TPU:1, one launch (start us, length us, event | category | flops | bytes accessed | tf_op | source)
XLA Modules:
  0.0 143.3 jit_solution(4890405410477970703)
XLA Ops:
  0.0 3.1 %pack.2 = bf16[32,17,16,128]{3,2,1,0:T(8,128)(2,1)} custom-call(s32[2,32]{1,0:T(2,128)} %bitcast.54, s32[2,1,256]{2,1,0:T(1,128)} %slots_ref.2, bf16[2,256,1024]{2,1,0:T(8,128)(2,1)} %tokens_ref.2), custom_call_target="tpu_custom_call" | custom-call | flops 536870912 | bytes 2752512 | tf_op jit(solution)/shard_map/pack/pallas_call | solution.py:55
  3.1 8.7 %all-to-all-start = ((bf16[32,17,16,128]{3,2,1,0:T(8,128)(2,1)}), bf16[32,17,16,128]{3,2,1,0:T(8,128)(2,1)S(1)}, u32[]{:S(2)}, u32[]{:S(2)}) async-start(bf16[32,17,16,128]{3,2,1,0:T(8,128)(2,1)} %pack.2), calls=%async_computation | async-start | bytes 4456448 | tf_op jit(solution)/shard_map/all_to_all | solution.py:299
  11.8 0.0 slice-start
  11.8 2.1 %shares.4 = f32[1,512,512]{2,1,0:T(8,128)S(1)} custom-call(s32[1]{0:T(128)S(6)} %rem.55.order_ref, bf16[512,1024]{1,0:T(8,128)(2,1)S(1)} %bitcast.44, bf16[1024,4096]{1,0:T(8,128)(2,1)} %weight_ref.5), custom_call_target="tpu_custom_call" | custom-call | flops 536870912 | bytes 2097152 | tf_op jit(solution)/shard_map/shares/pallas_call | solution.py:196
  13.9 0.0 copy-start.10
  13.9 0.1 convert_element_type.87
  14.0 1.7 %collective-permute-start.4 = (bf16[256,512]{1,0:T(8,128)(2,1)S(1)}, bf16[256,512]{1,0:T(8,128)(2,1)S(1)}, u32[]{:S(2)}, u32[]{:S(2)}) collective-permute-start(bf16[256,512]{1,0:T(8,128)(2,1)S(1)} %get-tuple-element.54), channel_id=1, source_target_pairs={{0,1},{1,2},{2,3},{3,4},{4,5},{5,6},{6,7},{7,0},{8,9},{9,10},{10,1... | collective-permute-start | bytes 786440 | tf_op jit(solution)/shard_map/ppermute | solution.py:311
  15.7 4.0 %collective-permute-start.5 = (bf16[256,512]{1,0:T(8,128)(2,1)S(1)}, bf16[256,512]{1,0:T(8,128)(2,1)S(1)}, u32[]{:S(2)}, u32[]{:S(2)}) collective-permute-start(bf16[256,512]{1,0:T(8,128)(2,1)S(1)} %get-tuple-element.53), channel_id=1, source_target_pairs={{0,7},{1,0},{2,1},{3,2},{4,3},{5,4},{6,5},{7,6},{8,15},{9,8},{10,9... | collective-permute-start | bytes 786440 | tf_op jit(solution)/shard_map/ppermute | solution.py:312
  19.8 3.4 %copy-done = bf16[1024,4096]{1,0:T(8,128)(2,1)S(1)} copy-done((bf16[1024,4096]{1,0:T(8,128)(2,1)S(1)}, bf16[1024,4096]{1,0:T(8,128)(2,1)}, u32[]{:S(2)}) %copy-start) | copy-done | bytes 8388632
  23.2 2.2 %shares.3.shares_ref = f32[2,512,512]{2,1,0:T(8,128)S(1)} custom-call(s32[2]{0:T(128)S(1)} %compare_select_fusion.2.order_ref, bf16[512,1024]{1,0:T(8,128)(2,1)S(1)} %bitcast.45, bf16[1024,4096]{1,0:T(8,128)(2,1)S(1)} %copy-done), custom_call_target="tpu_custom_call" | custom-call | flops 1073741824 | bytes 4194304 | tf_op jit(solution)/shard_map/shares/pallas_call | solution.py:196
  25.4 0.0 copy-start.5
  25.4 0.0 copy-start.6
  25.4 0.8 collective-permute-done.4.top_ref
  26.2 0.2 first_sums.1
  26.4 0.0 copy-start.9
  26.4 0.1 collective-permute-start.6
  26.5 2.7 %collective-permute-start.7 = (bf16[512,512]{1,0:T(8,128)(2,1)S(1)}, bf16[512,512]{1,0:T(8,128)(2,1)}, u32[]{:S(2)}, u32[]{:S(2)}) collective-permute-start(bf16[512,512]{1,0:T(8,128)(2,1)S(1)} %get-tuple-element.33), channel_id=1, source_target_pairs={{0,7},{1,0},{2,1},{3,2},{4,3},{5,4},{6,5},{7,6},{8,15},{9,8},{10,9... | collective-permute-start | bytes 1572872 | tf_op jit(solution)/shard_map/ppermute | solution.py:322
  29.2 1.0 pack.3
  30.2 1.4 copy-done.3
  31.6 4.6 %shares.5 = f32[5,512,512]{2,1,0:T(8,128)S(1)} custom-call(s32[5]{0:T(128)S(1)} %compare_select_fusion.order_ref, bf16[512,1024]{1,0:T(8,128)(2,1)S(1)} %bitcast.46, bf16[1024,4096]{1,0:T(8,128)(2,1)S(1)} %bitcast.43), custom_call_target="tpu_custom_call" | custom-call | flops 2684354560 | bytes 10485760 | tf_op jit(solution)/shard_map/shares/pallas_call | solution.py:196
  36.2 2.3 %copy-done.2 = f32[5,512,512]{2,1,0:T(8,128)} copy-done((f32[5,512,512]{2,1,0:T(8,128)}, f32[5,512,512]{2,1,0:T(8,128)S(1)}, u32[]{:S(2)}) %copy-start.2) | copy-done | bytes 5242904
  38.5 1.9 %collective-permute-done.6 = bf16[512,512]{1,0:T(8,128)(2,1)S(1)} collective-permute-done((bf16[512,512]{1,0:T(8,128)(2,1)S(1)}, bf16[512,512]{1,0:T(8,128)(2,1)S(1)}, u32[]{:S(2)}, u32[]{:S(2)}) %collective-permute-start.6) | collective-permute-done | bytes 524320 | tf_op jit(solution)/shard_map/ppermute | solution.py:321
  40.5 0.8 copy-done.7
  41.2 0.3 all-to-all-done
  41.5 8.3 %all-to-all-start.1 = ((bf16[32,16,16,128]{3,2,1,0:T(8,128)(2,1)}), bf16[32,16,16,128]{3,2,1,0:T(8,128)(2,1)}, u32[]{:S(2)}, u32[]{:S(2)}) async-start(bf16[32,16,16,128]{3,2,1,0:T(8,128)(2,1)} %copy-done.3), calls=%async_computation.1 | async-start | bytes 4194304 | tf_op jit(solution)/shard_map/all_to_all | solution.py:299
  49.8 0.0 copy-start.8
  49.8 4.5 %shrink.2.a_ref = bf16[16,32,128]{2,1,0:T(8,128)(2,1)S(1)} custom-call(bf16[2,16,17,16,128]{4,3,2,1,0:T(8,128)(2,1)S(1)} %bitcast.47, bf16[2,16,17,16,128]{4,3,2,1,0:T(8,128)(2,1)S(1)} %bitcast.48, bf16[1024,1024]{1,0:T(8,128)(2,1)} %bitcast.60), custom_call_target="tpu_custom_call" | custom-call | flops 2147483648 | bytes 4325376 | tf_op jit(solution)/shard_map/shrink/pallas_call | solution.py:118
  54.3 2.6 %collective-permute-start = (bf16[16,32,128]{2,1,0:T(8,128)(2,1)S(1)}, bf16[16,32,128]{2,1,0:T(8,128)(2,1)S(1)}, u32[]{:S(2)}, u32[]{:S(2)}) collective-permute-start(bf16[16,32,128]{2,1,0:T(8,128)(2,1)S(1)} %shrink.2.a_ref), channel_id=1, source_target_pairs={{1,0},{2,1},{3,2},{4,3},{5,4},{6,5},{7,6},{0,7},{9,8},{10,9},{11,1... | collective-permute-start | bytes 393224 | tf_op jit(solution)/shard_map/ppermute | solution.py:277
  56.9 0.1 convert_reduce_fusion
  57.0 0.1 collective-permute-start.1
  57.1 2.2 %collective-permute-done.b_ref = bf16[16,32,128]{2,1,0:T(8,128)(2,1)S(1)} collective-permute-done((bf16[16,32,128]{2,1,0:T(8,128)(2,1)S(1)}, bf16[16,32,128]{2,1,0:T(8,128)(2,1)S(1)}, u32[]{:S(2)}, u32[]{:S(2)}) %collective-permute-start) | collective-permute-done | bytes 131104 | tf_op jit(solution)/shard_map/ppermute | solution.py:277
  59.4 3.4 %collective-permute-done.1.c_ref = bf16[16,32,128]{2,1,0:T(8,128)(2,1)S(1)} collective-permute-done((bf16[16,32,128]{2,1,0:T(8,128)(2,1)S(1)}, bf16[16,32,128]{2,1,0:T(8,128)(2,1)S(1)}, u32[]{:S(2)}, u32[]{:S(2)}) %collective-permute-start.1) | collective-permute-done | bytes 131104 | tf_op jit(solution)/shard_map/ppermute | solution.py:277
  62.8 0.1 add_convert_fusion.1
  62.8 0.0 copy-start.4
  62.8 1.2 collective-permute-start.2
  64.1 2.1 %collective-permute-start.3 = (bf16[16,32,128]{2,1,0:T(8,128)(2,1)S(1)}, bf16[16,32,128]{2,1,0:T(8,128)(2,1)S(1)}, u32[]{:S(2)}, u32[]{:S(2)}) collective-permute-start(bf16[16,32,128]{2,1,0:T(8,128)(2,1)S(1)} %add_convert_fusion.2), channel_id=1, source_target_pairs={{5,0},{6,1},{7,2},{0,3},{1,4},{2,5},{3,6},{4,7},{13,8},{14,9},{15,... | collective-permute-start | bytes 393224 | tf_op jit(solution)/shard_map/ppermute | solution.py:277
  66.2 3.1 %fusion.3 = (bf16[512,512]{1,0:T(8,128)(2,1)}, bf16[512,512]{1,0:T(8,128)(2,1)}) fusion(f32[5,512,512]{2,1,0:T(8,128)} %copy-done.2, bf16[512,512]{1,0:T(8,128)(2,1)} %collective-permute-done.7, bf16[512,512]{1,0:T(8,128)(2,1)S(1)} %copy-done.8), kind=kLoop, calls=%fused_computation.7 | loop fusion | flops 1572864 | bytes 4194304 | tf_op jit(solution)/shard_map/convert_element_type | solution.py:328
  69.3 0.4 collective-permute-start.12
  69.6 2.3 %collective-permute-start.13 = (bf16[512,512]{1,0:T(8,128)(2,1)}, bf16[512,512]{1,0:T(8,128)(2,1)}, u32[]{:S(2)}, u32[]{:S(2)}) collective-permute-start(bf16[512,512]{1,0:T(8,128)(2,1)} %get-tuple-element.47), channel_id=1, source_target_pairs={{0,7},{1,0},{2,1},{3,2},{4,3},{5,4},{6,5},{7,6},{8,15},{9,8},{10,9... | collective-permute-start | bytes 1572872 | tf_op jit(solution)/shard_map/ppermute | solution.py:334
  71.9 3.6 %collective-permute-done.2.d_ref = bf16[16,32,128]{2,1,0:T(8,128)(2,1)S(1)} collective-permute-done((bf16[16,32,128]{2,1,0:T(8,128)(2,1)S(1)}, bf16[16,32,128]{2,1,0:T(8,128)(2,1)S(1)}, u32[]{:S(2)}, u32[]{:S(2)}) %collective-permute-start.2) | collective-permute-done | bytes 131104 | tf_op jit(solution)/shard_map/ppermute | solution.py:277
  75.5 2.7 %expand.2 = bf16[2,16,32,512]{3,2,1,0:T(8,128)(2,1)} custom-call(bf16[2,16,17,16,128]{4,3,2,1,0:T(8,128)(2,1)S(1)} %bitcast.49, bf16[16,32,128]{2,1,0:T(8,128)(2,1)S(1)} %shrink.2.a_ref, bf16[16,32,128]{2,1,0:T(8,128)(2,1)S(1)} %collective-permute-done.b_ref, bf16[16,32,128]{2,1,0:T(8,128)(2,1)S(1)} %collective-permute-done.1.c_ref, ...), custom_call_target="tpu_custom_call" | custom-call | flops 1073741824 | bytes 2752512 | tf_op jit(solution)/shard_map/expand/pallas_call | solution.py:166
  78.2 4.7 %shrink.3.a_ref = bf16[16,32,128]{2,1,0:T(8,128)(2,1)S(1)} custom-call(bf16[2,16,17,16,128]{4,3,2,1,0:T(8,128)(2,1)S(1)} %bitcast.50, bf16[2,16,16,16,128]{4,3,2,1,0:T(8,128)(2,1)} %bitcast.10.x_ref, bf16[1024,1024]{1,0:T(8,128)(2,1)} %bitcast.61), custom_call_target="tpu_custom_call" | custom-call | flops 2147483648 | bytes 4194304 | tf_op jit(solution)/shard_map/shrink/pallas_call | solution.py:118
  82.9 2.6 %collective-permute-start.8 = (bf16[16,32,128]{2,1,0:T(8,128)(2,1)S(1)}, bf16[16,32,128]{2,1,0:T(8,128)(2,1)S(1)}, u32[]{:S(2)}, u32[]{:S(2)}) collective-permute-start(bf16[16,32,128]{2,1,0:T(8,128)(2,1)S(1)} %shrink.3.a_ref), channel_id=1, source_target_pairs={{1,0},{2,1},{3,2},{4,3},{5,4},{6,5},{7,6},{0,7},{9,8},{10,9},{11,1... | collective-permute-start | bytes 393224 | tf_op jit(solution)/shard_map/ppermute | solution.py:277
  85.5 11.0 %all-to-all-start.3 = ((bf16[32,32,512]{2,1,0:T(8,128)(2,1)}), bf16[32,32,512]{2,1,0:T(8,128)(2,1)}, u32[]{:S(2)}, u32[]{:S(2)}) async-start(bf16[32,32,512]{2,1,0:T(8,128)(2,1)} %bitcast.56), calls=%async_computation.3 | async-start | bytes 2097152 | tf_op jit(solution)/shard_map/all_to_all | solution.py:299
  96.6 0.1 select_reduce_fusion
  96.7 1.0 fusion.6
  97.7 0.3 collective-permute-start.10
  98.0 3.0 %collective-permute-start.11 = (bf16[16,32,128]{2,1,0:T(8,128)(2,1)S(1)}, bf16[16,32,128]{2,1,0:T(8,128)(2,1)S(1)}, u32[]{:S(2)}, u32[]{:S(2)}) collective-permute-start(bf16[16,32,128]{2,1,0:T(8,128)(2,1)S(1)} %get-tuple-element.55), channel_id=1, source_target_pairs={{5,0},{6,1},{7,2},{0,3},{1,4},{2,5},{3,6},{4,7},{13,8},{14,9},{15,... | collective-permute-start | bytes 393224 | tf_op jit(solution)/shard_map/ppermute | solution.py:277
  101.0 3.2 %fusion.2 = (bf16[512,512]{1,0:T(8,128)(2,1)}, bf16[512,512]{1,0:T(8,128)(2,1)}) fusion(f32[5,512,512]{2,1,0:T(8,128)} %copy-done.2, bf16[512,512]{1,0:T(8,128)(2,1)} %collective-permute-done.13, bf16[512,512]{1,0:T(8,128)(2,1)} %collective-permute-done.12), kind=kLoop, calls=%fused_computation.5 | loop fusion | flops 1572864 | bytes 4194304 | tf_op jit(solution)/shard_map/convert_element_type | solution.py:340
  104.2 4.9 %collective-permute-done.10.d_ref = bf16[16,32,128]{2,1,0:T(8,128)(2,1)S(1)} collective-permute-done((bf16[16,32,128]{2,1,0:T(8,128)(2,1)S(1)}, bf16[16,32,128]{2,1,0:T(8,128)(2,1)S(1)}, u32[]{:S(2)}, u32[]{:S(2)}) %collective-permute-start.10) | collective-permute-done | bytes 131104 | tf_op jit(solution)/shard_map/ppermute | solution.py:277
  109.1 1.7 %collective-permute-done.11.e_ref = bf16[16,32,128]{2,1,0:T(8,128)(2,1)S(1)} collective-permute-done((bf16[16,32,128]{2,1,0:T(8,128)(2,1)S(1)}, bf16[16,32,128]{2,1,0:T(8,128)(2,1)S(1)}, u32[]{:S(2)}, u32[]{:S(2)}) %collective-permute-start.11) | collective-permute-done | bytes 131104 | tf_op jit(solution)/shard_map/ppermute | solution.py:277
  110.9 3.5 %expand.3 = bf16[2,16,32,512]{3,2,1,0:T(8,128)(2,1)} custom-call(bf16[2,16,17,16,128]{4,3,2,1,0:T(8,128)(2,1)S(1)} %bitcast.51, bf16[16,32,128]{2,1,0:T(8,128)(2,1)S(1)} %shrink.3.a_ref, bf16[16,32,128]{2,1,0:T(8,128)(2,1)S(1)} %collective-permute-done.8.b_ref, bf16[16,32,128]{2,1,0:T(8,128)(2,1)} %collective-permute-done.9.c_ref, ...), custom_call_target="tpu_custom_call" | custom-call | flops 1073741824 | bytes 2752512 | tf_op jit(solution)/shard_map/expand/pallas_call | solution.py:166
  114.4 0.2 collective-permute-start.14
  114.6 2.5 %collective-permute-start.15 = (bf16[512,512]{1,0:T(8,128)(2,1)}, bf16[512,512]{1,0:T(8,128)(2,1)S(1)}, u32[]{:S(2)}, u32[]{:S(2)}) collective-permute-start(bf16[512,512]{1,0:T(8,128)(2,1)} %get-tuple-element.43), channel_id=1, source_target_pairs={{0,7},{1,0},{2,1},{3,2},{4,3},{5,4},{6,5},{7,6},{8,15},{9,8},{10,9... | collective-permute-start | bytes 1572872 | tf_op jit(solution)/shard_map/ppermute | solution.py:344
  117.1 8.2 %all-to-all-start.2 = ((bf16[32,32,512]{2,1,0:T(8,128)(2,1)}), bf16[32,32,512]{2,1,0:T(8,128)(2,1)S(1)}, u32[]{:S(2)}, u32[]{:S(2)}) async-start(bf16[32,32,512]{2,1,0:T(8,128)(2,1)} %bitcast.57), calls=%async_computation.2 | async-start | bytes 2097152 | tf_op jit(solution)/shard_map/all_to_all | solution.py:299
  125.3 0.2 fusion
  125.5 0.1 slice_bitcast_fusion
  125.6 3.1 %collective-permute-done.14 = bf16[512,512]{1,0:T(8,128)(2,1)S(1)} collective-permute-done((bf16[512,512]{1,0:T(8,128)(2,1)}, bf16[512,512]{1,0:T(8,128)(2,1)S(1)}, u32[]{:S(2)}, u32[]{:S(2)}) %collective-permute-start.14) | collective-permute-done | bytes 524320 | tf_op jit(solution)/shard_map/ppermute | solution.py:343
  128.7 1.4 fusion.1
  130.1 0.1 fusion.9
  130.2 0.8 broadcast_in_dim.23.earlier_ref
  131.0 2.4 %join.2.earlier_ref = bf16[2,256,512]{2,1,0:T(8,128)(2,1)} custom-call(bf16[256,1024]{1,0:T(8,128)(2,1)S(1)} %get-tuple-element.51.spread_ref, bf16[32,32,512]{2,1,0:T(8,128)(2,1)} %all-to-all-done.3.back_ref, f32[256,512]{1,0:T(8,128)S(1)} %get-tuple-element.49.base_ref, ...), custom_call_target="tpu_custom_call", output_to_operand_aliasing={{}: (3, {})} | custom-call | flops 268435456 | bytes 2359296 | tf_op jit(solution)/shard_map/join/pallas_call | solution.py:250
  133.4 8.8 %all-to-all-done.2.back_ref = bf16[32,32,512]{2,1,0:T(8,128)(2,1)S(1)} async-done(((bf16[32,32,512]{2,1,0:T(8,128)(2,1)}), bf16[32,32,512]{2,1,0:T(8,128)(2,1)S(1)}, u32[]{:S(2)}, u32[]{:S(2)}) %all-to-all-start.2) | async-done | bytes 1048608 | tf_op jit(solution)/shard_map/all_to_all | solution.py:299
  142.2 1.2 join.3
  (34 shorter events, 0.2 us)
Async XLA Ops:
  3.1 8.7 %copy-start.1 = (bf16[2,256,1024]{2,1,0:T(8,128)(2,1)S(1)}, bf16[2,256,1024]{2,1,0:T(8,128)(2,1)}, u32[]{:S(2)}) copy-start(bf16[2,256,1024]{2,1,0:T(8,128)(2,1)} %tokens_ref.2) | copy-start | bytes 3145732
  3.1 38.4 %all-to-all-start = ((bf16[32,17,16,128]{3,2,1,0:T(8,128)(2,1)}), bf16[32,17,16,128]{3,2,1,0:T(8,128)(2,1)S(1)}, u32[]{:S(2)}, u32[]{:S(2)}) async-start(bf16[32,17,16,128]{3,2,1,0:T(8,128)(2,1)} %pack.2), calls=%async_computation | async-start | bytes 4456448 | tf_op jit(solution)/shard_map/all_to_all | solution.py:299
  11.8 19.8 %slice-start = ((s8[8388608]{0:T(1024)(128)(4,1)}), s8[4194304]{0:T(1024)(128)(4,1)S(1)}, s32[]{:S(2)}) async-start(s8[8388608]{0:T(1024)(128)(4,1)} %bitcast.42), calls=%async_computation.4 | async-start | bytes 8388608
  13.9 5.9 %copy-start.10 = (s32[2]{0:T(128)S(1)}, s32[2]{0:T(128)}, u32[]{:S(2)}) copy-start(s32[2]{0:T(128)} %constant.33.clone) | copy-start | bytes 28
  14.0 12.2 %collective-permute-start.4 = (bf16[256,512]{1,0:T(8,128)(2,1)S(1)}, bf16[256,512]{1,0:T(8,128)(2,1)S(1)}, u32[]{:S(2)}, u32[]{:S(2)}) collective-permute-start(bf16[256,512]{1,0:T(8,128)(2,1)S(1)} %get-tuple-element.54), channel_id=1, source_target_pairs={{0,1},{1,2},{2,3},{3,4},{4,5},{5,6},{6,7},{7,0},{8,9},{9,10},{10,1... | collective-permute-start | bytes 786440 | tf_op jit(solution)/shard_map/ppermute | solution.py:311
  15.7 10.5 %collective-permute-start.5 = (bf16[256,512]{1,0:T(8,128)(2,1)S(1)}, bf16[256,512]{1,0:T(8,128)(2,1)S(1)}, u32[]{:S(2)}, u32[]{:S(2)}) collective-permute-start(bf16[256,512]{1,0:T(8,128)(2,1)S(1)} %get-tuple-element.53), channel_id=1, source_target_pairs={{0,7},{1,0},{2,1},{3,2},{4,3},{5,4},{6,5},{7,6},{8,15},{9,8},{10,9... | collective-permute-start | bytes 786440 | tf_op jit(solution)/shard_map/ppermute | solution.py:312
  19.8 3.4 %copy-start = (bf16[1024,4096]{1,0:T(8,128)(2,1)S(1)}, bf16[1024,4096]{1,0:T(8,128)(2,1)}, u32[]{:S(2)}) copy-start(bf16[1024,4096]{1,0:T(8,128)(2,1)} %weight_ref.5) | copy-start | bytes 25165828
  23.2 8.4 %slice-start.1 = ((s8[8388608]{0:T(1024)(128)(4,1)}), s8[4194304]{0:T(1024)(128)(4,1)S(1)}, s32[]{:S(2)}) async-start(s8[8388608]{0:T(1024)(128)(4,1)} %bitcast.42), calls=%async_computation.5 | async-start | bytes 8388608
  25.4 3.8 %copy-start.5 = (s32[2,1,256]{2,1,0:T(1,128)S(1)}, s32[2,1,256]{2,1,0:T(1,128)}, u32[]{:S(2)}) copy-start(s32[2,1,256]{2,1,0:T(1,128)} %slots_ref.2) | copy-start | bytes 6148
  25.4 3.8 %copy-start.6 = (s32[2,1,32]{2,1,0:T(1,128)S(1)}, s32[2,1,32]{2,1,0:T(1,128)}, u32[]{:S(2)}) copy-start(s32[2,1,32]{2,1,0:T(1,128)} %param.13) | copy-start | bytes 772
  26.4 5.2 %copy-start.9 = (s32[5]{0:T(128)S(1)}, s32[5]{0:T(128)}, u32[]{:S(2)}) copy-start(s32[5]{0:T(128)} %constant.34.clone) | copy-start | bytes 64
  26.4 14.0 %collective-permute-start.6 = (bf16[512,512]{1,0:T(8,128)(2,1)S(1)}, bf16[512,512]{1,0:T(8,128)(2,1)S(1)}, u32[]{:S(2)}, u32[]{:S(2)}) collective-permute-start(bf16[512,512]{1,0:T(8,128)(2,1)S(1)} %get-tuple-element.32), channel_id=1, source_target_pairs={{0,1},{1,2},{2,3},{3,4},{4,5},{5,6},{6,7},{7,0},{8,9},{9,10},{10,1... | collective-permute-start | bytes 1572872 | tf_op jit(solution)/shard_map/ppermute | solution.py:321
  26.5 14.7 %collective-permute-start.7 = (bf16[512,512]{1,0:T(8,128)(2,1)S(1)}, bf16[512,512]{1,0:T(8,128)(2,1)}, u32[]{:S(2)}, u32[]{:S(2)}) collective-permute-start(bf16[512,512]{1,0:T(8,128)(2,1)S(1)} %get-tuple-element.33), channel_id=1, source_target_pairs={{0,7},{1,0},{2,1},{3,2},{4,3},{5,4},{6,5},{7,6},{8,15},{9,8},{10,9... | collective-permute-start | bytes 1572872 | tf_op jit(solution)/shard_map/ppermute | solution.py:322
  30.2 1.4 copy-start.3
  36.2 2.3 %copy-start.2 = (f32[5,512,512]{2,1,0:T(8,128)}, f32[5,512,512]{2,1,0:T(8,128)S(1)}, u32[]{:S(2)}) copy-start(f32[5,512,512]{2,1,0:T(8,128)S(1)} %shares.5) | copy-start | bytes 15728644
  40.4 0.8 copy-start.7
  41.5 36.7 %all-to-all-start.1 = ((bf16[32,16,16,128]{3,2,1,0:T(8,128)(2,1)}), bf16[32,16,16,128]{3,2,1,0:T(8,128)(2,1)}, u32[]{:S(2)}, u32[]{:S(2)}) async-start(bf16[32,16,16,128]{3,2,1,0:T(8,128)(2,1)} %copy-done.3), calls=%async_computation.1 | async-start | bytes 4194304 | tf_op jit(solution)/shard_map/all_to_all | solution.py:299
  49.8 16.4 %copy-start.8 = (bf16[512,512]{1,0:T(8,128)(2,1)S(1)}, bf16[512,512]{1,0:T(8,128)(2,1)}, u32[]{:S(2)}) copy-start(bf16[512,512]{1,0:T(8,128)(2,1)} %copy-done.7) | copy-start | bytes 1572868
  54.3 5.1 %collective-permute-start = (bf16[16,32,128]{2,1,0:T(8,128)(2,1)S(1)}, bf16[16,32,128]{2,1,0:T(8,128)(2,1)S(1)}, u32[]{:S(2)}, u32[]{:S(2)}) collective-permute-start(bf16[16,32,128]{2,1,0:T(8,128)(2,1)S(1)} %shrink.2.a_ref), channel_id=1, source_target_pairs={{1,0},{2,1},{3,2},{4,3},{5,4},{6,5},{7,6},{0,7},{9,8},{10,9},{11,1... | collective-permute-start | bytes 393224 | tf_op jit(solution)/shard_map/ppermute | solution.py:277
  57.0 5.7 %collective-permute-start.1 = (bf16[16,32,128]{2,1,0:T(8,128)(2,1)S(1)}, bf16[16,32,128]{2,1,0:T(8,128)(2,1)S(1)}, u32[]{:S(2)}, u32[]{:S(2)}) collective-permute-start(bf16[16,32,128]{2,1,0:T(8,128)(2,1)S(1)} %shrink.2.a_ref), channel_id=1, source_target_pairs={{7,0},{0,1},{1,2},{2,3},{3,4},{4,5},{5,6},{6,7},{15,8},{8,9},{9,10... | collective-permute-start | bytes 393224 | tf_op jit(solution)/shard_map/ppermute | solution.py:277
  62.8 12.7 %copy-start.4 = (bf16[16,64,512]{2,1,0:T(8,128)(2,1)S(1)}, bf16[16,64,512]{2,1,0:T(8,128)(2,1)}, u32[]{:S(2)}) copy-start(bf16[16,64,512]{2,1,0:T(8,128)(2,1)} %param.12) | copy-start | bytes 3145732
  62.8 12.7 %collective-permute-start.2 = (bf16[16,32,128]{2,1,0:T(8,128)(2,1)S(1)}, bf16[16,32,128]{2,1,0:T(8,128)(2,1)S(1)}, u32[]{:S(2)}, u32[]{:S(2)}) collective-permute-start(bf16[16,32,128]{2,1,0:T(8,128)(2,1)S(1)} %add_convert_fusion.1), channel_id=1, source_target_pairs={{3,0},{4,1},{5,2},{6,3},{7,4},{0,5},{1,6},{2,7},{11,8},{12,9},{13,... | collective-permute-start | bytes 393224 | tf_op jit(solution)/shard_map/ppermute | solution.py:277
  64.1 11.5 %collective-permute-start.3 = (bf16[16,32,128]{2,1,0:T(8,128)(2,1)S(1)}, bf16[16,32,128]{2,1,0:T(8,128)(2,1)S(1)}, u32[]{:S(2)}, u32[]{:S(2)}) collective-permute-start(bf16[16,32,128]{2,1,0:T(8,128)(2,1)S(1)} %add_convert_fusion.2), channel_id=1, source_target_pairs={{5,0},{6,1},{7,2},{0,3},{1,4},{2,5},{3,6},{4,7},{13,8},{14,9},{15,... | collective-permute-start | bytes 393224 | tf_op jit(solution)/shard_map/ppermute | solution.py:277
  69.3 31.7 %collective-permute-start.12 = (bf16[512,512]{1,0:T(8,128)(2,1)}, bf16[512,512]{1,0:T(8,128)(2,1)}, u32[]{:S(2)}, u32[]{:S(2)}) collective-permute-start(bf16[512,512]{1,0:T(8,128)(2,1)} %get-tuple-element.48), channel_id=1, source_target_pairs={{0,1},{1,2},{2,3},{3,4},{4,5},{5,6},{6,7},{7,0},{8,9},{9,10},{10,1... | collective-permute-start | bytes 1572872 | tf_op jit(solution)/shard_map/ppermute | solution.py:333
  69.6 31.4 %collective-permute-start.13 = (bf16[512,512]{1,0:T(8,128)(2,1)}, bf16[512,512]{1,0:T(8,128)(2,1)}, u32[]{:S(2)}, u32[]{:S(2)}) collective-permute-start(bf16[512,512]{1,0:T(8,128)(2,1)} %get-tuple-element.47), channel_id=1, source_target_pairs={{0,7},{1,0},{2,1},{3,2},{4,3},{5,4},{6,5},{7,6},{8,15},{9,8},{10,9... | collective-permute-start | bytes 1572872 | tf_op jit(solution)/shard_map/ppermute | solution.py:334
  82.9 13.8 %collective-permute-start.8 = (bf16[16,32,128]{2,1,0:T(8,128)(2,1)S(1)}, bf16[16,32,128]{2,1,0:T(8,128)(2,1)S(1)}, u32[]{:S(2)}, u32[]{:S(2)}) collective-permute-start(bf16[16,32,128]{2,1,0:T(8,128)(2,1)S(1)} %shrink.3.a_ref), channel_id=1, source_target_pairs={{1,0},{2,1},{3,2},{4,3},{5,4},{6,5},{7,6},{0,7},{9,8},{10,9},{11,1... | collective-permute-start | bytes 393224 | tf_op jit(solution)/shard_map/ppermute | solution.py:277
  85.5 11.1 %collective-permute-start.9 = (bf16[16,32,128]{2,1,0:T(8,128)(2,1)S(1)}, bf16[16,32,128]{2,1,0:T(8,128)(2,1)}, u32[]{:S(2)}, u32[]{:S(2)}) collective-permute-start(bf16[16,32,128]{2,1,0:T(8,128)(2,1)S(1)} %shrink.3.a_ref), channel_id=1, source_target_pairs={{7,0},{0,1},{1,2},{2,3},{3,4},{4,5},{5,6},{6,7},{15,8},{8,9},{9,10... | collective-permute-start | bytes 393224 | tf_op jit(solution)/shard_map/ppermute | solution.py:277
  85.5 31.5 %all-to-all-start.3 = ((bf16[32,32,512]{2,1,0:T(8,128)(2,1)}), bf16[32,32,512]{2,1,0:T(8,128)(2,1)}, u32[]{:S(2)}, u32[]{:S(2)}) async-start(bf16[32,32,512]{2,1,0:T(8,128)(2,1)} %bitcast.56), calls=%async_computation.3 | async-start | bytes 2097152 | tf_op jit(solution)/shard_map/all_to_all | solution.py:299
  97.7 11.5 %collective-permute-start.10 = (bf16[16,32,128]{2,1,0:T(8,128)(2,1)S(1)}, bf16[16,32,128]{2,1,0:T(8,128)(2,1)S(1)}, u32[]{:S(2)}, u32[]{:S(2)}) collective-permute-start(bf16[16,32,128]{2,1,0:T(8,128)(2,1)S(1)} %get-tuple-element.56), channel_id=1, source_target_pairs={{3,0},{4,1},{5,2},{6,3},{7,4},{0,5},{1,6},{2,7},{11,8},{12,9},{13,... | collective-permute-start | bytes 393224 | tf_op jit(solution)/shard_map/ppermute | solution.py:277
  98.0 12.9 %collective-permute-start.11 = (bf16[16,32,128]{2,1,0:T(8,128)(2,1)S(1)}, bf16[16,32,128]{2,1,0:T(8,128)(2,1)S(1)}, u32[]{:S(2)}, u32[]{:S(2)}) collective-permute-start(bf16[16,32,128]{2,1,0:T(8,128)(2,1)S(1)} %get-tuple-element.55), channel_id=1, source_target_pairs={{5,0},{6,1},{7,2},{0,3},{1,4},{2,5},{3,6},{4,7},{13,8},{14,9},{15,... | collective-permute-start | bytes 393224 | tf_op jit(solution)/shard_map/ppermute | solution.py:277
  114.4 14.3 %collective-permute-start.14 = (bf16[512,512]{1,0:T(8,128)(2,1)}, bf16[512,512]{1,0:T(8,128)(2,1)S(1)}, u32[]{:S(2)}, u32[]{:S(2)}) collective-permute-start(bf16[512,512]{1,0:T(8,128)(2,1)} %get-tuple-element.42), channel_id=1, source_target_pairs={{0,1},{1,2},{2,3},{3,4},{4,5},{5,6},{6,7},{7,0},{8,9},{9,10},{10,1... | collective-permute-start | bytes 1572872 | tf_op jit(solution)/shard_map/ppermute | solution.py:343
  114.6 14.1 %collective-permute-start.15 = (bf16[512,512]{1,0:T(8,128)(2,1)}, bf16[512,512]{1,0:T(8,128)(2,1)S(1)}, u32[]{:S(2)}, u32[]{:S(2)}) collective-permute-start(bf16[512,512]{1,0:T(8,128)(2,1)} %get-tuple-element.43), channel_id=1, source_target_pairs={{0,7},{1,0},{2,1},{3,2},{4,3},{5,4},{6,5},{7,6},{8,15},{9,8},{10,9... | collective-permute-start | bytes 1572872 | tf_op jit(solution)/shard_map/ppermute | solution.py:344
  117.1 25.1 %all-to-all-start.2 = ((bf16[32,32,512]{2,1,0:T(8,128)(2,1)}), bf16[32,32,512]{2,1,0:T(8,128)(2,1)S(1)}, u32[]{:S(2)}, u32[]{:S(2)}) async-start(bf16[32,32,512]{2,1,0:T(8,128)(2,1)} %bitcast.57), calls=%async_computation.2 | async-start | bytes 2097152 | tf_op jit(solution)/shard_map/all_to_all | solution.py:299

commit v8 on v7

--- a/solution.py
+++ b/solution.py
@@ -11,7 +11,7 @@
 F32 = jnp.float32
 LANES = 128
 TILE = 16
-VMEM = 18 << 20
+VMEM = 26 << 20
 FULL = 62 << 20
 
 
@@ -109,7 +109,7 @@
     out_ref[...] = out.astype(BF16).reshape(out_ref.shape)
 
 
-def shrink_rows(step, names, x, down, most, rank, block=8):
+def shrink_rows(step, names, x, down, most, rank, block=16):
     half = x.shape[0] // 2
     held, width = down.shape
     tiles = (most // TILE) * (width // LANES)
@@ -158,7 +158,7 @@
     out_ref[...] = out.astype(BF16).reshape(out_ref.shape)
 
 
-def expand_rows(step, names, parts, up, rank, block=8):
+def expand_rows(step, names, parts, up, rank, block=16):
     half, most, _ = parts[0].shape
     tiles = names.shape[1] - 1
     held, features = up.shape

time: 144 us -> 145 us (level)
    ppermute x1, waiting for transfers between devices: 3.09 us -> 1.27 us  [body(): from_left = lax.ppermute(going_right, 'tp', right).astype(F32)]
    all_to_all x4, waiting for transfers between devices: 9.04 us -> 10.7 us  [swap(): lax.all_to_all(value, 'pool', split_axis=0, concat_axis=0, tiled=True)]
  transfers between devices with their start and end apart: 20 -> 20, of which waited for: 10 -> 12; matrix products, arithmetic and copies ran while one was open for 7% -> 7% of each run, Pallas kernels for 19% -> 19%
where the time goes in v8:
time: 145 us; the launch traced here: 144 us
  starting transfers between devices  62.7 us (43%)
  Pallas kernels  31.7 us (22%)
  waiting for transfers between devices  31.4 us (22%)
  other arithmetic  9.24 us (6%)
  local copies, waits for them, and re-layouts  8.94 us (6%)
    all_to_all x4, starting transfers between devices, swap(): lax.all_to_all(value, 'pool', split_axis=0, concat_axis=0, tiled=True)  36.7 us
    ppermute x8, waiting for transfers between devices, fetch(): lax.ppermute(value, 'tp', [((i + ahead) % size, i) for i in range(size)])  16.2 us
    ppermute x8, starting transfers between devices, fetch(): lax.ppermute(value, 'tp', [((i + ahead) % size, i) for i in range(size)])  12.1 us
    all_to_all x4, waiting for transfers between devices, swap(): lax.all_to_all(value, 'pool', split_axis=0, concat_axis=0, tiled=True)  10.7 us
    pallas_call x2, Pallas kernels, shrink_rows(): pl.pallas_call(functools.partial(shrink_kernel, step, rank), out_shape=ja...  8.88 us
    pallas_call x3, Pallas kernels, base_shares(): pl.pallas_call(shares_kernel, out_shape=jax.ShapeDtypeStruct((amount, row...  8.8 us
    unnamed x27, local copies, waits for them, and re-layouts  7.93 us
    pallas_call x2, Pallas kernels, expand_rows(): pl.pallas_call(functools.partial(expand_kernel, step, rank), out_shape=pl...  6.24 us
  transfers between devices with their start and end apart: 20, of which 12 were waited for; matrix products, arithmetic and copies ran while one was open for 7% of the time, Pallas kernels for 19%

profile of v8, /device:TPU:1, one launch (start us, length us, event | category | flops | bytes accessed | tf_op | source)
XLA Modules:
  0.0 144.2 jit_solution(9296649528864723142)
XLA Ops:
  0.0 3.1 %pack.2 = bf16[32,17,16,128]{3,2,1,0:T(8,128)(2,1)} custom-call(s32[2,32]{1,0:T(2,128)} %bitcast.54, s32[2,1,256]{2,1,0:T(1,128)} %slots_ref.2, bf16[2,256,1024]{2,1,0:T(8,128)(2,1)} %tokens_ref.2), custom_call_target="tpu_custom_call" | custom-call | flops 536870912 | bytes 2752512 | tf_op jit(solution)/shard_map/pack/pallas_call | solution.py:55
  3.1 8.7 %all-to-all-start = ((bf16[32,17,16,128]{3,2,1,0:T(8,128)(2,1)}), bf16[32,17,16,128]{3,2,1,0:T(8,128)(2,1)S(1)}, u32[]{:S(2)}, u32[]{:S(2)}) async-start(bf16[32,17,16,128]{3,2,1,0:T(8,128)(2,1)} %pack.2), calls=%async_computation | async-start | bytes 4456448 | tf_op jit(solution)/shard_map/all_to_all | solution.py:299
  11.8 0.0 slice-start
  11.8 2.1 %shares.4 = f32[1,512,512]{2,1,0:T(8,128)S(1)} custom-call(s32[1]{0:T(128)S(6)} %rem.55.order_ref, bf16[512,1024]{1,0:T(8,128)(2,1)S(1)} %bitcast.44, bf16[1024,4096]{1,0:T(8,128)(2,1)} %weight_ref.5), custom_call_target="tpu_custom_call" | custom-call | flops 536870912 | bytes 2097152 | tf_op jit(solution)/shard_map/shares/pallas_call | solution.py:196
  13.9 0.0 copy-start.10
  13.9 0.1 convert_element_type.87
  14.0 1.7 %collective-permute-start.4 = (bf16[256,512]{1,0:T(8,128)(2,1)S(1)}, bf16[256,512]{1,0:T(8,128)(2,1)S(1)}, u32[]{:S(2)}, u32[]{:S(2)}) collective-permute-start(bf16[256,512]{1,0:T(8,128)(2,1)S(1)} %get-tuple-element.54), channel_id=1, source_target_pairs={{0,1},{1,2},{2,3},{3,4},{4,5},{5,6},{6,7},{7,0},{8,9},{9,10},{10,1... | collective-permute-start | bytes 786440 | tf_op jit(solution)/shard_map/ppermute | solution.py:311
  15.7 4.0 %collective-permute-start.5 = (bf16[256,512]{1,0:T(8,128)(2,1)S(1)}, bf16[256,512]{1,0:T(8,128)(2,1)S(1)}, u32[]{:S(2)}, u32[]{:S(2)}) collective-permute-start(bf16[256,512]{1,0:T(8,128)(2,1)S(1)} %get-tuple-element.53), channel_id=1, source_target_pairs={{0,7},{1,0},{2,1},{3,2},{4,3},{5,4},{6,5},{7,6},{8,15},{9,8},{10,9... | collective-permute-start | bytes 786440 | tf_op jit(solution)/shard_map/ppermute | solution.py:312
  19.8 3.4 %copy-done = bf16[1024,4096]{1,0:T(8,128)(2,1)S(1)} copy-done((bf16[1024,4096]{1,0:T(8,128)(2,1)S(1)}, bf16[1024,4096]{1,0:T(8,128)(2,1)}, u32[]{:S(2)}) %copy-start) | copy-done | bytes 8388632
  23.2 2.2 %shares.3.shares_ref = f32[2,512,512]{2,1,0:T(8,128)S(1)} custom-call(s32[2]{0:T(128)S(1)} %compare_select_fusion.2.order_ref, bf16[512,1024]{1,0:T(8,128)(2,1)S(1)} %bitcast.45, bf16[1024,4096]{1,0:T(8,128)(2,1)S(1)} %copy-done), custom_call_target="tpu_custom_call" | custom-call | flops 1073741824 | bytes 4194304 | tf_op jit(solution)/shard_map/shares/pallas_call | solution.py:196
  25.4 0.0 copy-start.5
  25.4 0.0 copy-start.6
  25.4 0.8 collective-permute-done.4.top_ref
  26.2 0.2 first_sums.1
  26.4 0.0 copy-start.9
  26.4 0.1 collective-permute-start.6
  26.5 2.7 %collective-permute-start.7 = (bf16[512,512]{1,0:T(8,128)(2,1)S(1)}, bf16[512,512]{1,0:T(8,128)(2,1)}, u32[]{:S(2)}, u32[]{:S(2)}) collective-permute-start(bf16[512,512]{1,0:T(8,128)(2,1)S(1)} %get-tuple-element.33), channel_id=1, source_target_pairs={{0,7},{1,0},{2,1},{3,2},{4,3},{5,4},{6,5},{7,6},{8,15},{9,8},{10,9... | collective-permute-start | bytes 1572872 | tf_op jit(solution)/shard_map/ppermute | solution.py:322
  29.2 1.0 pack.3
  30.2 1.4 copy-done.3
  31.6 4.6 %shares.5 = f32[5,512,512]{2,1,0:T(8,128)S(1)} custom-call(s32[5]{0:T(128)S(1)} %compare_select_fusion.order_ref, bf16[512,1024]{1,0:T(8,128)(2,1)S(1)} %bitcast.46, bf16[1024,4096]{1,0:T(8,128)(2,1)S(1)} %bitcast.43), custom_call_target="tpu_custom_call" | custom-call | flops 2684354560 | bytes 10485760 | tf_op jit(solution)/shard_map/shares/pallas_call | solution.py:196
  36.2 2.3 %copy-done.2 = f32[5,512,512]{2,1,0:T(8,128)} copy-done((f32[5,512,512]{2,1,0:T(8,128)}, f32[5,512,512]{2,1,0:T(8,128)S(1)}, u32[]{:S(2)}) %copy-start.2) | copy-done | bytes 5242904
  38.5 1.9 %collective-permute-done.6 = bf16[512,512]{1,0:T(8,128)(2,1)S(1)} collective-permute-done((bf16[512,512]{1,0:T(8,128)(2,1)S(1)}, bf16[512,512]{1,0:T(8,128)(2,1)S(1)}, u32[]{:S(2)}, u32[]{:S(2)}) %collective-permute-start.6) | collective-permute-done | bytes 524320 | tf_op jit(solution)/shard_map/ppermute | solution.py:321
  40.5 0.8 copy-done.7
  41.2 0.3 all-to-all-done
  41.5 8.3 %all-to-all-start.1 = ((bf16[32,16,16,128]{3,2,1,0:T(8,128)(2,1)}), bf16[32,16,16,128]{3,2,1,0:T(8,128)(2,1)}, u32[]{:S(2)}, u32[]{:S(2)}) async-start(bf16[32,16,16,128]{3,2,1,0:T(8,128)(2,1)} %copy-done.3), calls=%async_computation.1 | async-start | bytes 4194304 | tf_op jit(solution)/shard_map/all_to_all | solution.py:299
  49.8 0.0 copy-start.8
  49.8 4.2 %shrink.2.a_ref = bf16[16,32,128]{2,1,0:T(8,128)(2,1)S(1)} custom-call(bf16[2,16,17,16,128]{4,3,2,1,0:T(8,128)(2,1)S(1)} %bitcast.47, bf16[2,16,17,16,128]{4,3,2,1,0:T(8,128)(2,1)S(1)} %bitcast.48, bf16[1024,1024]{1,0:T(8,128)(2,1)} %bitcast.60), custom_call_target="tpu_custom_call" | custom-call | flops 2147483648 | bytes 4325376 | tf_op jit(solution)/shard_map/shrink/pallas_call | solution.py:118
  54.0 2.6 %collective-permute-start = (bf16[16,32,128]{2,1,0:T(8,128)(2,1)S(1)}, bf16[16,32,128]{2,1,0:T(8,128)(2,1)S(1)}, u32[]{:S(2)}, u32[]{:S(2)}) collective-permute-start(bf16[16,32,128]{2,1,0:T(8,128)(2,1)S(1)} %shrink.2.a_ref), channel_id=1, source_target_pairs={{1,0},{2,1},{3,2},{4,3},{5,4},{6,5},{7,6},{0,7},{9,8},{10,9},{11,1... | collective-permute-start | bytes 393224 | tf_op jit(solution)/shard_map/ppermute | solution.py:277
  56.6 0.1 convert_reduce_fusion
  56.8 0.1 collective-permute-start.1
  56.9 2.2 %collective-permute-done.b_ref = bf16[16,32,128]{2,1,0:T(8,128)(2,1)S(1)} collective-permute-done((bf16[16,32,128]{2,1,0:T(8,128)(2,1)S(1)}, bf16[16,32,128]{2,1,0:T(8,128)(2,1)S(1)}, u32[]{:S(2)}, u32[]{:S(2)}) %collective-permute-start) | collective-permute-done | bytes 131104 | tf_op jit(solution)/shard_map/ppermute | solution.py:277
  59.1 3.4 %collective-permute-done.1.c_ref = bf16[16,32,128]{2,1,0:T(8,128)(2,1)S(1)} collective-permute-done((bf16[16,32,128]{2,1,0:T(8,128)(2,1)S(1)}, bf16[16,32,128]{2,1,0:T(8,128)(2,1)S(1)}, u32[]{:S(2)}, u32[]{:S(2)}) %collective-permute-start.1) | collective-permute-done | bytes 131104 | tf_op jit(solution)/shard_map/ppermute | solution.py:277
  62.5 0.1 add_convert_fusion.1
  62.6 1.2 collective-permute-start.2
  63.8 2.1 %collective-permute-start.3 = (bf16[16,32,128]{2,1,0:T(8,128)(2,1)S(1)}, bf16[16,32,128]{2,1,0:T(8,128)(2,1)S(1)}, u32[]{:S(2)}, u32[]{:S(2)}) collective-permute-start(bf16[16,32,128]{2,1,0:T(8,128)(2,1)S(1)} %add_convert_fusion.2), channel_id=1, source_target_pairs={{5,0},{6,1},{7,2},{0,3},{1,4},{2,5},{3,6},{4,7},{13,8},{14,9},{15,... | collective-permute-start | bytes 393224 | tf_op jit(solution)/shard_map/ppermute | solution.py:277
  65.9 3.0 %fusion.3 = (bf16[512,512]{1,0:T(8,128)(2,1)}, bf16[512,512]{1,0:T(8,128)(2,1)}) fusion(f32[5,512,512]{2,1,0:T(8,128)} %copy-done.2, bf16[512,512]{1,0:T(8,128)(2,1)} %collective-permute-done.7, bf16[512,512]{1,0:T(8,128)(2,1)S(1)} %copy-done.8), kind=kLoop, calls=%fused_computation.7 | loop fusion | flops 1572864 | bytes 4194304 | tf_op jit(solution)/shard_map/convert_element_type | solution.py:328
  68.9 0.5 collective-permute-start.12
  69.5 2.1 %collective-permute-start.13 = (bf16[512,512]{1,0:T(8,128)(2,1)}, bf16[512,512]{1,0:T(8,128)(2,1)}, u32[]{:S(2)}, u32[]{:S(2)}) collective-permute-start(bf16[512,512]{1,0:T(8,128)(2,1)} %get-tuple-element.47), channel_id=1, source_target_pairs={{0,7},{1,0},{2,1},{3,2},{4,3},{5,4},{6,5},{7,6},{8,15},{9,8},{10,9... | collective-permute-start | bytes 1572872 | tf_op jit(solution)/shard_map/ppermute | solution.py:334
  71.6 3.6 %collective-permute-done.2.d_ref = bf16[16,32,128]{2,1,0:T(8,128)(2,1)S(1)} collective-permute-done((bf16[16,32,128]{2,1,0:T(8,128)(2,1)S(1)}, bf16[16,32,128]{2,1,0:T(8,128)(2,1)S(1)}, u32[]{:S(2)}, u32[]{:S(2)}) %collective-permute-start.2) | collective-permute-done | bytes 131104 | tf_op jit(solution)/shard_map/ppermute | solution.py:277
  75.2 2.7 %expand.2 = bf16[2,16,32,512]{3,2,1,0:T(8,128)(2,1)} custom-call(bf16[2,16,17,16,128]{4,3,2,1,0:T(8,128)(2,1)S(1)} %bitcast.49, bf16[16,32,128]{2,1,0:T(8,128)(2,1)S(1)} %shrink.2.a_ref, bf16[16,32,128]{2,1,0:T(8,128)(2,1)S(1)} %collective-permute-done.b_ref, bf16[16,32,128]{2,1,0:T(8,128)(2,1)S(1)} %collective-permute-done.1.c_ref, ...), custom_call_target="tpu_custom_call" | custom-call | flops 1073741824 | bytes 2752512 | tf_op jit(solution)/shard_map/expand/pallas_call | solution.py:166
  77.9 0.2 all-to-all-done.1
  78.1 4.7 %shrink.3.a_ref = bf16[16,32,128]{2,1,0:T(8,128)(2,1)S(1)} custom-call(bf16[2,16,17,16,128]{4,3,2,1,0:T(8,128)(2,1)S(1)} %bitcast.50, bf16[2,16,16,16,128]{4,3,2,1,0:T(8,128)(2,1)} %bitcast.10.x_ref, bf16[1024,1024]{1,0:T(8,128)(2,1)} %bitcast.61), custom_call_target="tpu_custom_call" | custom-call | flops 2147483648 | bytes 4194304 | tf_op jit(solution)/shard_map/shrink/pallas_call | solution.py:118
  82.8 2.7 %collective-permute-start.8 = (bf16[16,32,128]{2,1,0:T(8,128)(2,1)S(1)}, bf16[16,32,128]{2,1,0:T(8,128)(2,1)S(1)}, u32[]{:S(2)}, u32[]{:S(2)}) collective-permute-start(bf16[16,32,128]{2,1,0:T(8,128)(2,1)S(1)} %shrink.3.a_ref), channel_id=1, source_target_pairs={{1,0},{2,1},{3,2},{4,3},{5,4},{6,5},{7,6},{0,7},{9,8},{10,9},{11,1... | collective-permute-start | bytes 393224 | tf_op jit(solution)/shard_map/ppermute | solution.py:277
  85.5 10.7 %all-to-all-start.3 = ((bf16[32,32,512]{2,1,0:T(8,128)(2,1)}), bf16[32,32,512]{2,1,0:T(8,128)(2,1)}, u32[]{:S(2)}, u32[]{:S(2)}) async-start(bf16[32,32,512]{2,1,0:T(8,128)(2,1)} %bitcast.56), calls=%async_computation.3 | async-start | bytes 2097152 | tf_op jit(solution)/shard_map/all_to_all | solution.py:299
  96.2 0.1 select_reduce_fusion
  96.3 1.0 fusion.6
  97.3 0.4 collective-permute-start.10
  97.7 2.9 %collective-permute-start.11 = (bf16[16,32,128]{2,1,0:T(8,128)(2,1)S(1)}, bf16[16,32,128]{2,1,0:T(8,128)(2,1)S(1)}, u32[]{:S(2)}, u32[]{:S(2)}) collective-permute-start(bf16[16,32,128]{2,1,0:T(8,128)(2,1)S(1)} %get-tuple-element.55), channel_id=1, source_target_pairs={{5,0},{6,1},{7,2},{0,3},{1,4},{2,5},{3,6},{4,7},{13,8},{14,9},{15,... | collective-permute-start | bytes 393224 | tf_op jit(solution)/shard_map/ppermute | solution.py:277
  100.6 3.2 %fusion.2 = (bf16[512,512]{1,0:T(8,128)(2,1)}, bf16[512,512]{1,0:T(8,128)(2,1)}) fusion(f32[5,512,512]{2,1,0:T(8,128)} %copy-done.2, bf16[512,512]{1,0:T(8,128)(2,1)} %collective-permute-done.13, bf16[512,512]{1,0:T(8,128)(2,1)} %collective-permute-done.12), kind=kLoop, calls=%fused_computation.5 | loop fusion | flops 1572864 | bytes 4194304 | tf_op jit(solution)/shard_map/convert_element_type | solution.py:340
  103.8 5.0 %collective-permute-done.10.d_ref = bf16[16,32,128]{2,1,0:T(8,128)(2,1)S(1)} collective-permute-done((bf16[16,32,128]{2,1,0:T(8,128)(2,1)S(1)}, bf16[16,32,128]{2,1,0:T(8,128)(2,1)S(1)}, u32[]{:S(2)}, u32[]{:S(2)}) %collective-permute-start.10) | collective-permute-done | bytes 131104 | tf_op jit(solution)/shard_map/ppermute | solution.py:277
  108.8 2.0 %collective-permute-done.11.e_ref = bf16[16,32,128]{2,1,0:T(8,128)(2,1)S(1)} collective-permute-done((bf16[16,32,128]{2,1,0:T(8,128)(2,1)S(1)}, bf16[16,32,128]{2,1,0:T(8,128)(2,1)S(1)}, u32[]{:S(2)}, u32[]{:S(2)}) %collective-permute-start.11) | collective-permute-done | bytes 131104 | tf_op jit(solution)/shard_map/ppermute | solution.py:277
  110.8 3.6 %expand.3 = bf16[2,16,32,512]{3,2,1,0:T(8,128)(2,1)} custom-call(bf16[2,16,17,16,128]{4,3,2,1,0:T(8,128)(2,1)S(1)} %bitcast.51, bf16[16,32,128]{2,1,0:T(8,128)(2,1)S(1)} %shrink.3.a_ref, bf16[16,32,128]{2,1,0:T(8,128)(2,1)S(1)} %collective-permute-done.8.b_ref, bf16[16,32,128]{2,1,0:T(8,128)(2,1)} %collective-permute-done.9.c_ref, ...), custom_call_target="tpu_custom_call" | custom-call | flops 1073741824 | bytes 2752512 | tf_op jit(solution)/shard_map/expand/pallas_call | solution.py:166
  114.4 2.7 %collective-permute-start.15 = (bf16[512,512]{1,0:T(8,128)(2,1)}, bf16[512,512]{1,0:T(8,128)(2,1)S(1)}, u32[]{:S(2)}, u32[]{:S(2)}) collective-permute-start(bf16[512,512]{1,0:T(8,128)(2,1)} %get-tuple-element.43), channel_id=1, source_target_pairs={{0,7},{1,0},{2,1},{3,2},{4,3},{5,4},{6,5},{7,6},{8,15},{9,8},{10,9... | collective-permute-start | bytes 1572872 | tf_op jit(solution)/shard_map/ppermute | solution.py:344
  117.1 9.1 %all-to-all-start.2 = ((bf16[32,32,512]{2,1,0:T(8,128)(2,1)}), bf16[32,32,512]{2,1,0:T(8,128)(2,1)S(1)}, u32[]{:S(2)}, u32[]{:S(2)}) async-start(bf16[32,32,512]{2,1,0:T(8,128)(2,1)} %bitcast.57), calls=%async_computation.2 | async-start | bytes 2097152 | tf_op jit(solution)/shard_map/all_to_all | solution.py:299
  126.1 0.2 fusion
  126.4 0.1 slice_bitcast_fusion
  126.5 1.3 collective-permute-done.14
  127.7 0.4 collective-permute-done.15
  128.1 1.4 fusion.1
  129.5 0.1 fusion.9
  129.6 0.8 broadcast_in_dim.23.earlier_ref
  130.4 2.4 %join.2.earlier_ref = bf16[2,256,512]{2,1,0:T(8,128)(2,1)} custom-call(bf16[256,1024]{1,0:T(8,128)(2,1)S(1)} %get-tuple-element.51.spread_ref, bf16[32,32,512]{2,1,0:T(8,128)(2,1)} %all-to-all-done.3.back_ref, f32[256,512]{1,0:T(8,128)S(1)} %get-tuple-element.49.base_ref, ...), custom_call_target="tpu_custom_call", output_to_operand_aliasing={{}: (3, {})} | custom-call | flops 268435456 | bytes 2359296 | tf_op jit(solution)/shard_map/join/pallas_call | solution.py:250
  132.8 10.2 %all-to-all-done.2.back_ref = bf16[32,32,512]{2,1,0:T(8,128)(2,1)S(1)} async-done(((bf16[32,32,512]{2,1,0:T(8,128)(2,1)}), bf16[32,32,512]{2,1,0:T(8,128)(2,1)S(1)}, u32[]{:S(2)}, u32[]{:S(2)}) %all-to-all-start.2) | async-done | bytes 1048608 | tf_op jit(solution)/shard_map/all_to_all | solution.py:299
  143.0 1.1 join.3
  (34 shorter events, 0.2 us)
Async XLA Ops:
  3.1 8.7 %copy-start.1 = (bf16[2,256,1024]{2,1,0:T(8,128)(2,1)S(1)}, bf16[2,256,1024]{2,1,0:T(8,128)(2,1)}, u32[]{:S(2)}) copy-start(bf16[2,256,1024]{2,1,0:T(8,128)(2,1)} %tokens_ref.2) | copy-start | bytes 3145732
  3.1 38.4 %all-to-all-start = ((bf16[32,17,16,128]{3,2,1,0:T(8,128)(2,1)}), bf16[32,17,16,128]{3,2,1,0:T(8,128)(2,1)S(1)}, u32[]{:S(2)}, u32[]{:S(2)}) async-start(bf16[32,17,16,128]{3,2,1,0:T(8,128)(2,1)} %pack.2), calls=%async_computation | async-start | bytes 4456448 | tf_op jit(solution)/shard_map/all_to_all | solution.py:299
  11.8 19.8 %slice-start = ((s8[8388608]{0:T(1024)(128)(4,1)}), s8[4194304]{0:T(1024)(128)(4,1)S(1)}, s32[]{:S(2)}) async-start(s8[8388608]{0:T(1024)(128)(4,1)} %bitcast.42), calls=%async_computation.4 | async-start | bytes 8388608
  13.9 5.9 %copy-start.10 = (s32[2]{0:T(128)S(1)}, s32[2]{0:T(128)}, u32[]{:S(2)}) copy-start(s32[2]{0:T(128)} %constant.33.clone) | copy-start | bytes 28
  14.0 12.2 %collective-permute-start.4 = (bf16[256,512]{1,0:T(8,128)(2,1)S(1)}, bf16[256,512]{1,0:T(8,128)(2,1)S(1)}, u32[]{:S(2)}, u32[]{:S(2)}) collective-permute-start(bf16[256,512]{1,0:T(8,128)(2,1)S(1)} %get-tuple-element.54), channel_id=1, source_target_pairs={{0,1},{1,2},{2,3},{3,4},{4,5},{5,6},{6,7},{7,0},{8,9},{9,10},{10,1... | collective-permute-start | bytes 786440 | tf_op jit(solution)/shard_map/ppermute | solution.py:311
  15.7 10.5 %collective-permute-start.5 = (bf16[256,512]{1,0:T(8,128)(2,1)S(1)}, bf16[256,512]{1,0:T(8,128)(2,1)S(1)}, u32[]{:S(2)}, u32[]{:S(2)}) collective-permute-start(bf16[256,512]{1,0:T(8,128)(2,1)S(1)} %get-tuple-element.53), channel_id=1, source_target_pairs={{0,7},{1,0},{2,1},{3,2},{4,3},{5,4},{6,5},{7,6},{8,15},{9,8},{10,9... | collective-permute-start | bytes 786440 | tf_op jit(solution)/shard_map/ppermute | solution.py:312
  19.8 3.4 %copy-start = (bf16[1024,4096]{1,0:T(8,128)(2,1)S(1)}, bf16[1024,4096]{1,0:T(8,128)(2,1)}, u32[]{:S(2)}) copy-start(bf16[1024,4096]{1,0:T(8,128)(2,1)} %weight_ref.5) | copy-start | bytes 25165828
  23.2 8.4 %slice-start.1 = ((s8[8388608]{0:T(1024)(128)(4,1)}), s8[4194304]{0:T(1024)(128)(4,1)S(1)}, s32[]{:S(2)}) async-start(s8[8388608]{0:T(1024)(128)(4,1)} %bitcast.42), calls=%async_computation.5 | async-start | bytes 8388608
  25.4 3.8 %copy-start.5 = (s32[2,1,256]{2,1,0:T(1,128)S(1)}, s32[2,1,256]{2,1,0:T(1,128)}, u32[]{:S(2)}) copy-start(s32[2,1,256]{2,1,0:T(1,128)} %slots_ref.2) | copy-start | bytes 6148
  25.4 3.8 %copy-start.6 = (s32[2,1,32]{2,1,0:T(1,128)S(1)}, s32[2,1,32]{2,1,0:T(1,128)}, u32[]{:S(2)}) copy-start(s32[2,1,32]{2,1,0:T(1,128)} %param.13) | copy-start | bytes 772
  26.4 5.2 %copy-start.9 = (s32[5]{0:T(128)S(1)}, s32[5]{0:T(128)}, u32[]{:S(2)}) copy-start(s32[5]{0:T(128)} %constant.34.clone) | copy-start | bytes 64
  26.4 14.0 %collective-permute-start.6 = (bf16[512,512]{1,0:T(8,128)(2,1)S(1)}, bf16[512,512]{1,0:T(8,128)(2,1)S(1)}, u32[]{:S(2)}, u32[]{:S(2)}) collective-permute-start(bf16[512,512]{1,0:T(8,128)(2,1)S(1)} %get-tuple-element.32), channel_id=1, source_target_pairs={{0,1},{1,2},{2,3},{3,4},{4,5},{5,6},{6,7},{7,0},{8,9},{9,10},{10,1... | collective-permute-start | bytes 1572872 | tf_op jit(solution)/shard_map/ppermute | solution.py:321
  26.5 14.7 %collective-permute-start.7 = (bf16[512,512]{1,0:T(8,128)(2,1)S(1)}, bf16[512,512]{1,0:T(8,128)(2,1)}, u32[]{:S(2)}, u32[]{:S(2)}) collective-permute-start(bf16[512,512]{1,0:T(8,128)(2,1)S(1)} %get-tuple-element.33), channel_id=1, source_target_pairs={{0,7},{1,0},{2,1},{3,2},{4,3},{5,4},{6,5},{7,6},{8,15},{9,8},{10,9... | collective-permute-start | bytes 1572872 | tf_op jit(solution)/shard_map/ppermute | solution.py:322
  30.2 1.4 copy-start.3
  36.2 2.3 %copy-start.2 = (f32[5,512,512]{2,1,0:T(8,128)}, f32[5,512,512]{2,1,0:T(8,128)S(1)}, u32[]{:S(2)}) copy-start(f32[5,512,512]{2,1,0:T(8,128)S(1)} %shares.5) | copy-start | bytes 15728644
  40.4 0.8 copy-start.7
  41.5 36.6 %all-to-all-start.1 = ((bf16[32,16,16,128]{3,2,1,0:T(8,128)(2,1)}), bf16[32,16,16,128]{3,2,1,0:T(8,128)(2,1)}, u32[]{:S(2)}, u32[]{:S(2)}) async-start(bf16[32,16,16,128]{3,2,1,0:T(8,128)(2,1)} %copy-done.3), calls=%async_computation.1 | async-start | bytes 4194304 | tf_op jit(solution)/shard_map/all_to_all | solution.py:299
  49.8 16.1 %copy-start.8 = (bf16[512,512]{1,0:T(8,128)(2,1)S(1)}, bf16[512,512]{1,0:T(8,128)(2,1)}, u32[]{:S(2)}) copy-start(bf16[512,512]{1,0:T(8,128)(2,1)} %copy-done.7) | copy-start | bytes 1572868
  54.0 5.1 %collective-permute-start = (bf16[16,32,128]{2,1,0:T(8,128)(2,1)S(1)}, bf16[16,32,128]{2,1,0:T(8,128)(2,1)S(1)}, u32[]{:S(2)}, u32[]{:S(2)}) collective-permute-start(bf16[16,32,128]{2,1,0:T(8,128)(2,1)S(1)} %shrink.2.a_ref), channel_id=1, source_target_pairs={{1,0},{2,1},{3,2},{4,3},{5,4},{6,5},{7,6},{0,7},{9,8},{10,9},{11,1... | collective-permute-start | bytes 393224 | tf_op jit(solution)/shard_map/ppermute | solution.py:277
  56.8 5.7 %collective-permute-start.1 = (bf16[16,32,128]{2,1,0:T(8,128)(2,1)S(1)}, bf16[16,32,128]{2,1,0:T(8,128)(2,1)S(1)}, u32[]{:S(2)}, u32[]{:S(2)}) collective-permute-start(bf16[16,32,128]{2,1,0:T(8,128)(2,1)S(1)} %shrink.2.a_ref), channel_id=1, source_target_pairs={{7,0},{0,1},{1,2},{2,3},{3,4},{4,5},{5,6},{6,7},{15,8},{8,9},{9,10... | collective-permute-start | bytes 393224 | tf_op jit(solution)/shard_map/ppermute | solution.py:277
  62.5 12.7 %copy-start.4 = (bf16[16,64,512]{2,1,0:T(8,128)(2,1)S(1)}, bf16[16,64,512]{2,1,0:T(8,128)(2,1)}, u32[]{:S(2)}) copy-start(bf16[16,64,512]{2,1,0:T(8,128)(2,1)} %param.12) | copy-start | bytes 3145732
  62.6 12.7 %collective-permute-start.2 = (bf16[16,32,128]{2,1,0:T(8,128)(2,1)S(1)}, bf16[16,32,128]{2,1,0:T(8,128)(2,1)S(1)}, u32[]{:S(2)}, u32[]{:S(2)}) collective-permute-start(bf16[16,32,128]{2,1,0:T(8,128)(2,1)S(1)} %add_convert_fusion.1), channel_id=1, source_target_pairs={{3,0},{4,1},{5,2},{6,3},{7,4},{0,5},{1,6},{2,7},{11,8},{12,9},{13,... | collective-permute-start | bytes 393224 | tf_op jit(solution)/shard_map/ppermute | solution.py:277
  63.8 11.5 %collective-permute-start.3 = (bf16[16,32,128]{2,1,0:T(8,128)(2,1)S(1)}, bf16[16,32,128]{2,1,0:T(8,128)(2,1)S(1)}, u32[]{:S(2)}, u32[]{:S(2)}) collective-permute-start(bf16[16,32,128]{2,1,0:T(8,128)(2,1)S(1)} %add_convert_fusion.2), channel_id=1, source_target_pairs={{5,0},{6,1},{7,2},{0,3},{1,4},{2,5},{3,6},{4,7},{13,8},{14,9},{15,... | collective-permute-start | bytes 393224 | tf_op jit(solution)/shard_map/ppermute | solution.py:277
  68.9 31.7 %collective-permute-start.12 = (bf16[512,512]{1,0:T(8,128)(2,1)}, bf16[512,512]{1,0:T(8,128)(2,1)}, u32[]{:S(2)}, u32[]{:S(2)}) collective-permute-start(bf16[512,512]{1,0:T(8,128)(2,1)} %get-tuple-element.48), channel_id=1, source_target_pairs={{0,1},{1,2},{2,3},{3,4},{4,5},{5,6},{6,7},{7,0},{8,9},{9,10},{10,1... | collective-permute-start | bytes 1572872 | tf_op jit(solution)/shard_map/ppermute | solution.py:333
  69.5 31.1 %collective-permute-start.13 = (bf16[512,512]{1,0:T(8,128)(2,1)}, bf16[512,512]{1,0:T(8,128)(2,1)}, u32[]{:S(2)}, u32[]{:S(2)}) collective-permute-start(bf16[512,512]{1,0:T(8,128)(2,1)} %get-tuple-element.47), channel_id=1, source_target_pairs={{0,7},{1,0},{2,1},{3,2},{4,3},{5,4},{6,5},{7,6},{8,15},{9,8},{10,9... | collective-permute-start | bytes 1572872 | tf_op jit(solution)/shard_map/ppermute | solution.py:334
  82.8 13.5 %collective-permute-start.8 = (bf16[16,32,128]{2,1,0:T(8,128)(2,1)S(1)}, bf16[16,32,128]{2,1,0:T(8,128)(2,1)S(1)}, u32[]{:S(2)}, u32[]{:S(2)}) collective-permute-start(bf16[16,32,128]{2,1,0:T(8,128)(2,1)S(1)} %shrink.3.a_ref), channel_id=1, source_target_pairs={{1,0},{2,1},{3,2},{4,3},{5,4},{6,5},{7,6},{0,7},{9,8},{10,9},{11,1... | collective-permute-start | bytes 393224 | tf_op jit(solution)/shard_map/ppermute | solution.py:277
  85.5 10.8 %collective-permute-start.9 = (bf16[16,32,128]{2,1,0:T(8,128)(2,1)S(1)}, bf16[16,32,128]{2,1,0:T(8,128)(2,1)}, u32[]{:S(2)}, u32[]{:S(2)}) collective-permute-start(bf16[16,32,128]{2,1,0:T(8,128)(2,1)S(1)} %shrink.3.a_ref), channel_id=1, source_target_pairs={{7,0},{0,1},{1,2},{2,3},{3,4},{4,5},{5,6},{6,7},{15,8},{8,9},{9,10... | collective-permute-start | bytes 393224 | tf_op jit(solution)/shard_map/ppermute | solution.py:277
  85.5 31.5 %all-to-all-start.3 = ((bf16[32,32,512]{2,1,0:T(8,128)(2,1)}), bf16[32,32,512]{2,1,0:T(8,128)(2,1)}, u32[]{:S(2)}, u32[]{:S(2)}) async-start(bf16[32,32,512]{2,1,0:T(8,128)(2,1)} %bitcast.56), calls=%async_computation.3 | async-start | bytes 2097152 | tf_op jit(solution)/shard_map/all_to_all | solution.py:299
  97.3 11.5 %collective-permute-start.10 = (bf16[16,32,128]{2,1,0:T(8,128)(2,1)S(1)}, bf16[16,32,128]{2,1,0:T(8,128)(2,1)S(1)}, u32[]{:S(2)}, u32[]{:S(2)}) collective-permute-start(bf16[16,32,128]{2,1,0:T(8,128)(2,1)S(1)} %get-tuple-element.56), channel_id=1, source_target_pairs={{3,0},{4,1},{5,2},{6,3},{7,4},{0,5},{1,6},{2,7},{11,8},{12,9},{13,... | collective-permute-start | bytes 393224 | tf_op jit(solution)/shard_map/ppermute | solution.py:277
  97.7 13.1 %collective-permute-start.11 = (bf16[16,32,128]{2,1,0:T(8,128)(2,1)S(1)}, bf16[16,32,128]{2,1,0:T(8,128)(2,1)S(1)}, u32[]{:S(2)}, u32[]{:S(2)}) collective-permute-start(bf16[16,32,128]{2,1,0:T(8,128)(2,1)S(1)} %get-tuple-element.55), channel_id=1, source_target_pairs={{5,0},{6,1},{7,2},{0,3},{1,4},{2,5},{3,6},{4,7},{13,8},{14,9},{15,... | collective-permute-start | bytes 393224 | tf_op jit(solution)/shard_map/ppermute | solution.py:277
  114.4 13.4 %collective-permute-start.14 = (bf16[512,512]{1,0:T(8,128)(2,1)}, bf16[512,512]{1,0:T(8,128)(2,1)S(1)}, u32[]{:S(2)}, u32[]{:S(2)}) collective-permute-start(bf16[512,512]{1,0:T(8,128)(2,1)} %get-tuple-element.42), channel_id=1, source_target_pairs={{0,1},{1,2},{2,3},{3,4},{4,5},{5,6},{6,7},{7,0},{8,9},{9,10},{10,1... | collective-permute-start | bytes 1572872 | tf_op jit(solution)/shard_map/ppermute | solution.py:343
  114.4 13.7 %collective-permute-start.15 = (bf16[512,512]{1,0:T(8,128)(2,1)}, bf16[512,512]{1,0:T(8,128)(2,1)S(1)}, u32[]{:S(2)}, u32[]{:S(2)}) collective-permute-start(bf16[512,512]{1,0:T(8,128)(2,1)} %get-tuple-element.43), channel_id=1, source_target_pairs={{0,7},{1,0},{2,1},{3,2},{4,3},{5,4},{6,5},{7,6},{8,15},{9,8},{10,9... | collective-permute-start | bytes 1572872 | tf_op jit(solution)/shard_map/ppermute | solution.py:344
  117.1 26.0 %all-to-all-start.2 = ((bf16[32,32,512]{2,1,0:T(8,128)(2,1)}), bf16[32,32,512]{2,1,0:T(8,128)(2,1)S(1)}, u32[]{:S(2)}, u32[]{:S(2)}) async-start(bf16[32,32,512]{2,1,0:T(8,128)(2,1)} %bitcast.57), calls=%async_computation.2 | async-start | bytes 2097152 | tf_op jit(solution)/shard_map/all_to_all | solution.py:299
